TPU v7x, 768 devices: a whole 4x8x12 slice. The times are simulated.
768 devices in a mesh: rows: 96 (over z, y), rep: 8 (over x, core).
Axes of the slice: x: 4, y: 8, z: 12, core: 2. Of those that a mesh axis runs over, the one named last changes fastest.
Arguments:
- features: bfloat16 [98304, 256], P(('rows', 'rep')), may hold values from -6 to 6
- tile_table: bfloat16 [64, 64, 64], replicated, may hold values from -0.375 to 0.375
- weight: bfloat16 [256, 256], replicated, may hold values from -0.375 to 0.375
- bias_term: float32 [256], replicated, may hold values from -3 to 3
- cotangent: bfloat16 [98304, 256], P(('rows', 'rep')), may hold values from -6 to 6
- adj_rows: int32 [96, 8, 48], P('rows', 'rep'), may hold values from 0 to 15
- adj_cols: int32 [96, 8, 48], P('rows', 'rep'), may hold values from 0 to 191
- adj_tiles: int32 [96, 8, 48], P('rows', 'rep'), may hold values from 0 to 63
- adj_count: int32 [96, 8], P('rows', 'rep'), may hold values from 12 to 48, as said below
Outputs:
- output: bfloat16 [98304, 256], P(('rows', 'rep'))
- weight_grad: float32 [256, 256], replicated
- bias_grad: float32 [256], replicated
Inputs may be any that keep to these rules, and one draw needn't show every extreme that they name: Slots at and beyond adj_count hold no entry; some list fills all 48 slots.
All inputs are finite; a program needn't handle non-finite values.
Results may differ from a plain program's by a relative error of at most 0.015.
Values may be sent and summed in bfloat16 or wider, within the bound.
No kernel may reach another device: no remote copies, remote signals or barrier semaphores. Data moves between devices by JAX's collectives and lax.ppermute only.
A program may use at most 32 MiB of HBM per device.

v0:
```python
import math

import jax
import jax.numpy as jnp
from jax import lax
from jax.sharding import PartitionSpec as P

BLOCK = 64
BPD = 2
SLOTS = 48


def shards(
    features, tile_table, weight, bias_term, cotangent, adj_rows, adj_cols, adj_tiles, adj_count
):
    own_rows = features.shape[0]
    width = features.shape[1]
    rep_size = lax.axis_size("rep")
    local_blocks = rep_size * BPD
    cols_here = adj_cols[0, 0]
    chosen = tile_table[adj_tiles[0, 0]]
    live = jnp.arange(SLOTS, dtype=jnp.int32) < adj_count[0, 0]
    gathered = lax.all_gather(features, "rows", axis=0, tiled=True)
    picked = gathered.reshape(-1, BLOCK, width)[cols_here]
    products = jnp.einsum("sij,sjf->sif", chosen, picked, preferred_element_type=jnp.float32)
    onehot = (
        (adj_rows[0, 0][:, None] == jnp.arange(local_blocks, dtype=jnp.int32)[None, :])
        & live[:, None]
    ).astype(jnp.float32)
    summed = jnp.einsum("sr,sif->rif", onehot, products).reshape(local_blocks * BLOCK, width)
    agg = lax.psum_scatter(summed, "rep", scatter_dimension=0, tiled=True).astype(jnp.bfloat16)
    pre = jnp.dot(agg, weight, preferred_element_type=jnp.float32) + bias_term
    output = jax.nn.silu(pre).astype(jnp.bfloat16)
    sigma = jax.nn.sigmoid(pre)
    grad_pre = (cotangent.astype(jnp.float32) * (sigma * (1.0 + pre * (1.0 - sigma)))).astype(
        jnp.bfloat16
    )
    total_vertices = lax.axis_size("rows") * rep_size * own_rows
    factor = 1.0 / math.sqrt(total_vertices)
    local_weight = lax.dot_general(
        agg, grad_pre, (((0,), (0,)), ((), ())), preferred_element_type=jnp.float32
    )
    local_bias = jnp.sum(grad_pre.astype(jnp.float32), axis=0)
    weight_grad, bias_grad = lax.psum((local_weight, local_bias), ("rows", "rep"))
    return (output, weight_grad * factor, bias_grad * factor)


def solution(mesh):
    return jax.shard_map(
        shards,
        mesh=mesh,
        in_specs=(
            P(("rows", "rep"), None),
            P(),
            P(),
            P(),
            P(("rows", "rep"), None),
            P("rows", "rep", None),
            P("rows", "rep", None),
            P("rows", "rep", None),
            P("rows", "rep"),
        ),
        out_specs=(P(("rows", "rep"), None), P(), P()),
        check_vma=False,
    )
```

profile of v0, /device:TPU:1, one launch (start us, length us, event | category | flops | bytes accessed | tf_op | source)
XLA Modules:
  0.0 668.1 jit_solution(11167007002349075544)
XLA Ops:
  7.2 0.0 copy-start
  7.2 0.0 copy-start.5
  7.2 0.0 all-gather.2.cloned.1.call-start
  7.2 0.7 all-gather.2.cloned.1.call-update
  7.9 0.0 reduce-scatter.2.cloned.1.call-start
  8.6 0.7 fusion.10
  9.3 0.0 copy-done
  9.3 0.7 gather_fusion
  10.0 0.0 copy-done.5
  10.0 134.3 %all-gather.2.cloned.1.call-done = bf16[12288,256]{1,0:T(8,128)(2,1)} async-done(((bf16[128,256]{1,0:T(8,128)(2,1)}), bf16[12288,256]{1,0:T(8,128)(2,1)}) %all-gather.2.cloned.1.call-update) | async-done | bytes 6291472 | tf_op jit(solution)/shard_map/all_gather | solution.py:23
  144.3 3.4 gather_fusion.1
  147.8 0.0 copy-start.1
  147.8 0.6 fusion.12
  148.3 0.1 copy-done.1
  148.4 1.0 fusion
  149.4 0.0 copy-start.2
  149.4 0.0 copy-start.3
  149.4 0.0 copy-start.4
  149.4 1.6 copy.12
  151.0 0.0 reduce-scatter.2.cloned.1.call-update
  151.0 0.0 all-reduce.2.cloned.1.call-start
  151.0 39.8 %reduce-scatter.2.cloned.1.call-done = f32[128,256]{1,0:T(8,128)} async-done(((f32[1024,256]{1,0:T(8,128)}), f32[128,256]{1,0:T(8,128)}) %reduce-scatter.2.cloned.1.call-update) | async-done | bytes 131088 | tf_op jit(solution)/shard_map/reduce_scatter | solution.py:31
  190.9 0.0 copy-done.2
  190.9 0.0 copy-done.3
  190.9 0.0 copy-done.4
  190.9 1.8 convert_reduce_fusion
  192.7 1.8 fusion.2
  194.5 0.0 all-reduce.2.cloned.1.call-update
  194.5 111.6 %psum.15 = f32[256]{0:T(256)S(1)} all-reduce(f32[256]{0:T(256)S(1)} %get-tuple-element.3), channel_id=1, replica_groups=mesh['rows'=96,'rep'=8] {'rows','rep'}, use_global_device_ids=true, to_apply=%region_3.4 | all-reduce | flops 256 | bytes 2048 | tf_op jit(solution)/shard_map/psum | solution.py:44
  306.1 0.6 broadcast_multiply_fusion.1
  306.6 353.2 %all-reduce.2.cloned.1.call-done = f32[256,256]{1,0:T(8,128)} async-done(((f32[256,256]{1,0:T(8,128)}), f32[256,256]{1,0:T(8,128)}) %all-reduce.2.cloned.1.call-update) | async-done | bytes 262160 | tf_op jit(solution)/shard_map/psum | solution.py:44
  659.8 1.7 broadcast_multiply_fusion
  (4 shorter events, 0.0 us)
Async XLA Ops:
  7.2 2.1 copy-start
  7.2 2.8 copy-start.5
  7.2 137.1 %all-gather.2.cloned.1.call-start = ((), (), s32[]{:S(2)}) async-start(), calls=%async_computation.1 | async-start | bytes 6356992 | tf_op jit(solution)/shard_map/all_gather | solution.py:23
  7.9 183.0 %reduce-scatter.2.cloned.1.call-start = ((), (), s32[]{:S(2)}) async-start(), calls=%async_computation.2 | async-start | bytes 1179648 | tf_op jit(solution)/shard_map/reduce_scatter | solution.py:31
  147.8 0.7 copy-start.1
  149.4 41.5 %copy-start.2 = (bf16[256,256]{1,0:T(8,128)(2,1)S(1)}, bf16[256,256]{1,0:T(8,128)(2,1)}, u32[]{:S(2)}) copy-start(bf16[256,256]{1,0:T(8,128)(2,1)} %param.11) | copy-start | bytes 393220
  149.4 41.5 %copy-start.3 = (bf16[128,256]{1,0:T(8,128)(2,1)S(1)}, bf16[128,256]{1,0:T(8,128)(2,1)}, u32[]{:S(2)}) copy-start(bf16[128,256]{1,0:T(8,128)(2,1)} %param.13) | copy-start | bytes 196612
  149.4 41.5 %copy-start.4 = (f32[256]{0:T(256)S(1)}, f32[256]{0:T(256)}, u32[]{:S(2)}) copy-start(f32[256]{0:T(256)} %param.12) | copy-start | bytes 3076
  151.0 508.9 %all-reduce.2.cloned.1.call-start = ((), (), s32[]{:S(2)}) async-start(), calls=%async_computation.3 | async-start | bytes 524288 | tf_op jit(solution)/shard_map/psum | solution.py:44
Sparse Core Ops, SparseCore 0:
  11.8 132.5 all-gather.1
  151.1 39.7 reduce-scatter.1
  196.9 462.9 all-reduce.1
where the time goes:
time: 668 us
  waiting for transfers between devices  528 us (79%)
  blocking collectives  112 us (17%)
  between operations  14.5 us (2%)
    psum x1, waiting for transfers between devices, shards(): lax.psum((local_weight, local_bias), ('rows', 'rep'))  353 us
    all_gather x1, waiting for transfers between devices, shards(): gathered = lax.all_gather(features, 'rows', axis=0, tiled=True)  134 us
    psum x1, blocking collectives, shards(): lax.psum((local_weight, local_bias), ('rows', 'rep'))  112 us
    reduce_scatter x1, waiting for transfers between devices, shards(): lax.psum_scatter(summed, 'rep', scatter_dimension=0, tiled=True)  39.8 us
  transfers between devices with their start and end apart: 3, of which 3 were waited for; matrix products, arithmetic and copies ran while one was open for 0% of the time, Pallas kernels for 0%

commit v1 on v0

v1 whole, which is shorter than its diff:
```python
import functools
import math

import jax
import jax.numpy as jnp
from jax import lax
from jax.experimental import pallas as pl
from jax.experimental.pallas import tpu as pltpu
from jax.sharding import PartitionSpec as P

BLOCK = 64
BPD = 2
UNROLL = 4


def spmm_kernel(
    rows_ref,
    cols_ref,
    tiles_ref,
    count_ref,
    features_ref,
    table_ref,
    out_ref,
    picked,
    table,
    total,
    sems,
    table_sem,
):
    count = count_ref[0, 0]

    def fetch(s):
        start = pl.multiple_of(cols_ref[0, 0, s] * BLOCK, BLOCK)
        return pltpu.make_async_copy(
            features_ref.at[pl.ds(start, BLOCK)], picked.at[s], sems.at[s]
        )

    steps = (count + UNROLL - 1) // UNROLL
    table_copy = pltpu.make_async_copy(table_ref, table, table_sem)
    table_copy.start()

    def begin(i, carry):
        for k in range(UNROLL):
            fetch(i * UNROLL + k).start()
        return carry

    lax.fori_loop(0, steps, begin, 0)
    total[...] = jnp.zeros_like(total)
    table_copy.wait()

    def step(i, carry):
        products = []
        for k in range(UNROLL):
            s = i * UNROLL + k
            fetch(s).wait()
            product = jnp.dot(
                table[tiles_ref[0, 0, s]], picked[s], preferred_element_type=jnp.float32
            )
            products.append(jnp.where(s < count, product, 0.0))
        for k in range(UNROLL):
            row = pl.multiple_of(rows_ref[0, 0, i * UNROLL + k] * BLOCK, BLOCK)
            total[pl.ds(row, BLOCK)] += products[k]
        return carry

    lax.fori_loop(0, steps, step, 0)
    out_ref[...] = total[...].astype(out_ref.dtype)


def spmm(adj_rows, adj_cols, adj_tiles, adj_count, gathered, tile_table, out_rows):
    slots = adj_rows.shape[-1]
    width = gathered.shape[1]
    smem = pl.BlockSpec(memory_space=pltpu.SMEM)
    hbm = pl.BlockSpec(memory_space=pltpu.HBM)
    return pl.pallas_call(
        spmm_kernel,
        out_shape=jax.ShapeDtypeStruct((out_rows, width), jnp.bfloat16),
        in_specs=[smem, smem, smem, smem, hbm, hbm],
        out_specs=pl.BlockSpec(memory_space=pltpu.VMEM),
        scratch_shapes=[
            pltpu.VMEM((slots, BLOCK, width), jnp.bfloat16),
            pltpu.VMEM(tile_table.shape, tile_table.dtype),
            pltpu.VMEM((out_rows, width), jnp.float32),
            pltpu.SemaphoreType.DMA((slots,)),
            pltpu.SemaphoreType.DMA,
        ],
        compiler_params=pltpu.CompilerParams(vmem_limit_bytes=58 * 1024 * 1024),
        name="spmm",
    )(adj_rows, adj_cols, adj_tiles, adj_count, gathered, tile_table)


def layer_kernel(factor, parts_ref, weight_ref, bias_ref, cotangent_ref, out_ref, grads_ref):
    summed = parts_ref[0].astype(jnp.float32)
    for r in range(1, parts_ref.shape[0]):
        summed += parts_ref[r].astype(jnp.float32)
    agg = summed.astype(jnp.bfloat16)
    pre = jnp.dot(agg, weight_ref[...], preferred_element_type=jnp.float32) + bias_ref[...]
    sigma = 1.0 / (1.0 + jnp.exp(-pre))
    out_ref[...] = (pre * sigma).astype(out_ref.dtype)
    grad_pre = (
        cotangent_ref[...].astype(jnp.float32) * (sigma * (1.0 + pre * (1.0 - sigma)))
    ).astype(jnp.bfloat16)
    width = grad_pre.shape[1]
    grads_ref[:width] = factor * lax.dot_general(
        agg, grad_pre, (((0,), (0,)), ((), ())), preferred_element_type=jnp.float32
    )
    bias = factor * jnp.sum(grad_pre.astype(jnp.float32), axis=0, keepdims=True)
    first = lax.broadcasted_iota(jnp.int32, (8, width), 0) == 0
    grads_ref[width:] = jnp.where(first, bias, 0.0)


def layer(parts, weight, bias_term, cotangent, factor):
    width = weight.shape[0]
    vmem = pl.BlockSpec(memory_space=pltpu.VMEM)
    return pl.pallas_call(
        functools.partial(layer_kernel, factor),
        out_shape=(
            jax.ShapeDtypeStruct(cotangent.shape, jnp.bfloat16),
            jax.ShapeDtypeStruct((width + 8, width), jnp.float32),
        ),
        in_specs=[vmem] * 4,
        out_specs=(vmem, vmem),
        compiler_params=pltpu.CompilerParams(vmem_limit_bytes=16 * 1024 * 1024),
        name="layer",
    )(parts, weight, bias_term.reshape(1, -1), cotangent)


def shards(
    features, tile_table, weight, bias_term, cotangent, adj_rows, adj_cols, adj_tiles, adj_count
):
    own_rows, width = features.shape
    rep_size = lax.axis_size("rep")
    gathered = lax.all_gather(features, "rows", axis=0, tiled=True)
    share = spmm(
        adj_rows, adj_cols, adj_tiles, adj_count, gathered, tile_table, rep_size * own_rows
    )
    parts = lax.all_to_all(
        share.reshape(rep_size, own_rows, width), "rep", split_axis=0, concat_axis=0, tiled=True
    )
    factor = 1.0 / math.sqrt(lax.axis_size("rows") * rep_size * own_rows)
    output, grads = layer(parts, weight, bias_term, cotangent, factor)
    grads = lax.psum(grads, ("rows", "rep"))
    return (output, grads[:width], grads[width])


def solution(mesh):
    return jax.shard_map(
        shards,
        mesh=mesh,
        in_specs=(
            P(("rows", "rep"), None),
            P(),
            P(),
            P(),
            P(("rows", "rep"), None),
            P("rows", "rep", None),
            P("rows", "rep", None),
            P("rows", "rep", None),
            P("rows", "rep"),
        ),
        out_specs=(P(("rows", "rep"), None), P(), P()),
        check_vma=False,
    )
```

time: 668 us -> 642 us (0.961)
  blocking collectives: 112 us -> 18.2 us
  waiting for transfers between devices: 528 us -> 596 us
  Pallas kernels: 0 us -> 10.5 us
    psum x1 -> x0, blocking collectives: 112 us -> none  [shards(): lax.psum((local_weight, local_bias), ('rows', 'rep'))]
    psum x1, waiting for transfers between devices: 353 us -> 459 us  [shards(): grads = lax.psum(grads, ('rows', 'rep'))]
    reduce_scatter x1 -> x0, waiting for transfers between devices: 39.8 us -> none  [shards(): lax.psum_scatter(summed, 'rep', scatter_dimension=0, tiled=True)]
    all_to_all x0 -> x1, blocking collectives: none -> 18.2 us  [shards(): lax.all_to_all(share.reshape(rep_size, own_rows, width), 'rep', split_axi...]
    pallas_call x0 -> x2, Pallas kernels: none -> 10.5 us  [the longest x1 9.4 us: spmm(): pl.pallas_call(spmm_kernel, out_shape=jax.ShapeDtypeStruct((out_rows, wid...]
  transfers between devices with their start and end apart: 3 -> 2, of which waited for: 3 -> 2; matrix products, arithmetic and copies ran while one was open for 0% -> 0% of each run, Pallas kernels for 0% -> 0%
where the time goes in v1:
time: 642 us
  waiting for transfers between devices  596 us (93%)
  blocking collectives  18.2 us (3%)
  between operations  14.7 us (2%)
  Pallas kernels  10.5 us (2%)
    psum x1, waiting for transfers between devices, shards(): grads = lax.psum(grads, ('rows', 'rep'))  459 us
    all_gather x1, waiting for transfers between devices, shards(): gathered = lax.all_gather(features, 'rows', axis=0, tiled=True)  136 us
    all_to_all x1, blocking collectives, shards(): lax.all_to_all(share.reshape(rep_size, own_rows, width), 'rep', split_axi...  18.2 us
  transfers between devices with their start and end apart: 2, of which 2 were waited for; matrix products, arithmetic and copies ran while one was open for 0% of the time, Pallas kernels for 0%

profile of v1, /device:TPU:1, one launch (start us, length us, event | category | flops | bytes accessed | tf_op | source)
XLA Modules:
  0.0 642.0 jit_solution(16934409982503754234)
XLA Ops:
  7.2 0.0 copy-start.1
  7.2 0.0 copy-start.2
  7.2 0.0 copy-start
  7.2 0.0 all-gather.2.cloned.1.call-start
  7.2 0.7 all-gather.2.cloned.1.call-update
  7.9 0.0 all-reduce.2.cloned.1.call-start
  8.6 135.7 %all-gather.2.cloned.1.call-done.features_ref = bf16[12288,256]{1,0:T(8,128)(2,1)} async-done(((bf16[128,256]{1,0:T(8,128)(2,1)}), bf16[12288,256]{1,0:T(8,128)(2,1)}) %all-gather.2.cloned.1.call-update) | async-done | bytes 6291472 | tf_op jit(solution)/shard_map/all_gather | solution.py:132
  144.3 9.4 %spmm.1 = bf16[1024,256]{1,0:T(8,128)(2,1)} custom-call(s32[1,1,48]{2,1,0:T(1,128)} %rows_ref.1, s32[1,1,48]{2,1,0:T(1,128)} %cols_ref.1, s32[1,1,48]{2,1,0:T(1,128)} %tiles_ref.1, s32[1,1]{1,0:T(1,128)S(6)} %copy.13.count_ref, bf16[12288,256]{1,0:T(8,128)(2,1)} %all-gather.2.cloned.1.call-done.features_ref, bf16[64,64,64]{2,1,0:T(8,128)(2,1)} %table_ref.1), custom_call_target="tpu_custom_call" | custom-call | tf_op jit(solution)/shard_map/spmm/pallas_call | solution.py:74
  153.7 18.2 %all_to_all.5.parts_ref = bf16[8,128,256]{2,1,0:T(8,128)(2,1)S(1)} all-to-all(bf16[8,128,256]{2,1,0:T(8,128)(2,1)} %bitcast.4), channel_id=1, replica_groups=mesh['rows'=96,'rep'=8] {'rep'}, dimensions={0} | all-to-all | bytes 1048576 | tf_op jit(solution)/shard_map/all_to_all | solution.py:136
  171.9 0.0 copy-done.1
  171.9 0.0 copy-done.2
  171.9 0.0 copy-done
  171.9 1.1 layer.1
  173.1 0.0 all-reduce.2.cloned.1.call-update
  173.1 459.2 %all-reduce.2.cloned.1.call-done = f32[264,256]{1,0:T(8,128)} async-done(((f32[264,256]{1,0:T(8,128)}), f32[264,256]{1,0:T(8,128)}) %all-reduce.2.cloned.1.call-update) | async-done | bytes 270352 | tf_op jit(solution)/shard_map/psum | solution.py:141
  632.2 1.3 slice.9
  633.5 1.7 slice.8
Async XLA Ops:
  7.2 164.7 %copy-start.1 = (bf16[128,256]{1,0:T(8,128)(2,1)S(1)}, bf16[128,256]{1,0:T(8,128)(2,1)}, u32[]{:S(2)}) copy-start(bf16[128,256]{1,0:T(8,128)(2,1)} %cotangent_ref.1) | copy-start | bytes 196612
  7.2 164.7 %copy-start.2 = (f32[256]{0:T(256)S(1)}, f32[256]{0:T(256)}, u32[]{:S(2)}) copy-start(f32[256]{0:T(256)} %param.12) | copy-start | bytes 3076
  7.2 164.7 %copy-start = (bf16[256,256]{1,0:T(8,128)(2,1)S(1)}, bf16[256,256]{1,0:T(8,128)(2,1)}, u32[]{:S(2)}) copy-start(bf16[256,256]{1,0:T(8,128)(2,1)} %weight_ref.1) | copy-start | bytes 393220
  7.2 137.1 %all-gather.2.cloned.1.call-start = ((), (), s32[]{:S(2)}) async-start(), calls=%async_computation.1 | async-start | bytes 6356992 | tf_op jit(solution)/shard_map/all_gather | solution.py:132
  7.9 624.3 %all-reduce.2.cloned.1.call-start = ((), (), s32[]{:S(2)}) async-start(), calls=%async_computation.2 | async-start | bytes 540672 | tf_op jit(solution)/shard_map/psum | solution.py:141
Sparse Core Ops, SparseCore 0:
  11.8 132.5 all-gather.1
  173.2 458.9 all-reduce.1

commit v2 on v1

v2 whole, which is shorter than its diff:
```python
import functools
import math

import jax
import jax.numpy as jnp
import numpy as np
from jax import lax
from jax.experimental import pallas as pl
from jax.experimental.pallas import tpu as pltpu
from jax.sharding import Mesh, PartitionSpec as P

BLOCK = 64
BPD = 2
UNROLL = 4
HALF = 128
MIB = 1024 * 1024
REP = ("x", "core")
SMEM = pl.BlockSpec(memory_space=pltpu.SMEM)
HBM = pl.BlockSpec(memory_space=pltpu.HBM)
VMEM = pl.BlockSpec(memory_space=pltpu.VMEM)


def spmm_kernel(
    place,
    rows_ref,
    cols_ref,
    tiles_ref,
    count_ref,
    features_ref,
    table_ref,
    out_ref,
    picked,
    table,
    total,
    sems,
    table_sem,
):
    count = count_ref[0, 0]

    def fetch(s):
        start = pl.multiple_of(place(cols_ref[0, 0, s]) * BLOCK, BLOCK)
        return pltpu.make_async_copy(
            features_ref.at[pl.ds(start, BLOCK)], picked.at[s], sems.at[s]
        )

    steps = (count + UNROLL - 1) // UNROLL
    table_copy = pltpu.make_async_copy(table_ref, table, table_sem)
    table_copy.start()

    def begin(i, carry):
        for k in range(UNROLL):
            fetch(i * UNROLL + k).start()
        return carry

    lax.fori_loop(0, steps, begin, 0)
    total[...] = jnp.zeros_like(total)
    table_copy.wait()

    def step(i, carry):
        products = []
        for k in range(UNROLL):
            s = i * UNROLL + k
            fetch(s).wait()
            product = jnp.dot(
                table[tiles_ref[0, 0, s]], picked[s], preferred_element_type=jnp.float32
            )
            products.append(jnp.where(s < count, product, 0.0))
        for k in range(UNROLL):
            row = pl.multiple_of(rows_ref[0, 0, i * UNROLL + k] * BLOCK, BLOCK)
            total[pl.ds(row, BLOCK)] += products[k]
        return carry

    lax.fori_loop(0, steps, step, 0)
    out_ref[...] = total[...].astype(out_ref.dtype)


def spmm(place, lists, gathered, tile_table, out_rows):
    slots = lists[0].shape[-1]
    width = gathered.shape[1]
    return pl.pallas_call(
        functools.partial(spmm_kernel, place),
        out_shape=jax.ShapeDtypeStruct((out_rows, width), jnp.bfloat16),
        in_specs=[SMEM, SMEM, SMEM, SMEM, HBM, HBM],
        out_specs=VMEM,
        scratch_shapes=[
            pltpu.VMEM((slots, BLOCK, width), jnp.bfloat16),
            pltpu.VMEM(tile_table.shape, tile_table.dtype),
            pltpu.VMEM((out_rows, width), jnp.float32),
            pltpu.SemaphoreType.DMA((slots,)),
            pltpu.SemaphoreType.DMA,
        ],
        compiler_params=pltpu.CompilerParams(vmem_limit_bytes=58 * MIB),
        name="spmm",
    )(*lists, gathered, tile_table)


def layer_kernel(
    factor, left_ref, right_ref, weight_ref, bias_ref, cotangent_ref, out_ref, grads_ref
):
    def reduced(ref):
        summed = ref[0].astype(jnp.float32)
        for r in range(1, ref.shape[0]):
            summed += ref[r].astype(jnp.float32)
        return summed.astype(jnp.bfloat16)

    agg = jnp.concatenate([reduced(left_ref), reduced(right_ref)], axis=1)
    pre = jnp.dot(agg, weight_ref[...], preferred_element_type=jnp.float32) + bias_ref[...]
    sigma = 1.0 / (1.0 + jnp.exp(-pre))
    out_ref[...] = (pre * sigma).astype(out_ref.dtype)
    grad_pre = (
        cotangent_ref[...].astype(jnp.float32) * (sigma * (1.0 + pre * (1.0 - sigma)))
    ).astype(jnp.bfloat16)
    width = grad_pre.shape[1]
    grads_ref[:width] = factor * lax.dot_general(
        agg, grad_pre, (((0,), (0,)), ((), ())), preferred_element_type=jnp.float32
    )
    bias = factor * jnp.sum(grad_pre.astype(jnp.float32), axis=0, keepdims=True)
    extra = grads_ref.shape[0] - width
    first = lax.broadcasted_iota(jnp.int32, (extra, width), 0) == 0
    grads_ref[width:] = jnp.where(first, bias, 0.0)


def layer(left, right, weight, bias_term, cotangent, factor):
    width = weight.shape[0]
    return pl.pallas_call(
        functools.partial(layer_kernel, factor),
        out_shape=(
            jax.ShapeDtypeStruct(cotangent.shape, jnp.bfloat16),
            jax.ShapeDtypeStruct((width + 64, width), jnp.float32),
        ),
        in_specs=[VMEM] * 5,
        out_specs=(VMEM, VMEM),
        compiler_params=pltpu.CompilerParams(vmem_limit_bytes=16 * MIB),
        name="layer",
    )(left, right, weight, bias_term.reshape(1, -1), cotangent)


def spread(array, axis):
    copies = jnp.broadcast_to(array[None], (lax.axis_size(axis),) + array.shape)
    return lax.all_to_all(copies, axis, split_axis=0, concat_axis=0, tiled=True)


def scattered(array, axis):
    size = lax.axis_size(axis)
    parts = array.reshape(size, array.shape[0] // size, array.shape[1])
    return lax.all_to_all(parts, axis, split_axis=0, concat_axis=0, tiled=True)


def total_over_all(grads):
    share = jnp.sum(scattered(grads, REP), axis=0)
    share = jnp.sum(spread(share, "y"), axis=0)
    share = jnp.sum(spread(share, "z"), axis=0)
    return lax.all_gather(share, REP, axis=0, tiled=True)


def shards(
    features, tile_table, weight, bias_term, cotangent, adj_rows, adj_cols, adj_tiles, adj_count
):
    own_rows, width = features.shape
    rep_size = lax.axis_size(REP)
    lists = (adj_rows, adj_cols, adj_tiles, adj_count)
    ny, nz = lax.axis_size("y"), lax.axis_size("z")
    near_y = spread(features[:, :HALF], "y").reshape(ny * own_rows, HALF)
    near_z = spread(features[:, HALF:], "z").reshape(nz * own_rows, width - HALF)
    left = lax.all_gather(near_y, "z", axis=0, tiled=True)
    right = lax.all_gather(near_z, "y", axis=0, tiled=True)

    def by_z(col):
        return col

    def by_y(col):
        panel = col // BPD
        return ((panel % ny) * nz + panel // ny) * BPD + col % BPD

    rows = rep_size * own_rows
    left = scattered(spmm(by_z, lists, left, tile_table, rows), REP)
    right = scattered(spmm(by_y, lists, right, tile_table, rows), REP)
    factor = 1.0 / math.sqrt(nz * ny * rows)
    output, grads = layer(left, right, weight, bias_term, cotangent, factor)
    grads = total_over_all(grads)
    return (output, grads[:width], grads[width])


def solution(mesh):
    panels, rep = mesh.devices.shape
    ny = 8 if panels % 8 == 0 else 2
    devices = np.asarray(mesh.devices).reshape(panels // ny, ny, rep // 2, 2)
    rows = ("z", "y")
    return jax.shard_map(
        shards,
        mesh=Mesh(devices, ("z", "y", "x", "core")),
        in_specs=(
            P(rows + REP, None),
            P(),
            P(),
            P(),
            P(rows + REP, None),
            P(rows, REP, None),
            P(rows, REP, None),
            P(rows, REP, None),
            P(rows, REP),
        ),
        out_specs=(P(rows + REP, None), P(), P()),
        check_vma=False,
    )
```

time: 642 us -> 250 us (0.39)
  waiting for transfers between devices: 596 us -> 68.6 us
  blocking collectives: 18.2 us -> 137 us
  starting transfers between devices: 0.08 us -> 14 us
    psum x1 -> x0, waiting for transfers between devices: 459 us -> none  [shards(): grads = lax.psum(grads, ('rows', 'rep'))]
    all_to_all x1 -> x6, blocking collectives: 18.2 us -> 118 us  [the longest x4 91.9 us: spread(): return lax.all_to_all(copies, axis, split_axis=0, concat_axis=0, tiled=True)]
    all_gather x1 -> x2, waiting for transfers between devices: 136 us -> 68.6 us  [the longest x1 36.3 us: shards(): left = lax.all_gather(near_y, 'z', axis=0, tiled=True)]
    all_gather x0 -> x1, blocking collectives: none -> 18.9 us  [total_over_all(): return lax.all_gather(share, REP, axis=0, tiled=True)]
    all_to_all x0 -> x1, starting transfers between devices: none -> 14 us  [scattered(): return lax.all_to_all(parts, axis, split_axis=0, concat_axis=0, tiled=True)]
  transfers between devices with their start and end apart: 2 -> 3, of which waited for: 2 -> 2; matrix products, arithmetic and copies ran while one was open for 0% -> 0% of each run, Pallas kernels for 0% -> 5%
where the time goes in v2:
time: 250 us; the launch traced here: 249 us
  blocking collectives  137 us (55%)
  waiting for transfers between devices  68.6 us (27%)
  between operations  14.8 us (6%)
  starting transfers between devices  14 us (6%)
  Pallas kernels  12.2 us (5%)
    all_to_all x4, blocking collectives, spread(): return lax.all_to_all(copies, axis, split_axis=0, concat_axis=0, tiled=True)  91.9 us
    all_gather x1, waiting for transfers between devices, shards(): left = lax.all_gather(near_y, 'z', axis=0, tiled=True)  36.3 us
    all_gather x1, waiting for transfers between devices, shards(): right = lax.all_gather(near_z, 'y', axis=0, tiled=True)  32.3 us
    all_to_all x2, blocking collectives, scattered(): return lax.all_to_all(parts, axis, split_axis=0, concat_axis=0, tiled=True)  26.3 us
    all_gather x1, blocking collectives, total_over_all(): return lax.all_gather(share, REP, axis=0, tiled=True)  18.9 us
    all_to_all x1, starting transfers between devices, scattered(): return lax.all_to_all(parts, axis, split_axis=0, concat_axis=0, tiled=True)  14 us
    pallas_call x2, Pallas kernels, spmm(): pl.pallas_call(functools.partial(spmm_kernel, place), out_shape=jax.Shape...  11.3 us
  transfers between devices with their start and end apart: 3, of which 2 were waited for; matrix products, arithmetic and copies ran while one was open for 0% of the time, Pallas kernels for 5%

profile of v2, /device:TPU:1, one launch (start us, length us, event | category | flops | bytes accessed | tf_op | source)
XLA Modules:
  0.0 249.1 jit_solution(11210313556350071284)
XLA Ops:
  7.2 0.0 all-gather.3.cloned.1.call-start
  7.2 0.8 fusion
  8.0 16.9 %all_to_all.35 = bf16[8,128,128]{2,1,0:T(8,128)(2,1)} all-to-all(bf16[8,128,128]{2,1,0:T(8,128)(2,1)S(1)} %broadcast_in_dim.8), channel_id=1, replica_groups=mesh['z'=12,'y'=8,'x'=4,'core'=2] {'y'}, dimensions={0} | all-to-all | bytes 524288 | tf_op jit(solution)/shard_map/all_to_all | solution.py:140
  24.9 0.0 all-gather.3.cloned.1.call-update
  24.9 0.0 all-gather.5.cloned.1.call-start
  25.0 0.1 broadcast_in_dim.9
  25.1 31.6 %all_to_all.36 = bf16[12,128,128]{2,1,0:T(8,128)(2,1)} all-to-all(bf16[12,128,128]{2,1,0:T(8,128)(2,1)S(1)} %broadcast_in_dim.9), channel_id=1, replica_groups=mesh['z'=12,'y'=8,'x'=4,'core'=2] {'z'}, dimensions={0} | all-to-all | bytes 786432 | tf_op jit(solution)/shard_map/all_to_all | solution.py:140
  56.6 0.0 all-gather.5.cloned.1.call-update
  57.3 36.3 %all-gather.3.cloned.1.call-done.features_ref = bf16[12288,128]{1,0:T(8,128)(2,1)} async-done(((bf16[1024,128]{1,0:T(8,128)(2,1)}), bf16[12288,128]{1,0:T(8,128)(2,1)}) %all-gather.3.cloned.1.call-update) | async-done | bytes 3145744 | tf_op jit(solution)/shard_map/all_gather | solution.py:165
  93.6 5.7 %spmm.2 = bf16[1024,128]{1,0:T(8,128)(2,1)} custom-call(s32[1,1,48]{2,1,0:T(1,128)} %rows_ref.3, s32[1,1,48]{2,1,0:T(1,128)} %cols_ref.3, s32[1,1,48]{2,1,0:T(1,128)} %tiles_ref.3, s32[1,1]{1,0:T(1,128)S(6)} %copy.12.count_ref, bf16[12288,128]{1,0:T(8,128)(2,1)} %all-gather.3.cloned.1.call-done.features_ref, bf16[64,64,64]{2,1,0:T(8,128)(2,1)} %table_ref.3), custom_call_target="tpu_custom_call" | custom-call | tf_op jit(solution)/shard_map/spmm/pallas_call | solution.py:80
  99.3 0.0 copy-start
  99.3 0.0 copy-start.1
  99.3 0.0 copy-start.2
  99.3 14.0 %all-to-all-start.1 = ((bf16[8,128,128]{2,1,0:T(8,128)(2,1)}), bf16[8,128,128]{2,1,0:T(8,128)(2,1)S(1)}, u32[]{:S(2)}, u32[]{:S(2)}) async-start(bf16[8,128,128]{2,1,0:T(8,128)(2,1)} %bitcast.10), calls=%async_computation.1 | async-start | bytes 524288 | tf_op jit(solution)/shard_map/all_to_all | solution.py:146
  113.3 32.3 %all-gather.5.cloned.1.call-done.features_ref = bf16[12288,128]{1,0:T(8,128)(2,1)} async-done(((bf16[1536,128]{1,0:T(8,128)(2,1)}), bf16[12288,128]{1,0:T(8,128)(2,1)}) %all-gather.5.cloned.1.call-update) | async-done | bytes 3145744 | tf_op jit(solution)/shard_map/all_gather | solution.py:166
  145.6 5.7 %spmm.3 = bf16[1024,128]{1,0:T(8,128)(2,1)} custom-call(s32[1,1,48]{2,1,0:T(1,128)} %rows_ref.3, s32[1,1,48]{2,1,0:T(1,128)} %cols_ref.3, s32[1,1,48]{2,1,0:T(1,128)} %tiles_ref.3, s32[1,1]{1,0:T(1,128)S(6)} %copy.12.count_ref, bf16[12288,128]{1,0:T(8,128)(2,1)} %all-gather.5.cloned.1.call-done.features_ref, bf16[64,64,64]{2,1,0:T(8,128)(2,1)} %table_ref.3), custom_call_target="tpu_custom_call" | custom-call | tf_op jit(solution)/shard_map/spmm/pallas_call | solution.py:80
  151.3 0.0 all-to-all-done.1.left_ref
  151.3 15.4 %all_to_all.37.right_ref = bf16[8,128,128]{2,1,0:T(8,128)(2,1)S(1)} all-to-all(bf16[8,128,128]{2,1,0:T(8,128)(2,1)} %bitcast.11), channel_id=1, replica_groups=mesh['z'=12,'y'=8,'x'=4,'core'=2] {'x','core'}, dimensions={0} | all-to-all | bytes 524288 | tf_op jit(solution)/shard_map/all_to_all | solution.py:146
  166.7 0.0 copy-done
  166.7 0.0 copy-done.1
  166.7 0.0 copy-done.2
  166.7 0.9 layer.1
  167.5 10.9 %all_to_all.38 = f32[8,40,256]{2,1,0:T(8,128)S(1)} all-to-all(f32[8,40,256]{2,1,0:T(8,128)S(1)} %bitcast.7), channel_id=1, replica_groups=mesh['z'=12,'y'=8,'x'=4,'core'=2] {'x','core'}, dimensions={0} | all-to-all | bytes 655360 | tf_op jit(solution)/shard_map/all_to_all | solution.py:146
  178.5 15.6 %all_to_all.39 = f32[8,40,256]{2,1,0:T(8,128)S(1)} all-to-all(f32[8,40,256]{2,1,0:T(8,128)S(1)} %broadcast_in_dim.10), channel_id=1, replica_groups=mesh['z'=12,'y'=8,'x'=4,'core'=2] {'y'}, dimensions={0} | all-to-all | bytes 655360 | tf_op jit(solution)/shard_map/all_to_all | solution.py:140
  194.1 27.9 %all_to_all.40 = f32[12,40,256]{2,1,0:T(8,128)S(1)} all-to-all(f32[12,40,256]{2,1,0:T(8,128)S(1)} %broadcast_in_dim.11), channel_id=1, replica_groups=mesh['z'=12,'y'=8,'x'=4,'core'=2] {'z'}, dimensions={0} | all-to-all | bytes 983040 | tf_op jit(solution)/shard_map/all_to_all | solution.py:140
  222.0 18.9 %all_gather.11 = f32[320,256]{1,0:T(8,128)S(1)} all-gather(f32[40,256]{1,0:T(8,128)S(1)} %reduce_sum.29), channel_id=1, replica_groups=mesh['z'=12,'y'=8,'x'=4,'core'=2] {'x','core'}, dimensions={0}, use_global_device_ids=true | all-gather | bytes 368640 | tf_op jit(solution)/shard_map/all_gather | solution.py:153
  240.9 0.7 slice.16
  241.7 0.6 slice.17
  (6 shorter events, 0.2 us)
Async XLA Ops:
  7.2 86.4 %all-gather.3.cloned.1.call-start = ((), (), s32[]{:S(2)}) async-start(), calls=%async_computation.7 | async-start | bytes 3407872 | tf_op jit(solution)/shard_map/all_gather | solution.py:165
  24.9 120.6 %all-gather.5.cloned.1.call-start = ((), (), s32[]{:S(2)}) async-start(), calls=%async_computation.8 | async-start | bytes 3538944 | tf_op jit(solution)/shard_map/all_gather | solution.py:166
  99.3 67.4 %copy-start = (bf16[256,256]{1,0:T(8,128)(2,1)S(1)}, bf16[256,256]{1,0:T(8,128)(2,1)}, u32[]{:S(2)}) copy-start(bf16[256,256]{1,0:T(8,128)(2,1)} %weight_ref.1) | copy-start | bytes 393220
  99.3 67.4 %copy-start.1 = (bf16[128,256]{1,0:T(8,128)(2,1)S(1)}, bf16[128,256]{1,0:T(8,128)(2,1)}, u32[]{:S(2)}) copy-start(bf16[128,256]{1,0:T(8,128)(2,1)} %cotangent_ref.1) | copy-start | bytes 196612
  99.3 67.4 %copy-start.2 = (f32[256]{0:T(256)S(1)}, f32[256]{0:T(256)}, u32[]{:S(2)}) copy-start(f32[256]{0:T(256)} %param.12) | copy-start | bytes 3076
  99.3 52.0 %all-to-all-start.1 = ((bf16[8,128,128]{2,1,0:T(8,128)(2,1)}), bf16[8,128,128]{2,1,0:T(8,128)(2,1)S(1)}, u32[]{:S(2)}, u32[]{:S(2)}) async-start(bf16[8,128,128]{2,1,0:T(8,128)(2,1)} %bitcast.10), calls=%async_computation.1 | async-start | bytes 524288 | tf_op jit(solution)/shard_map/all_to_all | solution.py:146
Sparse Core Ops, SparseCore 0:
  25.1 68.4 all-gather.2
  96.0 49.5 all-gather.4

commit v3 on v2

--- a/solution.py
+++ b/solution.py
@@ -11,7 +11,7 @@
 
 BLOCK = 64
 BPD = 2
-UNROLL = 4
+UNROLL = 12
 HALF = 128
 MIB = 1024 * 1024
 REP = ("x", "core")
@@ -21,26 +21,14 @@
 
 
 def spmm_kernel(
-    place,
-    rows_ref,
-    cols_ref,
-    tiles_ref,
-    count_ref,
-    features_ref,
-    table_ref,
-    out_ref,
-    picked,
-    table,
-    total,
-    sems,
-    table_sem,
+    rows_ref, tiles_ref, count_ref, which_ref, start_ref, table_ref, *refs
 ):
+    *sources, out_ref, picked, table, total, sems, table_sem = refs
     count = count_ref[0, 0]
 
-    def fetch(s):
-        start = pl.multiple_of(place(cols_ref[0, 0, s]) * BLOCK, BLOCK)
+    def fetch(s, source, start):
         return pltpu.make_async_copy(
-            features_ref.at[pl.ds(start, BLOCK)], picked.at[s], sems.at[s]
+            source.at[pl.ds(start, BLOCK)], picked.at[s], sems.at[s]
         )
 
     steps = (count + UNROLL - 1) // UNROLL
@@ -49,7 +37,17 @@
 
     def begin(i, carry):
         for k in range(UNROLL):
-            fetch(i * UNROLL + k).start()
+            s = i * UNROLL + k
+            start = pl.multiple_of(start_ref[s], BLOCK)
+            if len(sources) == 1:
+                fetch(s, sources[0], start).start()
+                continue
+            for n, source in enumerate(sources):
+
+                @pl.when(which_ref[s] == n)
+                def _():
+                    fetch(s, source, start).start()
+
         return carry
 
     lax.fori_loop(0, steps, begin, 0)
@@ -57,30 +55,28 @@
     table_copy.wait()
 
     def step(i, carry):
-        products = []
+        for k in range(UNROLL):
+            fetch(i * UNROLL + k, sources[0], 0).wait()
         for k in range(UNROLL):
             s = i * UNROLL + k
-            fetch(s).wait()
             product = jnp.dot(
                 table[tiles_ref[0, 0, s]], picked[s], preferred_element_type=jnp.float32
             )
-            products.append(jnp.where(s < count, product, 0.0))
-        for k in range(UNROLL):
-            row = pl.multiple_of(rows_ref[0, 0, i * UNROLL + k] * BLOCK, BLOCK)
-            total[pl.ds(row, BLOCK)] += products[k]
+            row = pl.multiple_of(rows_ref[0, 0, s] * BLOCK, BLOCK)
+            total[pl.ds(row, BLOCK)] += jnp.where(s < count, product, 0.0)
         return carry
 
     lax.fori_loop(0, steps, step, 0)
     out_ref[...] = total[...].astype(out_ref.dtype)
 
 
-def spmm(place, lists, gathered, tile_table, out_rows):
-    slots = lists[0].shape[-1]
-    width = gathered.shape[1]
+def spmm(lists, which, start, sources, tile_table, out_rows):
+    slots = start.shape[0]
+    width = sources[0].shape[1]
     return pl.pallas_call(
-        functools.partial(spmm_kernel, place),
+        spmm_kernel,
         out_shape=jax.ShapeDtypeStruct((out_rows, width), jnp.bfloat16),
-        in_specs=[SMEM, SMEM, SMEM, SMEM, HBM, HBM],
+        in_specs=[SMEM] * 5 + [HBM] * (1 + len(sources)),
         out_specs=VMEM,
         scratch_shapes=[
             pltpu.VMEM((slots, BLOCK, width), jnp.bfloat16),
@@ -91,7 +87,7 @@
         ],
         compiler_params=pltpu.CompilerParams(vmem_limit_bytes=58 * MIB),
         name="spmm",
-    )(*lists, gathered, tile_table)
+    )(*lists, which, start, tile_table, *sources)
 
 
 def layer_kernel(
@@ -111,22 +107,23 @@
         cotangent_ref[...].astype(jnp.float32) * (sigma * (1.0 + pre * (1.0 - sigma)))
     ).astype(jnp.bfloat16)
     width = grad_pre.shape[1]
-    grads_ref[:width] = factor * lax.dot_general(
+    weight_grad = factor * lax.dot_general(
         agg, grad_pre, (((0,), (0,)), ((), ())), preferred_element_type=jnp.float32
     )
+    grads_ref[:width] = weight_grad.astype(grads_ref.dtype)
     bias = factor * jnp.sum(grad_pre.astype(jnp.float32), axis=0, keepdims=True)
     extra = grads_ref.shape[0] - width
     first = lax.broadcasted_iota(jnp.int32, (extra, width), 0) == 0
-    grads_ref[width:] = jnp.where(first, bias, 0.0)
-
-
-def layer(left, right, weight, bias_term, cotangent, factor):
+    grads_ref[width:] = jnp.where(first, bias, 0.0).astype(grads_ref.dtype)
+
+
+def layer(left, right, weight, bias_term, cotangent, factor, grad_rows):
     width = weight.shape[0]
     return pl.pallas_call(
         functools.partial(layer_kernel, factor),
         out_shape=(
             jax.ShapeDtypeStruct(cotangent.shape, jnp.bfloat16),
-            jax.ShapeDtypeStruct((width + 64, width), jnp.float32),
+            jax.ShapeDtypeStruct((grad_rows, width), jnp.bfloat16),
         ),
         in_specs=[VMEM] * 5,
         out_specs=(VMEM, VMEM),
@@ -146,11 +143,34 @@
     return lax.all_to_all(parts, axis, split_axis=0, concat_axis=0, tiled=True)
 
 
+def summed(parts):
+    total = parts[0].astype(jnp.float32)
+    for part in parts[1:]:
+        total += part.astype(jnp.float32)
+    return total.astype(jnp.bfloat16)
+
+
 def total_over_all(grads):
-    share = jnp.sum(scattered(grads, REP), axis=0)
-    share = jnp.sum(spread(share, "y"), axis=0)
-    share = jnp.sum(spread(share, "z"), axis=0)
-    return lax.all_gather(share, REP, axis=0, tiled=True)
+    share = summed(scattered(grads, "z"))
+    share = summed(spread(share, "y"))
+    share = summed(spread(share, REP))
+    return spread(share, "z").reshape(grads.shape).astype(jnp.float32)
+
+
+def both_ways(block, axis):
+    n = lax.axis_size(axis)
+    up = [(i, (i + 1) % n) for i in range(n)]
+    down = [(i, (i - 1) % n) for i in range(n)]
+    before, after = [block], [block]
+    for _ in range(n // 2 - 1):
+        before.append(lax.ppermute(before[-1], axis, up))
+        after.append(lax.ppermute(after[-1], axis, down))
+    half = block.shape[0] // 2
+    far = [
+        lax.ppermute(before[-1][:half], axis, up),
+        lax.ppermute(after[-1][half:], axis, down),
+    ]
+    return before + after[:0:-1] + far
 
 
 def shards(
@@ -158,25 +178,29 @@
 ):
     own_rows, width = features.shape
     rep_size = lax.axis_size(REP)
-    lists = (adj_rows, adj_cols, adj_tiles, adj_count)
+    lists = (adj_rows, adj_tiles, adj_count)
     ny, nz = lax.axis_size("y"), lax.axis_size("z")
     near_y = spread(features[:, :HALF], "y").reshape(ny * own_rows, HALF)
     near_z = spread(features[:, HALF:], "z").reshape(nz * own_rows, width - HALF)
     left = lax.all_gather(near_y, "z", axis=0, tiled=True)
-    right = lax.all_gather(near_z, "y", axis=0, tiled=True)
-
-    def by_z(col):
-        return col
-
-    def by_y(col):
-        panel = col // BPD
-        return ((panel % ny) * nz + panel // ny) * BPD + col % BPD
+    right = both_ways(near_z, "y")
+
+    cols = adj_cols[0, 0]
+    panel = cols // BPD
+    behind = (lax.axis_index("y") - panel) % ny
+    start = (panel // ny * BPD + cols % BPD) * BLOCK
+    half = near_z.shape[0] // 2
+    upper = start >= half
+    far = behind == ny // 2
+    which = jnp.where(far, ny - 1 + upper.astype(jnp.int32), behind - (behind > ny // 2))
+    start = jnp.where(far & upper, start - half, start)
 
     rows = rep_size * own_rows
-    left = scattered(spmm(by_z, lists, left, tile_table, rows), REP)
-    right = scattered(spmm(by_y, lists, right, tile_table, rows), REP)
+    left = scattered(spmm(lists, which, cols * BLOCK, [left], tile_table, rows), REP)
+    right = scattered(spmm(lists, which, start, right, tile_table, rows), REP)
     factor = 1.0 / math.sqrt(nz * ny * rows)
-    output, grads = layer(left, right, weight, bias_term, cotangent, factor)
+    grad_rows = -(-(width + 8) // (8 * nz)) * 8 * nz
+    output, grads = layer(left, right, weight, bias_term, cotangent, factor, grad_rows)
     grads = total_over_all(grads)
     return (output, grads[:width], grads[width])
 

time: 250 us -> 204 us (0.82)
  waiting for transfers between devices: 68.6 us -> 23.7 us
  blocking collectives: 137 us -> 108 us
  starting transfers between devices: 14 us -> 41.1 us
  Pallas kernels: 12.2 us -> 8.98 us
  other arithmetic: 0.08 us -> 2.99 us
    all_gather x1, waiting for transfers between devices: 36.3 us -> 0.01 us  [shards(): left = lax.all_gather(near_y, 'z', axis=0, tiled=True)]
    all_gather x1 -> x0, waiting for transfers between devices: 32.3 us -> none  [shards(): right = lax.all_gather(near_z, 'y', axis=0, tiled=True)]
    ppermute x0 -> x8, starting transfers between devices: none -> 24.2 us  [the longest x3 9.76 us: both_ways(): after.append(lax.ppermute(after[-1], axis, down))]
    ppermute x0 -> x8, waiting for transfers between devices: none -> 21.2 us  [the longest x3 13.1 us: both_ways(): after.append(lax.ppermute(after[-1], axis, down))]
    all_gather x1 -> x0, blocking collectives: 18.9 us -> none  [total_over_all(): return lax.all_gather(share, REP, axis=0, tiled=True)]
    all_to_all x4 -> x5, blocking collectives: 91.9 us -> 84 us  [spread(): return lax.all_to_all(copies, axis, split_axis=0, concat_axis=0, tiled=True)]
    pallas_call x2, Pallas kernels: 11.3 us -> 8.12 us  [spmm(): pl.pallas_call(spmm_kernel, out_shape=jax.ShapeDtypeStruct((out_rows, wid...]
    all_to_all x1, starting transfers between devices: 14 us -> 16.9 us  [scattered(): return lax.all_to_all(parts, axis, split_axis=0, concat_axis=0, tiled=True)]
  transfers between devices with their start and end apart: 3 -> 10, of which waited for: 2 -> 9; matrix products, arithmetic and copies ran while one was open for 0% -> 1% of each run, Pallas kernels for 5% -> 4%
where the time goes in v3:
time: 204 us; the launch traced here: 203 us
  blocking collectives  108 us (53%)
  starting transfers between devices  41.1 us (20%)
  waiting for transfers between devices  23.7 us (12%)
  between operations  14.9 us (7%)
  Pallas kernels  8.98 us (4%)
  other arithmetic  2.99 us (1%)
  local copies, waits for them, and re-layouts  2.88 us (1%)
    all_to_all x5, blocking collectives, spread(): return lax.all_to_all(copies, axis, split_axis=0, concat_axis=0, tiled=True)  84 us
    all_to_all x2, blocking collectives, scattered(): return lax.all_to_all(parts, axis, split_axis=0, concat_axis=0, tiled=True)  24.1 us
    all_to_all x1, starting transfers between devices, scattered(): return lax.all_to_all(parts, axis, split_axis=0, concat_axis=0, tiled=True)  16.9 us
    ppermute x3, waiting for transfers between devices, both_ways(): after.append(lax.ppermute(after[-1], axis, down))  13.1 us
    ppermute x3, starting transfers between devices, both_ways(): after.append(lax.ppermute(after[-1], axis, down))  9.76 us
    pallas_call x2, Pallas kernels, spmm(): pl.pallas_call(spmm_kernel, out_shape=jax.ShapeDtypeStruct((out_rows, wid...  8.12 us
    ppermute x3, starting transfers between devices, both_ways(): before.append(lax.ppermute(before[-1], axis, up))  7.18 us
    ppermute x1, waiting for transfers between devices, both_ways(): lax.ppermute(before[-1][:half], axis, up)  5.8 us
  transfers between devices with their start and end apart: 10, of which 9 were waited for; matrix products, arithmetic and copies ran while one was open for 1% of the time, Pallas kernels for 4%

profile of v3, /device:TPU:1, one launch (start us, length us, event | category | flops | bytes accessed | tf_op | source)
XLA Modules:
  0.0 202.6 jit_solution(1304507853603534614)
XLA Ops:
  7.2 0.0 all-gather.2.cloned.1.call-start
  7.2 0.8 fusion.9
  8.0 16.9 %all_to_all.40 = bf16[8,128,128]{2,1,0:T(8,128)(2,1)} all-to-all(bf16[8,128,128]{2,1,0:T(8,128)(2,1)S(1)} %broadcast_in_dim.16), channel_id=1, replica_groups=mesh['z'=12,'y'=8,'x'=4,'core'=2] {'y'}, dimensions={0} | all-to-all | bytes 524288 | tf_op jit(solution)/shard_map/all_to_all | solution.py:137
  24.9 0.0 all-gather.2.cloned.1.call-update
  24.9 0.1 broadcast_in_dim.17
  25.0 31.5 %all_to_all.41 = bf16[12,128,128]{2,1,0:T(8,128)(2,1)S(1)} all-to-all(bf16[12,128,128]{2,1,0:T(8,128)(2,1)S(1)} %broadcast_in_dim.17), channel_id=1, replica_groups=mesh['z'=12,'y'=8,'x'=4,'core'=2] {'z'}, dimensions={0} | all-to-all | bytes 786432 | tf_op jit(solution)/shard_map/all_to_all | solution.py:137
  56.5 1.9 collective-permute-start.3
  58.4 3.4 %collective-permute-start = (bf16[1536,128]{1,0:T(8,128)(2,1)S(1)}, bf16[1536,128]{1,0:T(8,128)(2,1)S(1)}, u32[]{:S(2)}, u32[]{:S(2)}) collective-permute-start(bf16[1536,128]{1,0:T(8,128)(2,1)S(1)} %bitcast.36), channel_id=1, source_target_pairs={{0,8},{8,16},{16,24},{24,32},{32,40},{40,48},{48,56},{56,0},{1,9},... | collective-permute-start | bytes 1179656 | tf_op jit(solution)/shard_map/ppermute | solution.py:166
  61.8 3.6 %collective-permute-done.3.refs_6_ = bf16[1536,128]{1,0:T(8,128)(2,1)S(1)} collective-permute-done((bf16[1536,128]{1,0:T(8,128)(2,1)S(1)}, bf16[1536,128]{1,0:T(8,128)(2,1)S(1)}, u32[]{:S(2)}, u32[]{:S(2)}) %collective-permute-start.3) | collective-permute-done | bytes 393248 | tf_op jit(solution)/shard_map/ppermute | solution.py:167
  65.4 3.2 %collective-permute-start.4 = (bf16[1536,128]{1,0:T(8,128)(2,1)S(1)}, bf16[1536,128]{1,0:T(8,128)(2,1)S(1)}, u32[]{:S(2)}, u32[]{:S(2)}) collective-permute-start(bf16[1536,128]{1,0:T(8,128)(2,1)S(1)} %collective-permute-done.3.refs_6_), channel_id=1, source_target_pairs={{0,56},{8,0},{16,8},{24,16},{32,24},{40,32},{48,40},{56,48},{1,57}... | collective-permute-start | bytes 1179656 | tf_op jit(solution)/shard_map/ppermute | solution.py:167
  68.6 0.9 collective-permute-done.refs_1_
  69.5 1.9 collective-permute-start.1
  72.0 5.6 %collective-permute-done.4.refs_5_ = bf16[1536,128]{1,0:T(8,128)(2,1)S(1)} collective-permute-done((bf16[1536,128]{1,0:T(8,128)(2,1)S(1)}, bf16[1536,128]{1,0:T(8,128)(2,1)S(1)}, u32[]{:S(2)}, u32[]{:S(2)}) %collective-permute-start.4) | collective-permute-done | bytes 393248 | tf_op jit(solution)/shard_map/ppermute | solution.py:167
  77.6 4.7 %collective-permute-start.5 = (bf16[1536,128]{1,0:T(8,128)(2,1)S(1)}, bf16[1536,128]{1,0:T(8,128)(2,1)S(1)}, u32[]{:S(2)}, u32[]{:S(2)}) collective-permute-start(bf16[1536,128]{1,0:T(8,128)(2,1)S(1)} %collective-permute-done.4.refs_5_), channel_id=1, source_target_pairs={{0,56},{8,0},{16,8},{24,16},{32,24},{40,32},{48,40},{56,48},{1,57}... | collective-permute-start | bytes 1179656 | tf_op jit(solution)/shard_map/ppermute | solution.py:167
  82.3 0.4 collective-permute-done.1.refs_2_
  82.6 1.9 collective-permute-start.2
  84.6 1.2 bitcast_multiply_fusion
  85.7 1.2 and_select_fusion
  86.9 4.0 %collective-permute-done.5.refs_4_ = bf16[1536,128]{1,0:T(8,128)(2,1)S(1)} collective-permute-done((bf16[1536,128]{1,0:T(8,128)(2,1)S(1)}, bf16[1536,128]{1,0:T(8,128)(2,1)S(1)}, u32[]{:S(2)}, u32[]{:S(2)}) %collective-permute-start.5) | collective-permute-done | bytes 393248 | tf_op jit(solution)/shard_map/ppermute | solution.py:167
  90.9 5.3 %collective-permute-start.7 = (bf16[768,128]{1,0:T(8,128)(2,1)S(1)}, bf16[768,128]{1,0:T(8,128)(2,1)S(1)}, u32[]{:S(2)}, u32[]{:S(2)}) collective-permute-start(bf16[768,128]{1,0:T(8,128)(2,1)S(1)} %slice.65), channel_id=1, source_target_pairs={{0,56},{8,0},{16,8},{24,16},{32,24},{40,32},{48,40},{56,48},{1,57}... | collective-permute-start | bytes 589832 | tf_op jit(solution)/shard_map/ppermute | solution.py:171
  96.2 0.4 collective-permute-done.2.refs_3_
  96.6 1.9 collective-permute-start.6
  98.6 0.5 compare_select_fusion.8.which_ref
  99.1 0.7 collective-permute-done.7.refs_8_
  99.8 5.8 %collective-permute-done.6.refs_7_ = bf16[768,128]{1,0:T(8,128)(2,1)S(1)} collective-permute-done((bf16[768,128]{1,0:T(8,128)(2,1)S(1)}, bf16[768,128]{1,0:T(8,128)(2,1)S(1)}, u32[]{:S(2)}, u32[]{:S(2)}) %collective-permute-start.6) | collective-permute-done | bytes 196640 | tf_op jit(solution)/shard_map/ppermute | solution.py:170
  105.6 0.0 copy-done.3
  105.6 0.0 copy-done.6
  105.6 0.0 copy-done.7
  105.6 0.0 copy-done.8
  105.6 0.0 copy-done.9
  105.6 0.0 copy-done.4
  105.6 0.6 copy-done.11
  106.3 4.0 %spmm.3 = bf16[1024,128]{1,0:T(8,128)(2,1)} custom-call(s32[1,1,48]{2,1,0:T(1,128)} %rows_ref.3, s32[1,1,48]{2,1,0:T(1,128)} %tiles_ref.3, s32[1,1]{1,0:T(1,128)S(6)} %copy.12.count_ref, s32[48]{0:T(128)} %compare_select_fusion.8.which_ref, s32[48]{0:T(128)} %get-tuple-element.7.start_ref, bf16[64,64,64]{2,1,0:T(8,128)(2,1)} %table_ref.3, ...), custom_call_target="tpu_custom_call" | custom-call | tf_op jit(solution)/shard_map/spmm/pallas_call | solution.py:76
  110.3 0.0 copy-start
  110.3 0.0 copy-start.1
  110.3 0.0 copy-start.2
  110.3 16.9 %all-to-all-start.3 = ((bf16[8,128,128]{2,1,0:T(8,128)(2,1)}), bf16[8,128,128]{2,1,0:T(8,128)(2,1)S(1)}, u32[]{:S(2)}, u32[]{:S(2)}) async-start(bf16[8,128,128]{2,1,0:T(8,128)(2,1)} %bitcast.38), calls=%async_computation.3 | async-start | bytes 524288 | tf_op jit(solution)/shard_map/all_to_all | solution.py:143
  127.2 4.1 %spmm.2 = bf16[1024,128]{1,0:T(8,128)(2,1)} custom-call(s32[1,1,48]{2,1,0:T(1,128)} %rows_ref.3, s32[1,1,48]{2,1,0:T(1,128)} %tiles_ref.3, s32[1,1]{1,0:T(1,128)S(6)} %copy.12.count_ref, s32[48]{0:T(128)} %compare_select_fusion.8.which_ref, s32[48]{0:T(128)} %get-tuple-element.12.start_ref, bf16[64,64,64]{2,1,0:T(8,128)(2,1)} %table_ref.3, ...), custom_call_target="tpu_custom_call" | custom-call | tf_op jit(solution)/shard_map/spmm/pallas_call | solution.py:76
  131.3 2.4 %all-to-all-done.3.right_ref = bf16[8,128,128]{2,1,0:T(8,128)(2,1)S(1)} async-done(((bf16[8,128,128]{2,1,0:T(8,128)(2,1)}), bf16[8,128,128]{2,1,0:T(8,128)(2,1)S(1)}, u32[]{:S(2)}, u32[]{:S(2)}) %all-to-all-start.3) | async-done | bytes 262176 | tf_op jit(solution)/shard_map/all_to_all | solution.py:143
  133.7 10.8 %all_to_all.42.left_ref = bf16[8,128,128]{2,1,0:T(8,128)(2,1)S(1)} all-to-all(bf16[8,128,128]{2,1,0:T(8,128)(2,1)} %bitcast.39), channel_id=1, replica_groups=mesh['z'=12,'y'=8,'x'=4,'core'=2] {'x','core'}, dimensions={0} | all-to-all | bytes 524288 | tf_op jit(solution)/shard_map/all_to_all | solution.py:143
  144.6 0.0 copy-done.2
  144.6 0.9 layer.1
  145.4 13.3 %all_to_all.43 = bf16[12,24,256]{2,1,0:T(8,128)(2,1)S(1)} all-to-all(bf16[12,24,256]{2,1,0:T(8,128)(2,1)S(1)} %bitcast.33), channel_id=1, replica_groups=mesh['z'=12,'y'=8,'x'=4,'core'=2] {'z'}, dimensions={0} | all-to-all | bytes 294912 | tf_op jit(solution)/shard_map/all_to_all | solution.py:143
  158.8 10.6 %all_to_all.44 = bf16[8,24,256]{2,1,0:T(8,128)(2,1)S(1)} all-to-all(bf16[8,24,256]{2,1,0:T(8,128)(2,1)S(1)} %broadcast_in_dim.19), channel_id=1, replica_groups=mesh['z'=12,'y'=8,'x'=4,'core'=2] {'y'}, dimensions={0} | all-to-all | bytes 196608 | tf_op jit(solution)/shard_map/all_to_all | solution.py:137
  169.4 11.4 %all_to_all.45 = bf16[8,24,256]{2,1,0:T(8,128)(2,1)S(1)} all-to-all(bf16[8,24,256]{2,1,0:T(8,128)(2,1)S(1)} %broadcast_in_dim.41), channel_id=1, replica_groups=mesh['z'=12,'y'=8,'x'=4,'core'=2] {'x','core'}, dimensions={0} | all-to-all | bytes 196608 | tf_op jit(solution)/shard_map/all_to_all | solution.py:137
  180.9 13.5 %all_to_all.46 = bf16[12,24,256]{2,1,0:T(8,128)(2,1)S(1)} all-to-all(bf16[12,24,256]{2,1,0:T(8,128)(2,1)S(1)} %broadcast_in_dim.43), channel_id=1, replica_groups=mesh['z'=12,'y'=8,'x'=4,'core'=2] {'z'}, dimensions={0} | all-to-all | bytes 294912 | tf_op jit(solution)/shard_map/all_to_all | solution.py:137
  194.5 0.6 slice.70
  195.0 0.7 slice.69
  (24 shorter events, 0.2 us)
Async XLA Ops:
  7.2 120.1 %all-gather.2.cloned.1.call-start = ((), (), s32[]{:S(2)}) async-start(), calls=%async_computation.8 | async-start | bytes 3407872 | tf_op jit(solution)/shard_map/all_gather | solution.py:185
  56.5 49.1 %copy-start.3 = (bf16[12,128,128]{2,1,0:T(8,128)(2,1)}, bf16[12,128,128]{2,1,0:T(8,128)(2,1)S(1)}, u32[]{:S(2)}) copy-start(bf16[12,128,128]{2,1,0:T(8,128)(2,1)S(1)} %all_to_all.41) | copy-start | bytes 1179652
  56.5 8.9 %collective-permute-start.3 = (bf16[1536,128]{1,0:T(8,128)(2,1)S(1)}, bf16[1536,128]{1,0:T(8,128)(2,1)S(1)}, u32[]{:S(2)}, u32[]{:S(2)}) collective-permute-start(bf16[1536,128]{1,0:T(8,128)(2,1)S(1)} %bitcast.35), channel_id=1, source_target_pairs={{0,56},{8,0},{16,8},{24,16},{32,24},{40,32},{48,40},{56,48},{1,57}... | collective-permute-start | bytes 1179656 | tf_op jit(solution)/shard_map/ppermute | solution.py:167
  58.4 11.0 %collective-permute-start = (bf16[1536,128]{1,0:T(8,128)(2,1)S(1)}, bf16[1536,128]{1,0:T(8,128)(2,1)S(1)}, u32[]{:S(2)}, u32[]{:S(2)}) collective-permute-start(bf16[1536,128]{1,0:T(8,128)(2,1)S(1)} %bitcast.36), channel_id=1, source_target_pairs={{0,8},{8,16},{16,24},{24,32},{32,40},{40,48},{48,56},{56,0},{1,9},... | collective-permute-start | bytes 1179656 | tf_op jit(solution)/shard_map/ppermute | solution.py:166
  65.4 40.2 %copy-start.6 = (bf16[1536,128]{1,0:T(8,128)(2,1)}, bf16[1536,128]{1,0:T(8,128)(2,1)S(1)}, u32[]{:S(2)}) copy-start(bf16[1536,128]{1,0:T(8,128)(2,1)S(1)} %collective-permute-done.3.refs_6_) | copy-start | bytes 1179652
  65.4 12.2 %collective-permute-start.4 = (bf16[1536,128]{1,0:T(8,128)(2,1)S(1)}, bf16[1536,128]{1,0:T(8,128)(2,1)S(1)}, u32[]{:S(2)}, u32[]{:S(2)}) collective-permute-start(bf16[1536,128]{1,0:T(8,128)(2,1)S(1)} %collective-permute-done.3.refs_6_), channel_id=1, source_target_pairs={{0,56},{8,0},{16,8},{24,16},{32,24},{40,32},{48,40},{56,48},{1,57}... | collective-permute-start | bytes 1179656 | tf_op jit(solution)/shard_map/ppermute | solution.py:167
  69.5 36.1 %copy-start.7 = (bf16[1536,128]{1,0:T(8,128)(2,1)}, bf16[1536,128]{1,0:T(8,128)(2,1)S(1)}, u32[]{:S(2)}) copy-start(bf16[1536,128]{1,0:T(8,128)(2,1)S(1)} %collective-permute-done.refs_1_) | copy-start | bytes 1179652
  69.5 13.2 %collective-permute-start.1 = (bf16[1536,128]{1,0:T(8,128)(2,1)S(1)}, bf16[1536,128]{1,0:T(8,128)(2,1)S(1)}, u32[]{:S(2)}, u32[]{:S(2)}) collective-permute-start(bf16[1536,128]{1,0:T(8,128)(2,1)S(1)} %collective-permute-done.refs_1_), channel_id=1, source_target_pairs={{0,8},{8,16},{16,24},{24,32},{32,40},{40,48},{48,56},{56,0},{1,9},... | collective-permute-start | bytes 1179656 | tf_op jit(solution)/shard_map/ppermute | solution.py:166
  77.6 28.0 %copy-start.8 = (bf16[1536,128]{1,0:T(8,128)(2,1)}, bf16[1536,128]{1,0:T(8,128)(2,1)S(1)}, u32[]{:S(2)}) copy-start(bf16[1536,128]{1,0:T(8,128)(2,1)S(1)} %collective-permute-done.4.refs_5_) | copy-start | bytes 1179652
  77.6 13.3 %collective-permute-start.5 = (bf16[1536,128]{1,0:T(8,128)(2,1)S(1)}, bf16[1536,128]{1,0:T(8,128)(2,1)S(1)}, u32[]{:S(2)}, u32[]{:S(2)}) collective-permute-start(bf16[1536,128]{1,0:T(8,128)(2,1)S(1)} %collective-permute-done.4.refs_5_), channel_id=1, source_target_pairs={{0,56},{8,0},{16,8},{24,16},{32,24},{40,32},{48,40},{56,48},{1,57}... | collective-permute-start | bytes 1179656 | tf_op jit(solution)/shard_map/ppermute | solution.py:167
  82.6 23.0 %copy-start.9 = (bf16[1536,128]{1,0:T(8,128)(2,1)}, bf16[1536,128]{1,0:T(8,128)(2,1)S(1)}, u32[]{:S(2)}) copy-start(bf16[1536,128]{1,0:T(8,128)(2,1)S(1)} %collective-permute-done.1.refs_2_) | copy-start | bytes 1179652
  82.6 14.0 %collective-permute-start.2 = (bf16[1536,128]{1,0:T(8,128)(2,1)S(1)}, bf16[1536,128]{1,0:T(8,128)(2,1)S(1)}, u32[]{:S(2)}, u32[]{:S(2)}) collective-permute-start(bf16[1536,128]{1,0:T(8,128)(2,1)S(1)} %collective-permute-done.1.refs_2_), channel_id=1, source_target_pairs={{0,8},{8,16},{16,24},{24,32},{32,40},{40,48},{48,56},{56,0},{1,9},... | collective-permute-start | bytes 1179656 | tf_op jit(solution)/shard_map/ppermute | solution.py:166
  90.9 14.7 %copy-start.4 = (bf16[1536,128]{1,0:T(8,128)(2,1)}, bf16[1536,128]{1,0:T(8,128)(2,1)S(1)}, u32[]{:S(2)}) copy-start(bf16[1536,128]{1,0:T(8,128)(2,1)S(1)} %collective-permute-done.5.refs_4_) | copy-start | bytes 1179652
  90.9 8.9 %collective-permute-start.7 = (bf16[768,128]{1,0:T(8,128)(2,1)S(1)}, bf16[768,128]{1,0:T(8,128)(2,1)S(1)}, u32[]{:S(2)}, u32[]{:S(2)}) collective-permute-start(bf16[768,128]{1,0:T(8,128)(2,1)S(1)} %slice.65), channel_id=1, source_target_pairs={{0,56},{8,0},{16,8},{24,16},{32,24},{40,32},{48,40},{56,48},{1,57}... | collective-permute-start | bytes 589832 | tf_op jit(solution)/shard_map/ppermute | solution.py:171
  96.6 9.0 %copy-start.5 = (bf16[1536,128]{1,0:T(8,128)(2,1)}, bf16[1536,128]{1,0:T(8,128)(2,1)S(1)}, u32[]{:S(2)}) copy-start(bf16[1536,128]{1,0:T(8,128)(2,1)S(1)} %collective-permute-done.2.refs_3_) | copy-start | bytes 1179652
  96.6 8.9 %collective-permute-start.6 = (bf16[768,128]{1,0:T(8,128)(2,1)S(1)}, bf16[768,128]{1,0:T(8,128)(2,1)S(1)}, u32[]{:S(2)}, u32[]{:S(2)}) collective-permute-start(bf16[768,128]{1,0:T(8,128)(2,1)S(1)} %slice.64), channel_id=1, source_target_pairs={{0,8},{8,16},{16,24},{24,32},{32,40},{40,48},{48,56},{56,0},{1,9},... | collective-permute-start | bytes 589832 | tf_op jit(solution)/shard_map/ppermute | solution.py:170
  99.8 5.9 %copy-start.10 = (bf16[768,128]{1,0:T(8,128)(2,1)}, bf16[768,128]{1,0:T(8,128)(2,1)S(1)}, u32[]{:S(2)}) copy-start(bf16[768,128]{1,0:T(8,128)(2,1)S(1)} %collective-permute-done.7.refs_8_) | copy-start | bytes 589828
  105.6 0.7 copy-start.11
  110.3 34.3 %copy-start = (bf16[256,256]{1,0:T(8,128)(2,1)S(1)}, bf16[256,256]{1,0:T(8,128)(2,1)}, u32[]{:S(2)}) copy-start(bf16[256,256]{1,0:T(8,128)(2,1)} %weight_ref.1) | copy-start | bytes 393220
  110.3 34.3 %copy-start.1 = (bf16[128,256]{1,0:T(8,128)(2,1)S(1)}, bf16[128,256]{1,0:T(8,128)(2,1)}, u32[]{:S(2)}) copy-start(bf16[128,256]{1,0:T(8,128)(2,1)} %cotangent_ref.1) | copy-start | bytes 196612
  110.3 34.3 %copy-start.2 = (f32[256]{0:T(256)S(1)}, f32[256]{0:T(256)}, u32[]{:S(2)}) copy-start(f32[256]{0:T(256)} %param.12) | copy-start | bytes 3076
  110.3 23.4 %all-to-all-start.3 = ((bf16[8,128,128]{2,1,0:T(8,128)(2,1)}), bf16[8,128,128]{2,1,0:T(8,128)(2,1)S(1)}, u32[]{:S(2)}, u32[]{:S(2)}) async-start(bf16[8,128,128]{2,1,0:T(8,128)(2,1)} %bitcast.38), calls=%async_computation.3 | async-start | bytes 524288 | tf_op jit(solution)/shard_map/all_to_all | solution.py:143
Sparse Core Ops, SparseCore 0:
  25.1 68.6 all-gather.1

commit v4 on v3

--- a/solution.py
+++ b/solution.py
@@ -12,7 +12,8 @@
 BLOCK = 64
 BPD = 2
 UNROLL = 12
-HALF = 128
+LEAD = 16
+ALIGN = 16
 MIB = 1024 * 1024
 REP = ("x", "core")
 SMEM = pl.BlockSpec(memory_space=pltpu.SMEM)
@@ -21,32 +22,37 @@
 
 
 def spmm_kernel(
-    rows_ref, tiles_ref, count_ref, which_ref, start_ref, table_ref, *refs
+    rows_ref, tiles_ref, count_ref, near_ref, which_ref, start_ref, table_ref, *refs
 ):
-    *sources, out_ref, picked, table, total, sems, table_sem = refs
+    near, *ring, out_ref, picked, table, total, sems, table_sem = refs
     count = count_ref[0, 0]
-
-    def fetch(s, source, start):
-        return pltpu.make_async_copy(
-            source.at[pl.ds(start, BLOCK)], picked.at[s], sems.at[s]
-        )
-
     steps = (count + UNROLL - 1) // UNROLL
     table_copy = pltpu.make_async_copy(table_ref, table, table_sem)
     table_copy.start()
 
+    def fetch(s, source, start, rows, at):
+        return pltpu.make_async_copy(
+            source.at[pl.ds(pl.multiple_of(start, ALIGN), rows)],
+            picked.at[s, pl.ds(at, rows)],
+            sems.at[s],
+        )
+
     def begin(i, carry):
         for k in range(UNROLL):
             s = i * UNROLL + k
-            start = pl.multiple_of(start_ref[s], BLOCK)
-            if len(sources) == 1:
-                fetch(s, sources[0], start).start()
-                continue
-            for n, source in enumerate(sources):
-
-                @pl.when(which_ref[s] == n)
-                def _():
-                    fetch(s, source, start).start()
+
+            @pl.when(which_ref[s] < 0)
+            def _():
+                fetch(s, near, near_ref[s], BLOCK, 0).start()
+
+            @pl.when(which_ref[s] >= 0)
+            def _():
+                fetch(s, near, near_ref[s], LEAD, 0).start()
+                for n, source in enumerate(ring):
+
+                    @pl.when(which_ref[s] == n)
+                    def _():
+                        fetch(s, source, start_ref[s], BLOCK - LEAD, LEAD).start()
 
         return carry
 
@@ -56,7 +62,7 @@
 
     def step(i, carry):
         for k in range(UNROLL):
-            fetch(i * UNROLL + k, sources[0], 0).wait()
+            fetch(i * UNROLL + k, near, 0, BLOCK, 0).wait()
         for k in range(UNROLL):
             s = i * UNROLL + k
             product = jnp.dot(
@@ -70,13 +76,13 @@
     out_ref[...] = total[...].astype(out_ref.dtype)
 
 
-def spmm(lists, which, start, sources, tile_table, out_rows):
+def spmm(lists, near_start, which, start, near, ring, tile_table, out_rows):
     slots = start.shape[0]
-    width = sources[0].shape[1]
+    width = near.shape[1]
     return pl.pallas_call(
         spmm_kernel,
         out_shape=jax.ShapeDtypeStruct((out_rows, width), jnp.bfloat16),
-        in_specs=[SMEM] * 5 + [HBM] * (1 + len(sources)),
+        in_specs=[SMEM] * 6 + [HBM] * (2 + len(ring)),
         out_specs=VMEM,
         scratch_shapes=[
             pltpu.VMEM((slots, BLOCK, width), jnp.bfloat16),
@@ -87,19 +93,16 @@
         ],
         compiler_params=pltpu.CompilerParams(vmem_limit_bytes=58 * MIB),
         name="spmm",
-    )(*lists, which, start, tile_table, *sources)
+    )(*lists, near_start, which, start, tile_table, near, *ring)
 
 
 def layer_kernel(
-    factor, left_ref, right_ref, weight_ref, bias_ref, cotangent_ref, out_ref, grads_ref
+    factor, parts_ref, weight_ref, bias_ref, cotangent_ref, out_ref, grads_ref
 ):
-    def reduced(ref):
-        summed = ref[0].astype(jnp.float32)
-        for r in range(1, ref.shape[0]):
-            summed += ref[r].astype(jnp.float32)
-        return summed.astype(jnp.bfloat16)
-
-    agg = jnp.concatenate([reduced(left_ref), reduced(right_ref)], axis=1)
+    summed = parts_ref[0].astype(jnp.float32)
+    for r in range(1, parts_ref.shape[0]):
+        summed += parts_ref[r].astype(jnp.float32)
+    agg = summed.astype(jnp.bfloat16)
     pre = jnp.dot(agg, weight_ref[...], preferred_element_type=jnp.float32) + bias_ref[...]
     sigma = 1.0 / (1.0 + jnp.exp(-pre))
     out_ref[...] = (pre * sigma).astype(out_ref.dtype)
@@ -117,7 +120,7 @@
     grads_ref[width:] = jnp.where(first, bias, 0.0).astype(grads_ref.dtype)
 
 
-def layer(left, right, weight, bias_term, cotangent, factor, grad_rows):
+def layer(parts, weight, bias_term, cotangent, factor, grad_rows):
     width = weight.shape[0]
     return pl.pallas_call(
         functools.partial(layer_kernel, factor),
@@ -125,11 +128,11 @@
             jax.ShapeDtypeStruct(cotangent.shape, jnp.bfloat16),
             jax.ShapeDtypeStruct((grad_rows, width), jnp.bfloat16),
         ),
-        in_specs=[VMEM] * 5,
+        in_specs=[VMEM] * 4,
         out_specs=(VMEM, VMEM),
         compiler_params=pltpu.CompilerParams(vmem_limit_bytes=16 * MIB),
         name="layer",
-    )(left, right, weight, bias_term.reshape(1, -1), cotangent)
+    )(parts, weight, bias_term.reshape(1, -1), cotangent)
 
 
 def spread(array, axis):
@@ -180,27 +183,30 @@
     rep_size = lax.axis_size(REP)
     lists = (adj_rows, adj_tiles, adj_count)
     ny, nz = lax.axis_size("y"), lax.axis_size("z")
-    near_y = spread(features[:, :HALF], "y").reshape(ny * own_rows, HALF)
-    near_z = spread(features[:, HALF:], "z").reshape(nz * own_rows, width - HALF)
-    left = lax.all_gather(near_y, "z", axis=0, tiled=True)
-    right = both_ways(near_z, "y")
+    kept = BLOCK + LEAD
+    near = spread(features[:kept], "y").reshape(ny * kept, width)
+    near = lax.all_gather(near, "z", axis=0, tiled=True)
+    ring = both_ways(lax.all_gather(features[kept:], "z", axis=0, tiled=True), "y")
 
     cols = adj_cols[0, 0]
     panel = cols // BPD
+    second = cols % BPD == 1
+    near_start = panel * kept + jnp.where(second, BLOCK, 0)
     behind = (lax.axis_index("y") - panel) % ny
-    start = (panel // ny * BPD + cols % BPD) * BLOCK
-    half = near_z.shape[0] // 2
+    start = panel // ny * (own_rows - kept)
+    half = ring[-1].shape[0]
     upper = start >= half
     far = behind == ny // 2
     which = jnp.where(far, ny - 1 + upper.astype(jnp.int32), behind - (behind > ny // 2))
+    which = jnp.where(second, which, -1)
     start = jnp.where(far & upper, start - half, start)
 
     rows = rep_size * own_rows
-    left = scattered(spmm(lists, which, cols * BLOCK, [left], tile_table, rows), REP)
-    right = scattered(spmm(lists, which, start, right, tile_table, rows), REP)
+    share = spmm(lists, near_start, which, start, near, ring, tile_table, rows)
+    parts = scattered(share, REP)
     factor = 1.0 / math.sqrt(nz * ny * rows)
     grad_rows = -(-(width + 8) // (8 * nz)) * 8 * nz
-    output, grads = layer(left, right, weight, bias_term, cotangent, factor, grad_rows)
+    output, grads = layer(parts, weight, bias_term, cotangent, factor, grad_rows)
     grads = total_over_all(grads)
     return (output, grads[:width], grads[width])
 

time: 204 us -> 190 us (0.931)
  starting transfers between devices: 41.1 us -> 25 us
  blocking collectives: 108 us -> 123 us
  waiting for transfers between devices: 23.7 us -> 16.2 us
  Pallas kernels: 8.98 us -> 4.81 us
    all_gather x0 -> x1, blocking collectives: none -> 30.5 us  [shards(): lax.all_gather(features[kept:], 'z', axis=0, tiled=True)]
    all_to_all x5 -> x4, blocking collectives: 84 us -> 53.5 us  [spread(): return lax.all_to_all(copies, axis, split_axis=0, concat_axis=0, tiled=True)]
    all_to_all x1 -> x0, starting transfers between devices: 16.9 us -> none  [scattered(): return lax.all_to_all(parts, axis, split_axis=0, concat_axis=0, tiled=True)]
    all_to_all x2, blocking collectives: 24.1 us -> 38.6 us  [scattered(): return lax.all_to_all(parts, axis, split_axis=0, concat_axis=0, tiled=True)]
    pallas_call x2 -> x1, Pallas kernels: 8.12 us -> 3.96 us  [spmm(): pl.pallas_call(spmm_kernel, out_shape=jax.ShapeDtypeStruct((out_rows, wid...]
    ppermute x3, waiting for transfers between devices: 13.1 us -> 9.35 us  [both_ways(): after.append(lax.ppermute(after[-1], axis, down))]
    all_to_all x1 -> x0, waiting for transfers between devices: 2.42 us -> none  [scattered(): return lax.all_to_all(parts, axis, split_axis=0, concat_axis=0, tiled=True)]
  transfers between devices with their start and end apart: 10 -> 9, of which waited for: 9 -> 7; matrix products, arithmetic and copies ran while one was open for 1% -> 1% of each run, Pallas kernels for 4% -> 0%
where the time goes in v4:
time: 190 us; the launch traced here: 189 us
  blocking collectives  123 us (65%)
  starting transfers between devices  25 us (13%)
  waiting for transfers between devices  16.2 us (9%)
  between operations  14.9 us (8%)
  Pallas kernels  4.81 us (3%)
  local copies, waits for them, and re-layouts  3.52 us (2%)
    all_to_all x4, blocking collectives, spread(): return lax.all_to_all(copies, axis, split_axis=0, concat_axis=0, tiled=True)  53.5 us
    all_to_all x2, blocking collectives, scattered(): return lax.all_to_all(parts, axis, split_axis=0, concat_axis=0, tiled=True)  38.6 us
    all_gather x1, blocking collectives, shards(): lax.all_gather(features[kept:], 'z', axis=0, tiled=True)  30.5 us
    ppermute x3, starting transfers between devices, both_ways(): after.append(lax.ppermute(after[-1], axis, down))  11.1 us
    ppermute x3, waiting for transfers between devices, both_ways(): after.append(lax.ppermute(after[-1], axis, down))  9.35 us
    ppermute x3, starting transfers between devices, both_ways(): before.append(lax.ppermute(before[-1], axis, up))  6.71 us
    ppermute x1, waiting for transfers between devices, both_ways(): lax.ppermute(before[-1][:half], axis, up)  5.84 us
    ppermute x1, starting transfers between devices, both_ways(): lax.ppermute(after[-1][half:], axis, down)  5.25 us
  transfers between devices with their start and end apart: 9, of which 7 were waited for; matrix products, arithmetic and copies ran while one was open for 1% of the time, Pallas kernels for 0%

profile of v4, /device:TPU:1, one launch (start us, length us, event | category | flops | bytes accessed | tf_op | source)
XLA Modules:
  0.0 188.8 jit_solution(5520059374240291964)
XLA Ops:
  7.2 0.0 all-gather.2.cloned.1.call-start
  7.2 0.8 slice.55
  8.0 17.6 %all_to_all.30 = bf16[8,80,256]{2,1,0:T(8,128)(2,1)} all-to-all(bf16[8,80,256]{2,1,0:T(8,128)(2,1)S(1)} %broadcast_in_dim.39), channel_id=1, replica_groups=mesh['z'=12,'y'=8,'x'=4,'core'=2] {'y'}, dimensions={0} | all-to-all | bytes 655360 | tf_op jit(solution)/shard_map/all_to_all | solution.py:140
  25.6 0.0 all-gather.2.cloned.1.call-update
  25.6 0.7 slice.56
  26.4 30.5 %all_gather.7.refs_1_ = bf16[576,256]{1,0:T(8,128)(2,1)S(1)} all-gather(bf16[48,256]{1,0:T(8,128)(2,1)S(1)} %slice.56), channel_id=1, replica_groups=mesh['z'=12,'y'=8,'x'=4,'core'=2] {'z'}, dimensions={0}, use_global_device_ids=true | all-gather | bytes 319488 | tf_op jit(solution)/shard_map/all_gather | solution.py:189
  56.9 0.0 copy-start.3
  56.9 2.4 %collective-permute-start.3 = (bf16[576,256]{1,0:T(8,128)(2,1)S(1)}, bf16[576,256]{1,0:T(8,128)(2,1)S(1)}, u32[]{:S(2)}, u32[]{:S(2)}) collective-permute-start(bf16[576,256]{1,0:T(8,128)(2,1)S(1)} %all_gather.7.refs_1_), channel_id=1, source_target_pairs={{0,56},{8,0},{16,8},{24,16},{32,24},{40,32},{48,40},{56,48},{1,57}... | collective-permute-start | bytes 884744 | tf_op jit(solution)/shard_map/ppermute | solution.py:170
  59.2 2.9 %collective-permute-start = (bf16[576,256]{1,0:T(8,128)(2,1)S(1)}, bf16[576,256]{1,0:T(8,128)(2,1)S(1)}, u32[]{:S(2)}, u32[]{:S(2)}) collective-permute-start(bf16[576,256]{1,0:T(8,128)(2,1)S(1)} %all_gather.7.refs_1_), channel_id=1, source_target_pairs={{0,8},{8,16},{16,24},{24,32},{32,40},{40,48},{48,56},{56,0},{1,9},... | collective-permute-start | bytes 884744 | tf_op jit(solution)/shard_map/ppermute | solution.py:169
  62.2 2.6 %collective-permute-done.3.refs_7_ = bf16[576,256]{1,0:T(8,128)(2,1)S(1)} collective-permute-done((bf16[576,256]{1,0:T(8,128)(2,1)S(1)}, bf16[576,256]{1,0:T(8,128)(2,1)S(1)}, u32[]{:S(2)}, u32[]{:S(2)}) %collective-permute-start.3) | collective-permute-done | bytes 294944 | tf_op jit(solution)/shard_map/ppermute | solution.py:170
  64.7 0.0 copy-start.6
  64.7 3.6 %collective-permute-start.4 = (bf16[576,256]{1,0:T(8,128)(2,1)S(1)}, bf16[576,256]{1,0:T(8,128)(2,1)S(1)}, u32[]{:S(2)}, u32[]{:S(2)}) collective-permute-start(bf16[576,256]{1,0:T(8,128)(2,1)S(1)} %collective-permute-done.3.refs_7_), channel_id=1, source_target_pairs={{0,56},{8,0},{16,8},{24,16},{32,24},{40,32},{48,40},{56,48},{1,57}... | collective-permute-start | bytes 884744 | tf_op jit(solution)/shard_map/ppermute | solution.py:170
  68.3 0.3 collective-permute-done.refs_2_
  68.6 0.0 copy-start.7
  68.7 1.9 %collective-permute-start.1 = (bf16[576,256]{1,0:T(8,128)(2,1)S(1)}, bf16[576,256]{1,0:T(8,128)(2,1)S(1)}, u32[]{:S(2)}, u32[]{:S(2)}) collective-permute-start(bf16[576,256]{1,0:T(8,128)(2,1)S(1)} %collective-permute-done.refs_2_), channel_id=1, source_target_pairs={{0,8},{8,16},{16,24},{24,32},{32,40},{40,48},{48,56},{56,0},{1,9},... | collective-permute-start | bytes 884744 | tf_op jit(solution)/shard_map/ppermute | solution.py:169
  70.6 4.0 %collective-permute-done.4.refs_6_ = bf16[576,256]{1,0:T(8,128)(2,1)S(1)} collective-permute-done((bf16[576,256]{1,0:T(8,128)(2,1)S(1)}, bf16[576,256]{1,0:T(8,128)(2,1)S(1)}, u32[]{:S(2)}, u32[]{:S(2)}) %collective-permute-start.4) | collective-permute-done | bytes 294944 | tf_op jit(solution)/shard_map/ppermute | solution.py:170
  74.6 5.1 %collective-permute-start.5 = (bf16[576,256]{1,0:T(8,128)(2,1)S(1)}, bf16[576,256]{1,0:T(8,128)(2,1)S(1)}, u32[]{:S(2)}, u32[]{:S(2)}) collective-permute-start(bf16[576,256]{1,0:T(8,128)(2,1)S(1)} %collective-permute-done.4.refs_6_), channel_id=1, source_target_pairs={{0,56},{8,0},{16,8},{24,16},{32,24},{40,32},{48,40},{56,48},{1,57}... | collective-permute-start | bytes 884744 | tf_op jit(solution)/shard_map/ppermute | solution.py:170
  79.7 0.3 collective-permute-done.1.refs_3_
  80.0 1.9 %collective-permute-start.2 = (bf16[576,256]{1,0:T(8,128)(2,1)S(1)}, bf16[576,256]{1,0:T(8,128)(2,1)S(1)}, u32[]{:S(2)}, u32[]{:S(2)}) collective-permute-start(bf16[576,256]{1,0:T(8,128)(2,1)S(1)} %collective-permute-done.1.refs_3_), channel_id=1, source_target_pairs={{0,8},{8,16},{16,24},{24,32},{32,40},{40,48},{48,56},{56,0},{1,9},... | collective-permute-start | bytes 884744 | tf_op jit(solution)/shard_map/ppermute | solution.py:169
  82.6 1.2 and_select_fusion
  83.8 2.8 %collective-permute-done.5.refs_5_ = bf16[576,256]{1,0:T(8,128)(2,1)S(1)} collective-permute-done((bf16[576,256]{1,0:T(8,128)(2,1)S(1)}, bf16[576,256]{1,0:T(8,128)(2,1)S(1)}, u32[]{:S(2)}, u32[]{:S(2)}) %collective-permute-start.5) | collective-permute-done | bytes 294944 | tf_op jit(solution)/shard_map/ppermute | solution.py:170
  86.5 5.3 %collective-permute-start.7 = (bf16[288,256]{1,0:T(8,128)(2,1)S(1)}, bf16[288,256]{1,0:T(8,128)(2,1)S(1)}, u32[]{:S(2)}, u32[]{:S(2)}) collective-permute-start(bf16[288,256]{1,0:T(8,128)(2,1)S(1)} %slice.65), channel_id=1, source_target_pairs={{0,56},{8,0},{16,8},{24,16},{32,24},{40,32},{48,40},{56,48},{1,57}... | collective-permute-start | bytes 442376 | tf_op jit(solution)/shard_map/ppermute | solution.py:174
  91.8 0.4 collective-permute-done.2.refs_4_
  92.2 1.9 %collective-permute-start.6 = (bf16[288,256]{1,0:T(8,128)(2,1)S(1)}, bf16[288,256]{1,0:T(8,128)(2,1)S(1)}, u32[]{:S(2)}, u32[]{:S(2)}) collective-permute-start(bf16[288,256]{1,0:T(8,128)(2,1)S(1)} %slice.64), channel_id=1, source_target_pairs={{0,8},{8,16},{16,24},{24,32},{32,40},{40,48},{48,56},{56,0},{1,9},... | collective-permute-start | bytes 442376 | tf_op jit(solution)/shard_map/ppermute | solution.py:173
  94.1 0.6 compare_select_fusion.9
  94.7 0.0 collective-permute-done.7.refs_9_
  94.7 5.8 %collective-permute-done.6.refs_8_ = bf16[288,256]{1,0:T(8,128)(2,1)S(1)} collective-permute-done((bf16[288,256]{1,0:T(8,128)(2,1)S(1)}, bf16[288,256]{1,0:T(8,128)(2,1)S(1)}, u32[]{:S(2)}, u32[]{:S(2)}) %collective-permute-start.6) | collective-permute-done | bytes 147488 | tf_op jit(solution)/shard_map/ppermute | solution.py:173
  100.5 0.0 copy-done.3
  100.6 0.0 copy-done.6
  100.6 0.0 copy-done.7
  100.6 0.0 copy-done.8
  100.6 0.0 copy-done.9
  100.6 0.0 copy-done.4
  100.6 0.0 copy-done.5
  100.6 0.0 copy-done.10
  100.6 0.6 copy-done.11
  101.2 4.0 %spmm.1 = bf16[1024,256]{1,0:T(8,128)(2,1)} custom-call(s32[1,1,48]{2,1,0:T(1,128)} %rows_ref.1, s32[1,1,48]{2,1,0:T(1,128)} %tiles_ref.1, s32[1,1]{1,0:T(1,128)S(6)} %copy.12.count_ref, s32[48]{0:T(128)} %get-tuple-element.13.near_ref, s32[48]{0:T(128)} %get-tuple-element.12.which_ref, s32[48]{0:T(128)} %get-tuple-element.7.start_ref, ...), custom_call_target="tpu_custom_call" | custom-call | tf_op jit(solution)/shard_map/spmm/pallas_call | solution.py:82
  105.2 25.3 %all_to_all.31.parts_ref = bf16[8,128,256]{2,1,0:T(8,128)(2,1)S(1)} all-to-all(bf16[8,128,256]{2,1,0:T(8,128)(2,1)} %bitcast.29), channel_id=1, replica_groups=mesh['z'=12,'y'=8,'x'=4,'core'=2] {'x','core'}, dimensions={0} | all-to-all | bytes 1048576 | tf_op jit(solution)/shard_map/all_to_all | solution.py:146
  130.5 0.0 copy-done
  130.5 0.0 copy-done.1
  130.5 0.0 copy-done.2
  130.5 0.9 layer.1
  131.3 13.3 %all_to_all.32 = bf16[12,24,256]{2,1,0:T(8,128)(2,1)S(1)} all-to-all(bf16[12,24,256]{2,1,0:T(8,128)(2,1)S(1)} %bitcast.27), channel_id=1, replica_groups=mesh['z'=12,'y'=8,'x'=4,'core'=2] {'z'}, dimensions={0} | all-to-all | bytes 294912 | tf_op jit(solution)/shard_map/all_to_all | solution.py:146
  144.7 10.9 %all_to_all.33 = bf16[8,24,256]{2,1,0:T(8,128)(2,1)S(1)} all-to-all(bf16[8,24,256]{2,1,0:T(8,128)(2,1)S(1)} %broadcast_in_dim.41), channel_id=1, replica_groups=mesh['z'=12,'y'=8,'x'=4,'core'=2] {'y'}, dimensions={0} | all-to-all | bytes 196608 | tf_op jit(solution)/shard_map/all_to_all | solution.py:140
  155.7 11.3 %all_to_all.34 = bf16[8,24,256]{2,1,0:T(8,128)(2,1)S(1)} all-to-all(bf16[8,24,256]{2,1,0:T(8,128)(2,1)S(1)} %broadcast_in_dim.43), channel_id=1, replica_groups=mesh['z'=12,'y'=8,'x'=4,'core'=2] {'x','core'}, dimensions={0} | all-to-all | bytes 196608 | tf_op jit(solution)/shard_map/all_to_all | solution.py:140
  167.0 13.7 %all_to_all.35 = bf16[12,24,256]{2,1,0:T(8,128)(2,1)S(1)} all-to-all(bf16[12,24,256]{2,1,0:T(8,128)(2,1)S(1)} %broadcast_in_dim.45), channel_id=1, replica_groups=mesh['z'=12,'y'=8,'x'=4,'core'=2] {'z'}, dimensions={0} | all-to-all | bytes 294912 | tf_op jit(solution)/shard_map/all_to_all | solution.py:140
  180.7 0.6 slice.70
  181.2 0.7 slice.69
  (20 shorter events, 0.2 us)
Async XLA Ops:
  7.2 93.4 %all-gather.2.cloned.1.call-start = ((), (), s32[]{:S(2)}) async-start(), calls=%async_computation.6 | async-start | bytes 4259840 | tf_op jit(solution)/shard_map/all_gather | solution.py:188
  56.9 43.7 %copy-start.3 = (bf16[576,256]{1,0:T(8,128)(2,1)}, bf16[576,256]{1,0:T(8,128)(2,1)S(1)}, u32[]{:S(2)}) copy-start(bf16[576,256]{1,0:T(8,128)(2,1)S(1)} %all_gather.7.refs_1_) | copy-start | bytes 884740
  56.9 7.9 %collective-permute-start.3 = (bf16[576,256]{1,0:T(8,128)(2,1)S(1)}, bf16[576,256]{1,0:T(8,128)(2,1)S(1)}, u32[]{:S(2)}, u32[]{:S(2)}) collective-permute-start(bf16[576,256]{1,0:T(8,128)(2,1)S(1)} %all_gather.7.refs_1_), channel_id=1, source_target_pairs={{0,56},{8,0},{16,8},{24,16},{32,24},{40,32},{48,40},{56,48},{1,57}... | collective-permute-start | bytes 884744 | tf_op jit(solution)/shard_map/ppermute | solution.py:170
  59.2 9.4 %collective-permute-start = (bf16[576,256]{1,0:T(8,128)(2,1)S(1)}, bf16[576,256]{1,0:T(8,128)(2,1)S(1)}, u32[]{:S(2)}, u32[]{:S(2)}) collective-permute-start(bf16[576,256]{1,0:T(8,128)(2,1)S(1)} %all_gather.7.refs_1_), channel_id=1, source_target_pairs={{0,8},{8,16},{16,24},{24,32},{32,40},{40,48},{48,56},{56,0},{1,9},... | collective-permute-start | bytes 884744 | tf_op jit(solution)/shard_map/ppermute | solution.py:169
  64.7 35.8 %copy-start.6 = (bf16[576,256]{1,0:T(8,128)(2,1)}, bf16[576,256]{1,0:T(8,128)(2,1)S(1)}, u32[]{:S(2)}) copy-start(bf16[576,256]{1,0:T(8,128)(2,1)S(1)} %collective-permute-done.3.refs_7_) | copy-start | bytes 884740
  64.7 9.9 %collective-permute-start.4 = (bf16[576,256]{1,0:T(8,128)(2,1)S(1)}, bf16[576,256]{1,0:T(8,128)(2,1)S(1)}, u32[]{:S(2)}, u32[]{:S(2)}) collective-permute-start(bf16[576,256]{1,0:T(8,128)(2,1)S(1)} %collective-permute-done.3.refs_7_), channel_id=1, source_target_pairs={{0,56},{8,0},{16,8},{24,16},{32,24},{40,32},{48,40},{56,48},{1,57}... | collective-permute-start | bytes 884744 | tf_op jit(solution)/shard_map/ppermute | solution.py:170
  68.6 31.9 %copy-start.7 = (bf16[576,256]{1,0:T(8,128)(2,1)}, bf16[576,256]{1,0:T(8,128)(2,1)S(1)}, u32[]{:S(2)}) copy-start(bf16[576,256]{1,0:T(8,128)(2,1)S(1)} %collective-permute-done.refs_2_) | copy-start | bytes 884740
  68.7 11.4 %collective-permute-start.1 = (bf16[576,256]{1,0:T(8,128)(2,1)S(1)}, bf16[576,256]{1,0:T(8,128)(2,1)S(1)}, u32[]{:S(2)}, u32[]{:S(2)}) collective-permute-start(bf16[576,256]{1,0:T(8,128)(2,1)S(1)} %collective-permute-done.refs_2_), channel_id=1, source_target_pairs={{0,8},{8,16},{16,24},{24,32},{32,40},{40,48},{48,56},{56,0},{1,9},... | collective-permute-start | bytes 884744 | tf_op jit(solution)/shard_map/ppermute | solution.py:169
  74.6 26.0 %copy-start.8 = (bf16[576,256]{1,0:T(8,128)(2,1)}, bf16[576,256]{1,0:T(8,128)(2,1)S(1)}, u32[]{:S(2)}) copy-start(bf16[576,256]{1,0:T(8,128)(2,1)S(1)} %collective-permute-done.4.refs_6_) | copy-start | bytes 884740
  74.6 11.9 %collective-permute-start.5 = (bf16[576,256]{1,0:T(8,128)(2,1)S(1)}, bf16[576,256]{1,0:T(8,128)(2,1)S(1)}, u32[]{:S(2)}, u32[]{:S(2)}) collective-permute-start(bf16[576,256]{1,0:T(8,128)(2,1)S(1)} %collective-permute-done.4.refs_6_), channel_id=1, source_target_pairs={{0,56},{8,0},{16,8},{24,16},{32,24},{40,32},{48,40},{56,48},{1,57}... | collective-permute-start | bytes 884744 | tf_op jit(solution)/shard_map/ppermute | solution.py:170
  80.0 20.6 %copy-start.9 = (bf16[576,256]{1,0:T(8,128)(2,1)}, bf16[576,256]{1,0:T(8,128)(2,1)S(1)}, u32[]{:S(2)}) copy-start(bf16[576,256]{1,0:T(8,128)(2,1)S(1)} %collective-permute-done.1.refs_3_) | copy-start | bytes 884740
  80.0 12.2 %collective-permute-start.2 = (bf16[576,256]{1,0:T(8,128)(2,1)S(1)}, bf16[576,256]{1,0:T(8,128)(2,1)S(1)}, u32[]{:S(2)}, u32[]{:S(2)}) collective-permute-start(bf16[576,256]{1,0:T(8,128)(2,1)S(1)} %collective-permute-done.1.refs_3_), channel_id=1, source_target_pairs={{0,8},{8,16},{16,24},{24,32},{32,40},{40,48},{48,56},{56,0},{1,9},... | collective-permute-start | bytes 884744 | tf_op jit(solution)/shard_map/ppermute | solution.py:169
  86.5 14.1 %copy-start.4 = (bf16[576,256]{1,0:T(8,128)(2,1)}, bf16[576,256]{1,0:T(8,128)(2,1)S(1)}, u32[]{:S(2)}) copy-start(bf16[576,256]{1,0:T(8,128)(2,1)S(1)} %collective-permute-done.5.refs_5_) | copy-start | bytes 884740
  86.5 8.2 %collective-permute-start.7 = (bf16[288,256]{1,0:T(8,128)(2,1)S(1)}, bf16[288,256]{1,0:T(8,128)(2,1)S(1)}, u32[]{:S(2)}, u32[]{:S(2)}) collective-permute-start(bf16[288,256]{1,0:T(8,128)(2,1)S(1)} %slice.65), channel_id=1, source_target_pairs={{0,56},{8,0},{16,8},{24,16},{32,24},{40,32},{48,40},{56,48},{1,57}... | collective-permute-start | bytes 442376 | tf_op jit(solution)/shard_map/ppermute | solution.py:174
  92.2 8.4 %copy-start.5 = (bf16[576,256]{1,0:T(8,128)(2,1)}, bf16[576,256]{1,0:T(8,128)(2,1)S(1)}, u32[]{:S(2)}) copy-start(bf16[576,256]{1,0:T(8,128)(2,1)S(1)} %collective-permute-done.2.refs_4_) | copy-start | bytes 884740
  92.2 8.3 %collective-permute-start.6 = (bf16[288,256]{1,0:T(8,128)(2,1)S(1)}, bf16[288,256]{1,0:T(8,128)(2,1)S(1)}, u32[]{:S(2)}, u32[]{:S(2)}) collective-permute-start(bf16[288,256]{1,0:T(8,128)(2,1)S(1)} %slice.64), channel_id=1, source_target_pairs={{0,8},{8,16},{16,24},{24,32},{32,40},{40,48},{48,56},{56,0},{1,9},... | collective-permute-start | bytes 442376 | tf_op jit(solution)/shard_map/ppermute | solution.py:173
  94.7 5.9 %copy-start.10 = (bf16[288,256]{1,0:T(8,128)(2,1)}, bf16[288,256]{1,0:T(8,128)(2,1)S(1)}, u32[]{:S(2)}) copy-start(bf16[288,256]{1,0:T(8,128)(2,1)S(1)} %collective-permute-done.7.refs_9_) | copy-start | bytes 442372
  100.5 0.7 copy-start.11
  101.2 29.3 %copy-start = (bf16[256,256]{1,0:T(8,128)(2,1)S(1)}, bf16[256,256]{1,0:T(8,128)(2,1)}, u32[]{:S(2)}) copy-start(bf16[256,256]{1,0:T(8,128)(2,1)} %weight_ref.1) | copy-start | bytes 393220
  101.2 29.3 %copy-start.1 = (bf16[128,256]{1,0:T(8,128)(2,1)S(1)}, bf16[128,256]{1,0:T(8,128)(2,1)}, u32[]{:S(2)}) copy-start(bf16[128,256]{1,0:T(8,128)(2,1)} %cotangent_ref.1) | copy-start | bytes 196612
  101.2 29.3 %copy-start.2 = (f32[256]{0:T(256)S(1)}, f32[256]{0:T(256)}, u32[]{:S(2)}) copy-start(f32[256]{0:T(256)} %param.12) | copy-start | bytes 3076
Sparse Core Ops, SparseCore 0:
  25.8 67.6 all-gather.1

commit v5 on v4

--- a/solution.py
+++ b/solution.py
@@ -140,6 +140,24 @@
     return lax.all_to_all(copies, axis, split_axis=0, concat_axis=0, tiled=True)
 
 
+def copies_kernel(features_ref, after_ref, out_ref):
+    for n in range(out_ref.shape[0]):
+        out_ref[n] = features_ref[: out_ref.shape[1]]
+
+
+def spread_later(features, rows, axis, after):
+    size, width = lax.axis_size(axis), features.shape[1]
+    copies = pl.pallas_call(
+        copies_kernel,
+        out_shape=jax.ShapeDtypeStruct((size, rows, width), features.dtype),
+        in_specs=[VMEM, pl.BlockSpec(memory_space=pl.ANY)],
+        out_specs=VMEM,
+        compiler_params=pltpu.CompilerParams(vmem_limit_bytes=8 * MIB),
+        name="copies",
+    )(features, after)
+    return lax.all_to_all(copies, axis, split_axis=0, concat_axis=0, tiled=True)
+
+
 def scattered(array, axis):
     size = lax.axis_size(axis)
     parts = array.reshape(size, array.shape[0] // size, array.shape[1])
@@ -184,9 +202,10 @@
     lists = (adj_rows, adj_tiles, adj_count)
     ny, nz = lax.axis_size("y"), lax.axis_size("z")
     kept = BLOCK + LEAD
-    near = spread(features[:kept], "y").reshape(ny * kept, width)
+    along_z = lax.all_gather(features[kept:], "z", axis=0, tiled=True)
+    near = spread_later(features, kept, "y", along_z).reshape(ny * kept, width)
     near = lax.all_gather(near, "z", axis=0, tiled=True)
-    ring = both_ways(lax.all_gather(features[kept:], "z", axis=0, tiled=True), "y")
+    ring = both_ways(along_z, "y")
 
     cols = adj_cols[0, 0]
     panel = cols // BPD

time: 190 us -> 203 us (1.068)
  waiting for transfers between devices: 16.2 us -> 33.8 us
  starting transfers between devices: 25 us -> 21.9 us
    all_to_all x0 -> x1, blocking collectives: none -> 16.8 us  [spread_later(): return lax.all_to_all(copies, axis, split_axis=0, concat_axis=0, tiled=True)]
    all_gather x1, waiting for transfers between devices: 0.01 us -> 15.7 us  [shards(): near = lax.all_gather(near, 'z', axis=0, tiled=True)]
    all_to_all x4 -> x3, blocking collectives: 53.5 us -> 39.8 us  [spread(): return lax.all_to_all(copies, axis, split_axis=0, concat_axis=0, tiled=True)]
    all_to_all x2, blocking collectives: 38.6 us -> 34.9 us  [scattered(): return lax.all_to_all(parts, axis, split_axis=0, concat_axis=0, tiled=True)]
    ppermute x3, starting transfers between devices: 11.1 us -> 7.86 us  [both_ways(): after.append(lax.ppermute(after[-1], axis, down))]
where the time goes in v5:
time: 203 us; the launch traced here: 201 us
  blocking collectives  121 us (60%)
  waiting for transfers between devices  33.8 us (17%)
  starting transfers between devices  21.9 us (11%)
  between operations  14.9 us (7%)
  Pallas kernels  4.86 us (2%)
  local copies, waits for them, and re-layouts  2.97 us (1%)
    all_to_all x3, blocking collectives, spread(): return lax.all_to_all(copies, axis, split_axis=0, concat_axis=0, tiled=True)  39.8 us
    all_to_all x2, blocking collectives, scattered(): return lax.all_to_all(parts, axis, split_axis=0, concat_axis=0, tiled=True)  34.9 us
    all_gather x1, blocking collectives, shards(): along_z = lax.all_gather(features[kept:], 'z', axis=0, tiled=True)  29.6 us
    all_to_all x1, blocking collectives, spread_later(): return lax.all_to_all(copies, axis, split_axis=0, concat_axis=0, tiled=True)  16.8 us
    all_gather x1, waiting for transfers between devices, shards(): near = lax.all_gather(near, 'z', axis=0, tiled=True)  15.7 us
    ppermute x3, waiting for transfers between devices, both_ways(): after.append(lax.ppermute(after[-1], axis, down))  10.5 us
    ppermute x3, starting transfers between devices, both_ways(): after.append(lax.ppermute(after[-1], axis, down))  7.86 us
    ppermute x3, starting transfers between devices, both_ways(): before.append(lax.ppermute(before[-1], axis, up))  7.42 us
  transfers between devices with their start and end apart: 9, of which 7 were waited for; matrix products, arithmetic and copies ran while one was open for 1% of the time, Pallas kernels for 0%

profile of v5, /device:TPU:1, one launch (start us, length us, event | category | flops | bytes accessed | tf_op | source)
XLA Modules:
  0.0 201.3 jit_solution(2104869104373403974)
XLA Ops:
  7.2 0.0 all-gather.2.cloned.1.call-start
  7.2 0.7 slice.52
  8.0 29.6 %all_gather.6.after_ref.refs_1_ = bf16[576,256]{1,0:T(8,128)(2,1)S(1)} all-gather(bf16[48,256]{1,0:T(8,128)(2,1)S(1)} %slice.52), channel_id=1, replica_groups=mesh['z'=12,'y'=8,'x'=4,'core'=2] {'z'}, dimensions={0}, use_global_device_ids=true | all-gather | bytes 319488 | tf_op jit(solution)/shard_map/all_gather | solution.py:205
  37.5 0.8 copy-done.2
  38.4 16.8 %all_to_all.30 = bf16[8,80,256]{2,1,0:T(8,128)(2,1)} all-to-all(bf16[8,80,256]{2,1,0:T(8,128)(2,1)S(1)} %copies.1), channel_id=1, replica_groups=mesh['z'=12,'y'=8,'x'=4,'core'=2] {'y'}, dimensions={0} | all-to-all | bytes 655360 | tf_op jit(solution)/shard_map/all_to_all | solution.py:158
  55.2 0.0 all-gather.2.cloned.1.call-update
  55.2 1.9 collective-permute-start.3
  57.1 3.4 %collective-permute-start = (bf16[576,256]{1,0:T(8,128)(2,1)S(1)}, bf16[576,256]{1,0:T(8,128)(2,1)S(1)}, u32[]{:S(2)}, u32[]{:S(2)}) collective-permute-start(bf16[576,256]{1,0:T(8,128)(2,1)S(1)} %all_gather.6.after_ref.refs_1_), channel_id=1, source_target_pairs={{0,8},{8,16},{16,24},{24,32},{32,40},{40,48},{48,56},{56,0},{1,9},... | collective-permute-start | bytes 884744 | tf_op jit(solution)/shard_map/ppermute | solution.py:187
  60.5 2.2 %collective-permute-done.3.refs_7_ = bf16[576,256]{1,0:T(8,128)(2,1)S(1)} collective-permute-done((bf16[576,256]{1,0:T(8,128)(2,1)S(1)}, bf16[576,256]{1,0:T(8,128)(2,1)S(1)}, u32[]{:S(2)}, u32[]{:S(2)}) %collective-permute-start.3) | collective-permute-done | bytes 294944 | tf_op jit(solution)/shard_map/ppermute | solution.py:188
  62.7 3.1 %collective-permute-start.4 = (bf16[576,256]{1,0:T(8,128)(2,1)S(1)}, bf16[576,256]{1,0:T(8,128)(2,1)S(1)}, u32[]{:S(2)}, u32[]{:S(2)}) collective-permute-start(bf16[576,256]{1,0:T(8,128)(2,1)S(1)} %collective-permute-done.3.refs_7_), channel_id=1, source_target_pairs={{0,56},{8,0},{16,8},{24,16},{32,24},{40,32},{48,40},{56,48},{1,57}... | collective-permute-start | bytes 884744 | tf_op jit(solution)/shard_map/ppermute | solution.py:188
  65.8 0.0 collective-permute-done.refs_2_
  65.8 0.0 copy-start.8
  65.8 2.2 %collective-permute-start.1 = (bf16[576,256]{1,0:T(8,128)(2,1)S(1)}, bf16[576,256]{1,0:T(8,128)(2,1)S(1)}, u32[]{:S(2)}, u32[]{:S(2)}) collective-permute-start(bf16[576,256]{1,0:T(8,128)(2,1)S(1)} %collective-permute-done.refs_2_), channel_id=1, source_target_pairs={{0,8},{8,16},{16,24},{24,32},{32,40},{40,48},{48,56},{56,0},{1,9},... | collective-permute-start | bytes 884744 | tf_op jit(solution)/shard_map/ppermute | solution.py:187
  68.0 5.5 %collective-permute-done.4.refs_6_ = bf16[576,256]{1,0:T(8,128)(2,1)S(1)} collective-permute-done((bf16[576,256]{1,0:T(8,128)(2,1)S(1)}, bf16[576,256]{1,0:T(8,128)(2,1)S(1)}, u32[]{:S(2)}, u32[]{:S(2)}) %collective-permute-start.4) | collective-permute-done | bytes 294944 | tf_op jit(solution)/shard_map/ppermute | solution.py:188
  73.5 2.8 %collective-permute-start.5 = (bf16[576,256]{1,0:T(8,128)(2,1)S(1)}, bf16[576,256]{1,0:T(8,128)(2,1)S(1)}, u32[]{:S(2)}, u32[]{:S(2)}) collective-permute-start(bf16[576,256]{1,0:T(8,128)(2,1)S(1)} %collective-permute-done.4.refs_6_), channel_id=1, source_target_pairs={{0,56},{8,0},{16,8},{24,16},{32,24},{40,32},{48,40},{56,48},{1,57}... | collective-permute-start | bytes 884744 | tf_op jit(solution)/shard_map/ppermute | solution.py:188
  76.3 0.7 collective-permute-done.1.refs_3_
  77.0 1.9 collective-permute-start.2
  79.6 1.2 and_select_fusion
  80.8 2.8 %collective-permute-done.5.refs_5_ = bf16[576,256]{1,0:T(8,128)(2,1)S(1)} collective-permute-done((bf16[576,256]{1,0:T(8,128)(2,1)S(1)}, bf16[576,256]{1,0:T(8,128)(2,1)S(1)}, u32[]{:S(2)}, u32[]{:S(2)}) %collective-permute-start.5) | collective-permute-done | bytes 294944 | tf_op jit(solution)/shard_map/ppermute | solution.py:188
  83.6 4.7 %collective-permute-start.7 = (bf16[288,256]{1,0:T(8,128)(2,1)S(1)}, bf16[288,256]{1,0:T(8,128)(2,1)S(1)}, u32[]{:S(2)}, u32[]{:S(2)}) collective-permute-start(bf16[288,256]{1,0:T(8,128)(2,1)S(1)} %slice.61), channel_id=1, source_target_pairs={{0,56},{8,0},{16,8},{24,16},{32,24},{40,32},{48,40},{56,48},{1,57}... | collective-permute-start | bytes 442376 | tf_op jit(solution)/shard_map/ppermute | solution.py:192
  88.3 0.7 collective-permute-done.2.refs_4_
  89.0 1.9 collective-permute-start.6
  90.9 0.5 compare_select_fusion.9
  91.4 0.0 collective-permute-done.7.refs_9_
  91.4 6.2 %collective-permute-done.6.refs_8_ = bf16[288,256]{1,0:T(8,128)(2,1)S(1)} collective-permute-done((bf16[288,256]{1,0:T(8,128)(2,1)S(1)}, bf16[288,256]{1,0:T(8,128)(2,1)S(1)}, u32[]{:S(2)}, u32[]{:S(2)}) %collective-permute-start.6) | collective-permute-done | bytes 147488 | tf_op jit(solution)/shard_map/ppermute | solution.py:191
  97.6 15.7 %all-gather.2.cloned.1.call-done.refs_0_ = bf16[7680,256]{1,0:T(8,128)(2,1)} async-done(((bf16[640,256]{1,0:T(8,128)(2,1)}), bf16[7680,256]{1,0:T(8,128)(2,1)}) %all-gather.2.cloned.1.call-update) | async-done | bytes 3932176 | tf_op jit(solution)/shard_map/all_gather | solution.py:207
  113.3 0.0 copy-done
  113.3 0.0 copy-done.7
  113.4 0.0 copy-done.8
  113.4 0.0 copy-done.9
  113.4 0.0 copy-done.10
  113.4 0.0 copy-done.5
  113.4 0.0 copy-done.6
  113.4 0.0 copy-done.11
  113.4 0.0 copy-done.12
  113.4 0.0 copy-start.1
  113.4 0.0 copy-start.3
  113.4 0.0 copy-start.4
  113.4 4.0 %spmm.1 = bf16[1024,256]{1,0:T(8,128)(2,1)} custom-call(s32[1,1,48]{2,1,0:T(1,128)} %rows_ref.1, s32[1,1,48]{2,1,0:T(1,128)} %tiles_ref.1, s32[1,1]{1,0:T(1,128)S(6)} %copy.12.count_ref, s32[48]{0:T(128)} %get-tuple-element.13.near_ref, s32[48]{0:T(128)} %get-tuple-element.12.which_ref, s32[48]{0:T(128)} %get-tuple-element.7.start_ref, ...), custom_call_target="tpu_custom_call" | custom-call | tf_op jit(solution)/shard_map/spmm/pallas_call | solution.py:82
  117.4 19.0 %all_to_all.31.parts_ref = bf16[8,128,256]{2,1,0:T(8,128)(2,1)S(1)} all-to-all(bf16[8,128,256]{2,1,0:T(8,128)(2,1)} %bitcast.29), channel_id=1, replica_groups=mesh['z'=12,'y'=8,'x'=4,'core'=2] {'x','core'}, dimensions={0} | all-to-all | bytes 1048576 | tf_op jit(solution)/shard_map/all_to_all | solution.py:164
  136.4 0.0 copy-done.1
  136.4 0.9 layer.1
  137.3 15.9 %all_to_all.32 = bf16[12,24,256]{2,1,0:T(8,128)(2,1)S(1)} all-to-all(bf16[12,24,256]{2,1,0:T(8,128)(2,1)S(1)} %bitcast.27), channel_id=1, replica_groups=mesh['z'=12,'y'=8,'x'=4,'core'=2] {'z'}, dimensions={0} | all-to-all | bytes 294912 | tf_op jit(solution)/shard_map/all_to_all | solution.py:164
  153.2 14.8 %all_to_all.33 = bf16[8,24,256]{2,1,0:T(8,128)(2,1)S(1)} all-to-all(bf16[8,24,256]{2,1,0:T(8,128)(2,1)S(1)} %broadcast_in_dim.34), channel_id=1, replica_groups=mesh['z'=12,'y'=8,'x'=4,'core'=2] {'y'}, dimensions={0} | all-to-all | bytes 196608 | tf_op jit(solution)/shard_map/all_to_all | solution.py:140
  168.1 11.5 %all_to_all.34 = bf16[8,24,256]{2,1,0:T(8,128)(2,1)S(1)} all-to-all(bf16[8,24,256]{2,1,0:T(8,128)(2,1)S(1)} %broadcast_in_dim.36), channel_id=1, replica_groups=mesh['z'=12,'y'=8,'x'=4,'core'=2] {'x','core'}, dimensions={0} | all-to-all | bytes 196608 | tf_op jit(solution)/shard_map/all_to_all | solution.py:140
  179.6 13.5 %all_to_all.35 = bf16[12,24,256]{2,1,0:T(8,128)(2,1)S(1)} all-to-all(bf16[12,24,256]{2,1,0:T(8,128)(2,1)S(1)} %broadcast_in_dim.38), channel_id=1, replica_groups=mesh['z'=12,'y'=8,'x'=4,'core'=2] {'z'}, dimensions={0} | all-to-all | bytes 294912 | tf_op jit(solution)/shard_map/all_to_all | solution.py:140
  193.1 0.6 slice.66
  193.7 0.7 slice.65
  (21 shorter events, 0.2 us)
Async XLA Ops:
  7.2 106.2 %all-gather.2.cloned.1.call-start = ((), (), s32[]{:S(2)}) async-start(), calls=%async_computation.6 | async-start | bytes 4259840 | tf_op jit(solution)/shard_map/all_gather | solution.py:207
  37.5 0.8 copy-start.2
  38.4 75.0 %copy-start = (bf16[576,256]{1,0:T(8,128)(2,1)}, bf16[576,256]{1,0:T(8,128)(2,1)S(1)}, u32[]{:S(2)}) copy-start(bf16[576,256]{1,0:T(8,128)(2,1)S(1)} %all_gather.6.after_ref.refs_1_) | copy-start | bytes 884740
  55.2 7.5 %collective-permute-start.3 = (bf16[576,256]{1,0:T(8,128)(2,1)S(1)}, bf16[576,256]{1,0:T(8,128)(2,1)S(1)}, u32[]{:S(2)}, u32[]{:S(2)}) collective-permute-start(bf16[576,256]{1,0:T(8,128)(2,1)S(1)} %all_gather.6.after_ref.refs_1_), channel_id=1, source_target_pairs={{0,56},{8,0},{16,8},{24,16},{32,24},{40,32},{48,40},{56,48},{1,57}... | collective-permute-start | bytes 884744 | tf_op jit(solution)/shard_map/ppermute | solution.py:188
  57.1 8.7 %collective-permute-start = (bf16[576,256]{1,0:T(8,128)(2,1)S(1)}, bf16[576,256]{1,0:T(8,128)(2,1)S(1)}, u32[]{:S(2)}, u32[]{:S(2)}) collective-permute-start(bf16[576,256]{1,0:T(8,128)(2,1)S(1)} %all_gather.6.after_ref.refs_1_), channel_id=1, source_target_pairs={{0,8},{8,16},{16,24},{24,32},{32,40},{40,48},{48,56},{56,0},{1,9},... | collective-permute-start | bytes 884744 | tf_op jit(solution)/shard_map/ppermute | solution.py:187
  62.7 50.7 %copy-start.7 = (bf16[576,256]{1,0:T(8,128)(2,1)}, bf16[576,256]{1,0:T(8,128)(2,1)S(1)}, u32[]{:S(2)}) copy-start(bf16[576,256]{1,0:T(8,128)(2,1)S(1)} %collective-permute-done.3.refs_7_) | copy-start | bytes 884740
  62.7 10.8 %collective-permute-start.4 = (bf16[576,256]{1,0:T(8,128)(2,1)S(1)}, bf16[576,256]{1,0:T(8,128)(2,1)S(1)}, u32[]{:S(2)}, u32[]{:S(2)}) collective-permute-start(bf16[576,256]{1,0:T(8,128)(2,1)S(1)} %collective-permute-done.3.refs_7_), channel_id=1, source_target_pairs={{0,56},{8,0},{16,8},{24,16},{32,24},{40,32},{48,40},{56,48},{1,57}... | collective-permute-start | bytes 884744 | tf_op jit(solution)/shard_map/ppermute | solution.py:188
  65.8 47.6 %copy-start.8 = (bf16[576,256]{1,0:T(8,128)(2,1)}, bf16[576,256]{1,0:T(8,128)(2,1)S(1)}, u32[]{:S(2)}) copy-start(bf16[576,256]{1,0:T(8,128)(2,1)S(1)} %collective-permute-done.refs_2_) | copy-start | bytes 884740
  65.8 11.2 %collective-permute-start.1 = (bf16[576,256]{1,0:T(8,128)(2,1)S(1)}, bf16[576,256]{1,0:T(8,128)(2,1)S(1)}, u32[]{:S(2)}, u32[]{:S(2)}) collective-permute-start(bf16[576,256]{1,0:T(8,128)(2,1)S(1)} %collective-permute-done.refs_2_), channel_id=1, source_target_pairs={{0,8},{8,16},{16,24},{24,32},{32,40},{40,48},{48,56},{56,0},{1,9},... | collective-permute-start | bytes 884744 | tf_op jit(solution)/shard_map/ppermute | solution.py:187
  73.5 39.9 %copy-start.9 = (bf16[576,256]{1,0:T(8,128)(2,1)}, bf16[576,256]{1,0:T(8,128)(2,1)S(1)}, u32[]{:S(2)}) copy-start(bf16[576,256]{1,0:T(8,128)(2,1)S(1)} %collective-permute-done.4.refs_6_) | copy-start | bytes 884740
  73.5 10.1 %collective-permute-start.5 = (bf16[576,256]{1,0:T(8,128)(2,1)S(1)}, bf16[576,256]{1,0:T(8,128)(2,1)S(1)}, u32[]{:S(2)}, u32[]{:S(2)}) collective-permute-start(bf16[576,256]{1,0:T(8,128)(2,1)S(1)} %collective-permute-done.4.refs_6_), channel_id=1, source_target_pairs={{0,56},{8,0},{16,8},{24,16},{32,24},{40,32},{48,40},{56,48},{1,57}... | collective-permute-start | bytes 884744 | tf_op jit(solution)/shard_map/ppermute | solution.py:188
  77.0 36.3 %copy-start.10 = (bf16[576,256]{1,0:T(8,128)(2,1)}, bf16[576,256]{1,0:T(8,128)(2,1)S(1)}, u32[]{:S(2)}) copy-start(bf16[576,256]{1,0:T(8,128)(2,1)S(1)} %collective-permute-done.1.refs_3_) | copy-start | bytes 884740
  77.0 11.9 %collective-permute-start.2 = (bf16[576,256]{1,0:T(8,128)(2,1)S(1)}, bf16[576,256]{1,0:T(8,128)(2,1)S(1)}, u32[]{:S(2)}, u32[]{:S(2)}) collective-permute-start(bf16[576,256]{1,0:T(8,128)(2,1)S(1)} %collective-permute-done.1.refs_3_), channel_id=1, source_target_pairs={{0,8},{8,16},{16,24},{24,32},{32,40},{40,48},{48,56},{56,0},{1,9},... | collective-permute-start | bytes 884744 | tf_op jit(solution)/shard_map/ppermute | solution.py:187
  83.6 29.8 %copy-start.5 = (bf16[576,256]{1,0:T(8,128)(2,1)}, bf16[576,256]{1,0:T(8,128)(2,1)S(1)}, u32[]{:S(2)}) copy-start(bf16[576,256]{1,0:T(8,128)(2,1)S(1)} %collective-permute-done.5.refs_5_) | copy-start | bytes 884740
  83.6 7.8 %collective-permute-start.7 = (bf16[288,256]{1,0:T(8,128)(2,1)S(1)}, bf16[288,256]{1,0:T(8,128)(2,1)S(1)}, u32[]{:S(2)}, u32[]{:S(2)}) collective-permute-start(bf16[288,256]{1,0:T(8,128)(2,1)S(1)} %slice.61), channel_id=1, source_target_pairs={{0,56},{8,0},{16,8},{24,16},{32,24},{40,32},{48,40},{56,48},{1,57}... | collective-permute-start | bytes 442376 | tf_op jit(solution)/shard_map/ppermute | solution.py:192
  89.0 24.4 %copy-start.6 = (bf16[576,256]{1,0:T(8,128)(2,1)}, bf16[576,256]{1,0:T(8,128)(2,1)S(1)}, u32[]{:S(2)}) copy-start(bf16[576,256]{1,0:T(8,128)(2,1)S(1)} %collective-permute-done.2.refs_4_) | copy-start | bytes 884740
  89.0 8.6 %collective-permute-start.6 = (bf16[288,256]{1,0:T(8,128)(2,1)S(1)}, bf16[288,256]{1,0:T(8,128)(2,1)S(1)}, u32[]{:S(2)}, u32[]{:S(2)}) collective-permute-start(bf16[288,256]{1,0:T(8,128)(2,1)S(1)} %slice.60), channel_id=1, source_target_pairs={{0,8},{8,16},{16,24},{24,32},{32,40},{40,48},{48,56},{56,0},{1,9},... | collective-permute-start | bytes 442376 | tf_op jit(solution)/shard_map/ppermute | solution.py:191
  91.4 22.0 %copy-start.11 = (bf16[288,256]{1,0:T(8,128)(2,1)}, bf16[288,256]{1,0:T(8,128)(2,1)S(1)}, u32[]{:S(2)}) copy-start(bf16[288,256]{1,0:T(8,128)(2,1)S(1)} %collective-permute-done.7.refs_9_) | copy-start | bytes 442372
  97.6 15.8 %copy-start.12 = (bf16[288,256]{1,0:T(8,128)(2,1)}, bf16[288,256]{1,0:T(8,128)(2,1)S(1)}, u32[]{:S(2)}) copy-start(bf16[288,256]{1,0:T(8,128)(2,1)S(1)} %collective-permute-done.6.refs_8_) | copy-start | bytes 442372
  113.4 23.0 %copy-start.1 = (bf16[256,256]{1,0:T(8,128)(2,1)S(1)}, bf16[256,256]{1,0:T(8,128)(2,1)}, u32[]{:S(2)}) copy-start(bf16[256,256]{1,0:T(8,128)(2,1)} %weight_ref.1) | copy-start | bytes 393220
  113.4 23.0 %copy-start.3 = (bf16[128,256]{1,0:T(8,128)(2,1)S(1)}, bf16[128,256]{1,0:T(8,128)(2,1)}, u32[]{:S(2)}) copy-start(bf16[128,256]{1,0:T(8,128)(2,1)} %cotangent_ref.1) | copy-start | bytes 196612
  113.4 23.0 %copy-start.4 = (f32[256]{0:T(256)S(1)}, f32[256]{0:T(256)}, u32[]{:S(2)}) copy-start(f32[256]{0:T(256)} %param.12) | copy-start | bytes 3076
Sparse Core Ops, SparseCore 0:
  55.3 57.9 all-gather.1

commit v6 on v4

v6 whole, which is shorter than its diff:
```python
import functools
import math

import jax
import jax.numpy as jnp
import numpy as np
from jax import lax
from jax.experimental import pallas as pl
from jax.experimental.pallas import tpu as pltpu
from jax.sharding import Mesh, PartitionSpec as P

BLOCK = 64
BPD = 2
UNROLL = 12
SPMM_MIB = 58
STREAMS = 2
MIB = 1024 * 1024
REP = ("x", "core")
PLANE = ("y", "x", "core")
SUB, LANES = 8, 128
SMEM = pl.BlockSpec(memory_space=pltpu.SMEM)
HBM = pl.BlockSpec(memory_space=pltpu.HBM)
VMEM = pl.BlockSpec(memory_space=pltpu.VMEM)


def choose(index, low, actions):
    if len(actions) == 1:
        actions[0]()
        return
    middle = len(actions) // 2

    @pl.when(index < low + middle)
    def _():
        choose(index, low, actions[:middle])

    @pl.when(index >= low + middle)
    def _():
        choose(index, low + middle, actions[middle:])


def spmm_kernel(
    rows_ref, tiles_ref, count_ref, which_ref, start_ref, table_ref, *refs
):
    *sources, out_ref, picked, table, total, sems, table_sem = refs
    count = count_ref[0, 0]
    steps = (count + UNROLL - 1) // UNROLL
    table_copy = pltpu.make_async_copy(table_ref, table, table_sem)
    table_copy.start()

    def fetch(s, source, start):
        return pltpu.make_async_copy(
            source.at[pl.ds(pl.multiple_of(start, BLOCK), BLOCK)], picked.at[s], sems.at[s]
        )

    def begin(s, carry):
        start = start_ref[s]
        choose(which_ref[s], 0, [fetch(s, source, start).start for source in sources])
        return carry

    lax.fori_loop(0, steps * UNROLL, begin, 0)
    total[...] = jnp.zeros_like(total)
    table_copy.wait()

    def step(i, carry):
        for k in range(UNROLL):
            fetch(i * UNROLL + k, sources[0], 0).wait()
        for k in range(UNROLL):
            s = i * UNROLL + k
            product = jnp.dot(
                table[tiles_ref[0, 0, s]], picked[s], preferred_element_type=jnp.float32
            )
            row = pl.multiple_of(rows_ref[0, 0, s] * BLOCK, BLOCK)
            total[pl.ds(row, BLOCK)] += jnp.where(s < count, product, 0.0)
        return carry

    lax.fori_loop(0, steps, step, 0)
    out_ref[...] = total[...].astype(out_ref.dtype)


def spmm(lists, which, start, sources, tile_table, out_rows):
    slots = start.shape[0]
    width = sources[0].shape[1]
    return pl.pallas_call(
        spmm_kernel,
        out_shape=jax.ShapeDtypeStruct((out_rows, width), jnp.bfloat16),
        in_specs=[SMEM] * 5 + [HBM] * (1 + len(sources)),
        out_specs=VMEM,
        scratch_shapes=[
            pltpu.VMEM((slots, BLOCK, width), jnp.bfloat16),
            pltpu.VMEM(tile_table.shape, tile_table.dtype),
            pltpu.VMEM((out_rows, width), jnp.float32),
            pltpu.SemaphoreType.DMA((slots,)),
            pltpu.SemaphoreType.DMA,
        ],
        compiler_params=pltpu.CompilerParams(vmem_limit_bytes=SPMM_MIB * MIB),
        name="spmm",
    )(*lists, which, start, tile_table, *sources)


def layer_kernel(
    factor, parts_ref, weight_ref, bias_ref, cotangent_ref, out_ref, grads_ref
):
    summed = parts_ref[0].astype(jnp.float32)
    for r in range(1, parts_ref.shape[0]):
        summed += parts_ref[r].astype(jnp.float32)
    agg = summed.astype(jnp.bfloat16)
    pre = jnp.dot(agg, weight_ref[...], preferred_element_type=jnp.float32) + bias_ref[...]
    sigma = 1.0 / (1.0 + jnp.exp(-pre))
    out_ref[...] = (pre * sigma).astype(out_ref.dtype)
    grad_pre = (
        cotangent_ref[...].astype(jnp.float32) * (sigma * (1.0 + pre * (1.0 - sigma)))
    ).astype(jnp.bfloat16)
    weight_grad = factor * lax.dot_general(
        agg, grad_pre, (((0,), (0,)), ((), ())), preferred_element_type=jnp.float32
    )
    bias = factor * jnp.sum(grad_pre.astype(jnp.float32), axis=0, keepdims=True)
    first = lax.broadcasted_iota(jnp.int32, (SUB, LANES), 0) == 0
    across = bias.shape[1] // LANES
    for n in range(grads_ref.shape[0]):
        row, col = n // across * SUB, n % across * LANES
        tile = weight_grad[row : row + SUB, col : col + LANES]
        extra = jnp.where(first, bias[:, col : col + LANES], 0.0)
        if n >= across:
            extra = jnp.zeros_like(extra)
        grads_ref[n] = jnp.concatenate([tile, extra]).astype(grads_ref.dtype)


def fold_kernel(parts_ref, out_ref):
    total = parts_ref[0].astype(jnp.float32)
    for n in range(1, parts_ref.shape[0]):
        total += parts_ref[n].astype(jnp.float32)
    for n in range(out_ref.shape[0]):
        out_ref[n] = total.astype(out_ref.dtype)


def fold(parts, copies):
    return pl.pallas_call(
        fold_kernel,
        out_shape=jax.ShapeDtypeStruct((copies,) + parts.shape[1:], parts.dtype),
        in_specs=[VMEM],
        out_specs=VMEM,
        compiler_params=pltpu.CompilerParams(vmem_limit_bytes=16 * MIB),
        name="fold",
    )(parts)


def finish_kernel(grads_ref, weight_ref, bias_ref):
    across = bias_ref.shape[1] // LANES
    for n in range(grads_ref.shape[0]):
        row, col = n // across * SUB, n % across * LANES
        tile = grads_ref[n].astype(jnp.float32)
        weight_ref[row : row + SUB, col : col + LANES] = tile[:SUB]
        if n < across:
            bias_ref[:, col : col + LANES] = tile[SUB : SUB + 1]


def finish(grads, width):
    return pl.pallas_call(
        finish_kernel,
        out_shape=(
            jax.ShapeDtypeStruct((width, width), jnp.float32),
            jax.ShapeDtypeStruct((1, width), jnp.float32),
        ),
        in_specs=[VMEM],
        out_specs=(VMEM, VMEM),
        compiler_params=pltpu.CompilerParams(vmem_limit_bytes=16 * MIB),
        name="finish",
    )(grads)


def layer(parts, weight, bias_term, cotangent, factor):
    width = weight.shape[0]
    return pl.pallas_call(
        functools.partial(layer_kernel, factor),
        out_shape=(
            jax.ShapeDtypeStruct(cotangent.shape, jnp.bfloat16),
            jax.ShapeDtypeStruct((width * width // (SUB * LANES), 2 * SUB, LANES), jnp.bfloat16),
        ),
        in_specs=[VMEM] * 4,
        out_specs=(VMEM, VMEM),
        compiler_params=pltpu.CompilerParams(vmem_limit_bytes=16 * MIB),
        name="layer",
    )(parts, weight, bias_term.reshape(1, -1), cotangent)


def scattered(array, axis):
    size = lax.axis_size(axis)
    parts = array.reshape(size, array.shape[0] // size, array.shape[1])
    return lax.all_to_all(parts, axis, split_axis=0, concat_axis=0, tiled=True)


def total_over_all(grads):
    size = lax.axis_size(PLANE)
    parts = grads.reshape(size, -1, LANES)

    def swap(array, axis):
        return lax.all_to_all(array, axis, split_axis=0, concat_axis=0, tiled=True)

    share = fold(swap(parts, PLANE), lax.axis_size("z"))
    share = fold(swap(share, "z"), size)
    return swap(share, PLANE).reshape(grads.shape)


def both_ways(block, axis, last_up):
    n = lax.axis_size(axis)
    up = [(i, (i + 1) % n) for i in range(n)]
    down = [(i, (i - 1) % n) for i in range(n)]
    before, after = [block], [block]
    for _ in range(n // 2 - 1):
        before.append(lax.ppermute(before[-1], axis, up))
        after.append(lax.ppermute(after[-1], axis, down))
    far = lax.ppermute(before[-1], axis, up) if last_up else lax.ppermute(after[-1], axis, down)
    return before + after[:0:-1] + [far]


def shards(
    features, tile_table, weight, bias_term, cotangent, adj_rows, adj_cols, adj_tiles, adj_count
):
    own_rows, width = features.shape
    rep_size = lax.axis_size(REP)
    lists = (adj_rows, adj_tiles, adj_count)
    ny, nz = lax.axis_size("y"), lax.axis_size("z")
    along_z = lax.all_gather(features, "z", axis=0, tiled=True)
    depth = along_z.shape[0] // STREAMS
    sources = []
    for n in range(STREAMS):
        sources += both_ways(along_z[n * depth : (n + 1) * depth], "y", n % 2 == 0)

    cols = adj_cols[0, 0]
    panel = cols // BPD
    start = panel // ny * own_rows + cols % BPD * BLOCK
    stream, start = start // depth, start % depth
    behind = (lax.axis_index("y") - panel) % ny
    which = jnp.where(behind == ny // 2, ny - 1, behind - (behind > ny // 2)) + stream * ny

    rows = rep_size * own_rows
    share = spmm(lists, which, start, sources, tile_table, rows)
    parts = scattered(share, REP)
    factor = 1.0 / math.sqrt(nz * ny * rows)
    output, grads = layer(parts, weight, bias_term, cotangent, factor)
    weight_grad, bias_grad = finish(total_over_all(grads), width)
    return (output, weight_grad, bias_grad.reshape(width))


def solution(mesh):
    panels, rep = mesh.devices.shape
    ny = 8 if panels % 8 == 0 else 2
    devices = np.asarray(mesh.devices).reshape(panels // ny, ny, rep // 2, 2)
    rows = ("z", "y")
    return jax.shard_map(
        shards,
        mesh=Mesh(devices, ("z", "y", "x", "core")),
        in_specs=(
            P(rows + REP, None),
            P(),
            P(),
            P(),
            P(rows + REP, None),
            P(rows, REP, None),
            P(rows, REP, None),
            P(rows, REP, None),
            P(rows, REP),
        ),
        out_specs=(P(rows + REP, None), P(), P()),
        check_vma=False,
    )
```

time: 190 us -> 177 us (0.932)
  starting transfers between devices: 25 us -> 44.3 us
  blocking collectives: 123 us -> 104 us
  between operations: 14.9 us -> 1.64 us
  local copies, waits for them, and re-layouts: 3.52 us -> 1.44 us
  waiting for transfers between devices: 16.2 us -> 18.1 us
    all_to_all x2 -> x1, blocking collectives: 38.6 us -> 19.8 us  [scattered(): return lax.all_to_all(parts, axis, split_axis=0, concat_axis=0, tiled=True)]
    ppermute x3 -> x6, starting transfers between devices: 11.1 us -> 27.5 us  [both_ways(): after.append(lax.ppermute(after[-1], axis, down))]
    ppermute x3 -> x6, waiting for transfers between devices: 9.35 us -> 0.57 us  [both_ways(): after.append(lax.ppermute(after[-1], axis, down))]
    ppermute x3 -> x6, waiting for transfers between devices: 1.02 us -> 9.19 us  [both_ways(): before.append(lax.ppermute(before[-1], axis, up))]
    ppermute x3 -> x6, starting transfers between devices: 6.71 us -> 11.5 us  [both_ways(): before.append(lax.ppermute(before[-1], axis, up))]
    slice x6 -> x1, local copies, waits for them, and re-layouts: 2.83 us -> 0.05 us  [shards(): sources += both_ways(along_z[n * depth:(n + 1) * depth], 'y', n % 2 == 0)]
    all_to_all x4 -> x3, blocking collectives: 53.5 us -> 50.9 us  [swap(): return lax.all_to_all(array, axis, split_axis=0, concat_axis=0, tiled=True)]
    ppermute x2, waiting for transfers between devices: 5.85 us -> 8.31 us  [the longest x1 5.6 us: both_ways(): lax.ppermute(before[-1], axis, up)]
  transfers between devices with their start and end apart: 9 -> 14, of which waited for: 7 -> 6; matrix products, arithmetic and copies ran while one was open for 1% -> 1% of each run, Pallas kernels for 0% -> 0%
where the time goes in v6:
time: 177 us
  blocking collectives  104 us (59%)
  starting transfers between devices  44.3 us (25%)
  waiting for transfers between devices  18.1 us (10%)
  Pallas kernels  6.5 us (4%)
    all_to_all x3, blocking collectives, swap(): return lax.all_to_all(array, axis, split_axis=0, concat_axis=0, tiled=True)  50.9 us
    all_gather x1, blocking collectives, shards(): along_z = lax.all_gather(features, 'z', axis=0, tiled=True)  32.9 us
    ppermute x6, starting transfers between devices, both_ways(): after.append(lax.ppermute(after[-1], axis, down))  27.5 us
    all_to_all x1, blocking collectives, scattered(): return lax.all_to_all(parts, axis, split_axis=0, concat_axis=0, tiled=True)  19.8 us
    ppermute x6, starting transfers between devices, both_ways(): before.append(lax.ppermute(before[-1], axis, up))  11.5 us
    ppermute x6, waiting for transfers between devices, both_ways(): before.append(lax.ppermute(before[-1], axis, up))  9.19 us
    ppermute x1, waiting for transfers between devices, both_ways(): lax.ppermute(before[-1], axis, up)  5.6 us
    pallas_call x1, Pallas kernels, spmm(): pl.pallas_call(spmm_kernel, out_shape=jax.ShapeDtypeStruct((out_rows, wid...  4.82 us
  transfers between devices with their start and end apart: 14, of which 6 were waited for; matrix products, arithmetic and copies ran while one was open for 1% of the time, Pallas kernels for 0%

profile of v6, /device:TPU:1, one launch (start us, length us, event | category | flops | bytes accessed | tf_op | source)
XLA Modules:
  0.0 176.6 jit_solution(1579291935893349628)
XLA Ops:
  0.6 32.9 %all_gather.3 = bf16[1536,256]{1,0:T(8,128)(2,1)S(1)} all-gather(bf16[128,256]{1,0:T(8,128)(2,1)} %param.9), channel_id=1, replica_groups=mesh['z'=12,'y'=8,'x'=4,'core'=2] {'z'}, dimensions={0}, use_global_device_ids=true | all-gather | bytes 851968 | tf_op jit(solution)/shard_map/all_gather | solution.py:223
  33.6 0.1 fusion.6
  33.6 0.0 copy-start.3
  33.6 5.1 %collective-permute-start.10 = (bf16[768,256]{1,0:T(8,128)(2,1)S(1)}, bf16[768,256]{1,0:T(8,128)(2,1)S(1)}, u32[]{:S(2)}, u32[]{:S(2)}) collective-permute-start(bf16[768,256]{1,0:T(8,128)(2,1)S(1)} %get-tuple-element.14.refs_8_), channel_id=1, source_target_pairs={{0,56},{8,0},{16,8},{24,16},{32,24},{40,32},{48,40},{56,48},{1,57}... | collective-permute-start | bytes 1179656 | tf_op jit(solution)/shard_map/ppermute | solution.py:211
  38.7 1.9 %collective-permute-start = (bf16[768,256]{1,0:T(8,128)(2,1)S(1)}, bf16[768,256]{1,0:T(8,128)(2,1)S(1)}, u32[]{:S(2)}, u32[]{:S(2)}) collective-permute-start(bf16[768,256]{1,0:T(8,128)(2,1)S(1)} %get-tuple-element.15.refs_0_), channel_id=1, source_target_pairs={{0,8},{8,16},{16,24},{24,32},{32,40},{40,48},{48,56},{56,0},{1,9},... | collective-permute-start | bytes 1179656 | tf_op jit(solution)/shard_map/ppermute | solution.py:210
  40.7 1.9 %collective-permute-start.7 = (bf16[768,256]{1,0:T(8,128)(2,1)S(1)}, bf16[768,256]{1,0:T(8,128)(2,1)S(1)}, u32[]{:S(2)}, u32[]{:S(2)}) collective-permute-start(bf16[768,256]{1,0:T(8,128)(2,1)S(1)} %get-tuple-element.14.refs_8_), channel_id=1, source_target_pairs={{0,8},{8,16},{16,24},{24,32},{32,40},{40,48},{48,56},{56,0},{1,9},... | collective-permute-start | bytes 1179656 | tf_op jit(solution)/shard_map/ppermute | solution.py:210
  42.6 4.6 %collective-permute-start.3 = (bf16[768,256]{1,0:T(8,128)(2,1)S(1)}, bf16[768,256]{1,0:T(8,128)(2,1)S(1)}, u32[]{:S(2)}, u32[]{:S(2)}) collective-permute-start(bf16[768,256]{1,0:T(8,128)(2,1)S(1)} %get-tuple-element.15.refs_0_), channel_id=1, source_target_pairs={{0,56},{8,0},{16,8},{24,16},{32,24},{40,32},{48,40},{56,48},{1,57}... | collective-permute-start | bytes 1179656 | tf_op jit(solution)/shard_map/ppermute | solution.py:211
  47.2 0.0 collective-permute-done.10.refs_14_
  47.2 3.4 %collective-permute-start.11 = (bf16[768,256]{1,0:T(8,128)(2,1)S(1)}, bf16[768,256]{1,0:T(8,128)(2,1)S(1)}, u32[]{:S(2)}, u32[]{:S(2)}) collective-permute-start(bf16[768,256]{1,0:T(8,128)(2,1)S(1)} %collective-permute-done.10.refs_14_), channel_id=1, source_target_pairs={{0,56},{8,0},{16,8},{24,16},{32,24},{40,32},{48,40},{56,48},{1,57}... | collective-permute-start | bytes 1179656 | tf_op jit(solution)/shard_map/ppermute | solution.py:211
  50.6 0.0 collective-permute-done.refs_1_
  50.6 0.0 copy-start.6
  50.6 1.9 %collective-permute-start.1 = (bf16[768,256]{1,0:T(8,128)(2,1)S(1)}, bf16[768,256]{1,0:T(8,128)(2,1)S(1)}, u32[]{:S(2)}, u32[]{:S(2)}) collective-permute-start(bf16[768,256]{1,0:T(8,128)(2,1)S(1)} %collective-permute-done.refs_1_), channel_id=1, source_target_pairs={{0,8},{8,16},{16,24},{24,32},{32,40},{40,48},{48,56},{56,0},{1,9},... | collective-permute-start | bytes 1179656 | tf_op jit(solution)/shard_map/ppermute | solution.py:210
  52.5 2.2 %collective-permute-done.7.refs_9_ = bf16[768,256]{1,0:T(8,128)(2,1)S(1)} collective-permute-done((bf16[768,256]{1,0:T(8,128)(2,1)S(1)}, bf16[768,256]{1,0:T(8,128)(2,1)S(1)}, u32[]{:S(2)}, u32[]{:S(2)}) %collective-permute-start.7) | collective-permute-done | bytes 393248 | tf_op jit(solution)/shard_map/ppermute | solution.py:210
  54.7 1.9 %collective-permute-start.8 = (bf16[768,256]{1,0:T(8,128)(2,1)S(1)}, bf16[768,256]{1,0:T(8,128)(2,1)S(1)}, u32[]{:S(2)}, u32[]{:S(2)}) collective-permute-start(bf16[768,256]{1,0:T(8,128)(2,1)S(1)} %collective-permute-done.7.refs_9_), channel_id=1, source_target_pairs={{0,8},{8,16},{16,24},{24,32},{32,40},{40,48},{48,56},{56,0},{1,9},... | collective-permute-start | bytes 1179656 | tf_op jit(solution)/shard_map/ppermute | solution.py:210
  56.6 0.0 collective-permute-done.3.refs_6_
  56.6 4.6 %collective-permute-start.4 = (bf16[768,256]{1,0:T(8,128)(2,1)S(1)}, bf16[768,256]{1,0:T(8,128)(2,1)}, u32[]{:S(2)}, u32[]{:S(2)}) collective-permute-start(bf16[768,256]{1,0:T(8,128)(2,1)S(1)} %collective-permute-done.3.refs_6_), channel_id=1, source_target_pairs={{0,56},{8,0},{16,8},{24,16},{32,24},{40,32},{48,40},{56,48},{1,57}... | collective-permute-start | bytes 1179656 | tf_op jit(solution)/shard_map/ppermute | solution.py:211
  61.2 0.6 collective-permute-done.11.refs_13_
  61.8 5.3 %collective-permute-start.12 = (bf16[768,256]{1,0:T(8,128)(2,1)S(1)}, bf16[768,256]{1,0:T(8,128)(2,1)}, u32[]{:S(2)}, u32[]{:S(2)}) collective-permute-start(bf16[768,256]{1,0:T(8,128)(2,1)S(1)} %collective-permute-done.11.refs_13_), channel_id=1, source_target_pairs={{0,56},{8,0},{16,8},{24,16},{32,24},{40,32},{48,40},{56,48},{1,57}... | collective-permute-start | bytes 1179656 | tf_op jit(solution)/shard_map/ppermute | solution.py:211
  67.1 0.0 collective-permute-done.1.refs_2_
  67.1 1.9 %collective-permute-start.2 = (bf16[768,256]{1,0:T(8,128)(2,1)S(1)}, bf16[768,256]{1,0:T(8,128)(2,1)}, u32[]{:S(2)}, u32[]{:S(2)}) collective-permute-start(bf16[768,256]{1,0:T(8,128)(2,1)S(1)} %collective-permute-done.1.refs_2_), channel_id=1, source_target_pairs={{0,8},{8,16},{16,24},{24,32},{32,40},{40,48},{48,56},{56,0},{1,9},... | collective-permute-start | bytes 1179656 | tf_op jit(solution)/shard_map/ppermute | solution.py:210
  69.1 0.0 copy-start.16
  69.7 3.6 %collective-permute-done.8.refs_10_ = bf16[768,256]{1,0:T(8,128)(2,1)S(1)} collective-permute-done((bf16[768,256]{1,0:T(8,128)(2,1)S(1)}, bf16[768,256]{1,0:T(8,128)(2,1)S(1)}, u32[]{:S(2)}, u32[]{:S(2)}) %collective-permute-start.8) | collective-permute-done | bytes 393248 | tf_op jit(solution)/shard_map/ppermute | solution.py:210
  73.3 1.9 %collective-permute-start.9 = (bf16[768,256]{1,0:T(8,128)(2,1)S(1)}, bf16[768,256]{1,0:T(8,128)(2,1)S(1)}, u32[]{:S(2)}, u32[]{:S(2)}) collective-permute-start(bf16[768,256]{1,0:T(8,128)(2,1)S(1)} %collective-permute-done.8.refs_10_), channel_id=1, source_target_pairs={{0,8},{8,16},{16,24},{24,32},{32,40},{40,48},{48,56},{56,0},{1,9},... | collective-permute-start | bytes 1179656 | tf_op jit(solution)/shard_map/ppermute | solution.py:210
  75.2 0.0 collective-permute-done.4.refs_5_
  75.2 4.6 %collective-permute-start.5 = (bf16[768,256]{1,0:T(8,128)(2,1)}, bf16[768,256]{1,0:T(8,128)(2,1)S(1)}, u32[]{:S(2)}, u32[]{:S(2)}) collective-permute-start(bf16[768,256]{1,0:T(8,128)(2,1)} %collective-permute-done.4.refs_5_), channel_id=1, source_target_pairs={{0,56},{8,0},{16,8},{24,16},{32,24},{40,32},{48,40},{56,48},{1,57}... | collective-permute-start | bytes 1179656 | tf_op jit(solution)/shard_map/ppermute | solution.py:211
  79.8 0.0 collective-permute-done.12.refs_12_
  79.8 1.9 %collective-permute-start.13 = (bf16[768,256]{1,0:T(8,128)(2,1)}, bf16[768,256]{1,0:T(8,128)(2,1)S(1)}, u32[]{:S(2)}, u32[]{:S(2)}) collective-permute-start(bf16[768,256]{1,0:T(8,128)(2,1)} %collective-permute-done.12.refs_12_), channel_id=1, source_target_pairs={{0,56},{8,0},{16,8},{24,16},{32,24},{40,32},{48,40},{56,48},{1,57}... | collective-permute-start | bytes 1179656 | tf_op jit(solution)/shard_map/ppermute | solution.py:212
  81.8 0.0 collective-permute-done.2.refs_3_
  81.8 3.4 %collective-permute-start.6 = (bf16[768,256]{1,0:T(8,128)(2,1)}, bf16[768,256]{1,0:T(8,128)(2,1)S(1)}, u32[]{:S(2)}, u32[]{:S(2)}) collective-permute-start(bf16[768,256]{1,0:T(8,128)(2,1)} %collective-permute-done.2.refs_3_), channel_id=1, source_target_pairs={{0,8},{8,16},{16,24},{24,32},{32,40},{40,48},{48,56},{56,0},{1,9},... | collective-permute-start | bytes 1179656 | tf_op jit(solution)/shard_map/ppermute | solution.py:212
  85.2 0.5 and_select_fusion
  85.7 0.5 fusion.1.which_ref
  86.2 3.4 %collective-permute-done.9.refs_11_ = bf16[768,256]{1,0:T(8,128)(2,1)S(1)} collective-permute-done((bf16[768,256]{1,0:T(8,128)(2,1)S(1)}, bf16[768,256]{1,0:T(8,128)(2,1)S(1)}, u32[]{:S(2)}, u32[]{:S(2)}) %collective-permute-start.9) | collective-permute-done | bytes 393248 | tf_op jit(solution)/shard_map/ppermute | solution.py:210
  89.6 0.0 collective-permute-done.5.refs_4_
  89.6 2.7 %collective-permute-done.13.refs_15_ = bf16[768,256]{1,0:T(8,128)(2,1)S(1)} collective-permute-done((bf16[768,256]{1,0:T(8,128)(2,1)}, bf16[768,256]{1,0:T(8,128)(2,1)S(1)}, u32[]{:S(2)}, u32[]{:S(2)}) %collective-permute-start.13) | collective-permute-done | bytes 393248 | tf_op jit(solution)/shard_map/ppermute | solution.py:212
  92.3 5.6 %collective-permute-done.6.refs_7_ = bf16[768,256]{1,0:T(8,128)(2,1)S(1)} collective-permute-done((bf16[768,256]{1,0:T(8,128)(2,1)}, bf16[768,256]{1,0:T(8,128)(2,1)S(1)}, u32[]{:S(2)}, u32[]{:S(2)}) %collective-permute-start.6) | collective-permute-done | bytes 393248 | tf_op jit(solution)/shard_map/ppermute | solution.py:212
  97.9 0.0 copy-done.4
  98.0 0.6 copy-done.15
  98.7 4.8 %spmm.1 = bf16[1024,256]{1,0:T(8,128)(2,1)} custom-call(s32[1,1,48]{2,1,0:T(1,128)} %rows_ref.1, s32[1,1,48]{2,1,0:T(1,128)} %tiles_ref.1, s32[1,1]{1,0:T(1,128)S(6)} %copy.12.count_ref, s32[48]{0:T(128)} %fusion.1.which_ref, s32[48]{0:T(128)} %get-tuple-element.11.start_ref, bf16[64,64,64]{2,1,0:T(8,128)(2,1)} %table_ref.1, bf16[768,256]{1,0:T(8,128)(2,1)} %copy-done.4, ...), custom_call_target="tpu_custom_call" | custom-call | tf_op jit(solution)/shard_map/spmm/pallas_call | solution.py:83
  103.5 0.0 copy-start
  103.5 0.0 copy-start.1
  103.5 19.8 %all_to_all.20.parts_ref = bf16[8,128,256]{2,1,0:T(8,128)(2,1)S(1)} all-to-all(bf16[8,128,256]{2,1,0:T(8,128)(2,1)} %bitcast.21), channel_id=1, replica_groups=mesh['z'=12,'y'=8,'x'=4,'core'=2] {'x','core'}, dimensions={0} | all-to-all | bytes 1048576 | tf_op jit(solution)/shard_map/all_to_all | solution.py:189
  123.3 0.7 copy-done.2
  124.0 0.9 layer.1
  124.9 19.4 %all_to_all.21.parts_ref = bf16[64,16,128]{2,1,0:T(8,128)(2,1)S(1)} all-to-all(bf16[64,16,128]{2,1,0:T(8,128)(2,1)S(1)} %get-tuple-element.8), channel_id=1, replica_groups=mesh['z'=12,'y'=8,'x'=4,'core'=2] {'y','x','core'}, dimensions={0} | all-to-all | bytes 524288 | tf_op jit(solution)/shard_map/all_to_all | solution.py:197
  144.3 0.1 fold.2
  144.3 12.3 %all_to_all.22.parts_ref = bf16[12,16,128]{2,1,0:T(8,128)(2,1)S(1)} all-to-all(bf16[12,16,128]{2,1,0:T(8,128)(2,1)S(1)} %fold.2), channel_id=1, replica_groups=mesh['z'=12,'y'=8,'x'=4,'core'=2] {'z'}, dimensions={0} | all-to-all | bytes 98304 | tf_op jit(solution)/shard_map/all_to_all | solution.py:197
  156.6 19.2 %all_to_all.23.grads_ref = bf16[64,16,128]{2,1,0:T(8,128)(2,1)S(1)} all-to-all(bf16[64,16,128]{2,1,0:T(8,128)(2,1)S(1)} %fold.3), channel_id=1, replica_groups=mesh['z'=12,'y'=8,'x'=4,'core'=2] {'y','x','core'}, dimensions={0} | all-to-all | bytes 524288 | tf_op jit(solution)/shard_map/all_to_all | solution.py:197
  175.8 0.7 finish.1
  (27 shorter events, 0.1 us)
Async XLA Ops:
  33.6 64.3 %copy-start.3 = (bf16[768,256]{1,0:T(8,128)(2,1)}, bf16[768,256]{1,0:T(8,128)(2,1)S(1)}, u32[]{:S(2)}) copy-start(bf16[768,256]{1,0:T(8,128)(2,1)S(1)} %get-tuple-element.14.refs_8_) | copy-start | bytes 1179652
  33.6 64.3 %copy-start.4 = (bf16[768,256]{1,0:T(8,128)(2,1)}, bf16[768,256]{1,0:T(8,128)(2,1)S(1)}, u32[]{:S(2)}) copy-start(bf16[768,256]{1,0:T(8,128)(2,1)S(1)} %get-tuple-element.15.refs_0_) | copy-start | bytes 1179652
  33.6 13.5 %collective-permute-start.10 = (bf16[768,256]{1,0:T(8,128)(2,1)S(1)}, bf16[768,256]{1,0:T(8,128)(2,1)S(1)}, u32[]{:S(2)}, u32[]{:S(2)}) collective-permute-start(bf16[768,256]{1,0:T(8,128)(2,1)S(1)} %get-tuple-element.14.refs_8_), channel_id=1, source_target_pairs={{0,56},{8,0},{16,8},{24,16},{32,24},{40,32},{48,40},{56,48},{1,57}... | collective-permute-start | bytes 1179656 | tf_op jit(solution)/shard_map/ppermute | solution.py:211
  38.7 11.8 %collective-permute-start = (bf16[768,256]{1,0:T(8,128)(2,1)S(1)}, bf16[768,256]{1,0:T(8,128)(2,1)S(1)}, u32[]{:S(2)}, u32[]{:S(2)}) collective-permute-start(bf16[768,256]{1,0:T(8,128)(2,1)S(1)} %get-tuple-element.15.refs_0_), channel_id=1, source_target_pairs={{0,8},{8,16},{16,24},{24,32},{32,40},{40,48},{48,56},{56,0},{1,9},... | collective-permute-start | bytes 1179656 | tf_op jit(solution)/shard_map/ppermute | solution.py:210
  40.7 14.0 %collective-permute-start.7 = (bf16[768,256]{1,0:T(8,128)(2,1)S(1)}, bf16[768,256]{1,0:T(8,128)(2,1)S(1)}, u32[]{:S(2)}, u32[]{:S(2)}) collective-permute-start(bf16[768,256]{1,0:T(8,128)(2,1)S(1)} %get-tuple-element.14.refs_8_), channel_id=1, source_target_pairs={{0,8},{8,16},{16,24},{24,32},{32,40},{40,48},{48,56},{56,0},{1,9},... | collective-permute-start | bytes 1179656 | tf_op jit(solution)/shard_map/ppermute | solution.py:210
  42.6 14.0 %collective-permute-start.3 = (bf16[768,256]{1,0:T(8,128)(2,1)S(1)}, bf16[768,256]{1,0:T(8,128)(2,1)S(1)}, u32[]{:S(2)}, u32[]{:S(2)}) collective-permute-start(bf16[768,256]{1,0:T(8,128)(2,1)S(1)} %get-tuple-element.15.refs_0_), channel_id=1, source_target_pairs={{0,56},{8,0},{16,8},{24,16},{32,24},{40,32},{48,40},{56,48},{1,57}... | collective-permute-start | bytes 1179656 | tf_op jit(solution)/shard_map/ppermute | solution.py:211
  47.2 50.8 %copy-start.5 = (bf16[768,256]{1,0:T(8,128)(2,1)}, bf16[768,256]{1,0:T(8,128)(2,1)S(1)}, u32[]{:S(2)}) copy-start(bf16[768,256]{1,0:T(8,128)(2,1)S(1)} %collective-permute-done.10.refs_14_) | copy-start | bytes 1179652
  47.2 14.6 %collective-permute-start.11 = (bf16[768,256]{1,0:T(8,128)(2,1)S(1)}, bf16[768,256]{1,0:T(8,128)(2,1)S(1)}, u32[]{:S(2)}, u32[]{:S(2)}) collective-permute-start(bf16[768,256]{1,0:T(8,128)(2,1)S(1)} %collective-permute-done.10.refs_14_), channel_id=1, source_target_pairs={{0,56},{8,0},{16,8},{24,16},{32,24},{40,32},{48,40},{56,48},{1,57}... | collective-permute-start | bytes 1179656 | tf_op jit(solution)/shard_map/ppermute | solution.py:211
  50.6 47.4 %copy-start.6 = (bf16[768,256]{1,0:T(8,128)(2,1)}, bf16[768,256]{1,0:T(8,128)(2,1)S(1)}, u32[]{:S(2)}) copy-start(bf16[768,256]{1,0:T(8,128)(2,1)S(1)} %collective-permute-done.refs_1_) | copy-start | bytes 1179652
  50.6 16.5 %collective-permute-start.1 = (bf16[768,256]{1,0:T(8,128)(2,1)S(1)}, bf16[768,256]{1,0:T(8,128)(2,1)S(1)}, u32[]{:S(2)}, u32[]{:S(2)}) collective-permute-start(bf16[768,256]{1,0:T(8,128)(2,1)S(1)} %collective-permute-done.refs_1_), channel_id=1, source_target_pairs={{0,8},{8,16},{16,24},{24,32},{32,40},{40,48},{48,56},{56,0},{1,9},... | collective-permute-start | bytes 1179656 | tf_op jit(solution)/shard_map/ppermute | solution.py:210
  54.7 43.3 %copy-start.7 = (bf16[768,256]{1,0:T(8,128)(2,1)}, bf16[768,256]{1,0:T(8,128)(2,1)S(1)}, u32[]{:S(2)}) copy-start(bf16[768,256]{1,0:T(8,128)(2,1)S(1)} %collective-permute-done.7.refs_9_) | copy-start | bytes 1179652
  54.7 18.6 %collective-permute-start.8 = (bf16[768,256]{1,0:T(8,128)(2,1)S(1)}, bf16[768,256]{1,0:T(8,128)(2,1)S(1)}, u32[]{:S(2)}, u32[]{:S(2)}) collective-permute-start(bf16[768,256]{1,0:T(8,128)(2,1)S(1)} %collective-permute-done.7.refs_9_), channel_id=1, source_target_pairs={{0,8},{8,16},{16,24},{24,32},{32,40},{40,48},{48,56},{56,0},{1,9},... | collective-permute-start | bytes 1179656 | tf_op jit(solution)/shard_map/ppermute | solution.py:210
  56.6 41.3 %copy-start.8 = (bf16[768,256]{1,0:T(8,128)(2,1)}, bf16[768,256]{1,0:T(8,128)(2,1)S(1)}, u32[]{:S(2)}) copy-start(bf16[768,256]{1,0:T(8,128)(2,1)S(1)} %collective-permute-done.3.refs_6_) | copy-start | bytes 1179652
  56.6 18.6 %collective-permute-start.4 = (bf16[768,256]{1,0:T(8,128)(2,1)S(1)}, bf16[768,256]{1,0:T(8,128)(2,1)}, u32[]{:S(2)}, u32[]{:S(2)}) collective-permute-start(bf16[768,256]{1,0:T(8,128)(2,1)S(1)} %collective-permute-done.3.refs_6_), channel_id=1, source_target_pairs={{0,56},{8,0},{16,8},{24,16},{32,24},{40,32},{48,40},{56,48},{1,57}... | collective-permute-start | bytes 1179656 | tf_op jit(solution)/shard_map/ppermute | solution.py:211
  61.8 36.2 %copy-start.9 = (bf16[768,256]{1,0:T(8,128)(2,1)}, bf16[768,256]{1,0:T(8,128)(2,1)S(1)}, u32[]{:S(2)}) copy-start(bf16[768,256]{1,0:T(8,128)(2,1)S(1)} %collective-permute-done.11.refs_13_) | copy-start | bytes 1179652
  61.8 18.0 %collective-permute-start.12 = (bf16[768,256]{1,0:T(8,128)(2,1)S(1)}, bf16[768,256]{1,0:T(8,128)(2,1)}, u32[]{:S(2)}, u32[]{:S(2)}) collective-permute-start(bf16[768,256]{1,0:T(8,128)(2,1)S(1)} %collective-permute-done.11.refs_13_), channel_id=1, source_target_pairs={{0,56},{8,0},{16,8},{24,16},{32,24},{40,32},{48,40},{56,48},{1,57}... | collective-permute-start | bytes 1179656 | tf_op jit(solution)/shard_map/ppermute | solution.py:211
  67.1 30.9 %copy-start.10 = (bf16[768,256]{1,0:T(8,128)(2,1)}, bf16[768,256]{1,0:T(8,128)(2,1)S(1)}, u32[]{:S(2)}) copy-start(bf16[768,256]{1,0:T(8,128)(2,1)S(1)} %collective-permute-done.1.refs_2_) | copy-start | bytes 1179652
  67.1 14.6 %collective-permute-start.2 = (bf16[768,256]{1,0:T(8,128)(2,1)S(1)}, bf16[768,256]{1,0:T(8,128)(2,1)}, u32[]{:S(2)}, u32[]{:S(2)}) collective-permute-start(bf16[768,256]{1,0:T(8,128)(2,1)S(1)} %collective-permute-done.1.refs_2_), channel_id=1, source_target_pairs={{0,8},{8,16},{16,24},{24,32},{32,40},{40,48},{48,56},{56,0},{1,9},... | collective-permute-start | bytes 1179656 | tf_op jit(solution)/shard_map/ppermute | solution.py:210
  69.1 16.1 %copy-start.16 = (s32[1,1,48]{2,1,0:T(1,128)S(1)}, s32[1,1,48]{2,1,0:T(1,128)}, u32[]{:S(2)}) copy-start(s32[1,1,48]{2,1,0:T(1,128)} %param.15) | copy-start | bytes 580
  73.3 24.7 %copy-start.11 = (bf16[768,256]{1,0:T(8,128)(2,1)}, bf16[768,256]{1,0:T(8,128)(2,1)S(1)}, u32[]{:S(2)}) copy-start(bf16[768,256]{1,0:T(8,128)(2,1)S(1)} %collective-permute-done.8.refs_10_) | copy-start | bytes 1179652
  73.3 16.3 %collective-permute-start.9 = (bf16[768,256]{1,0:T(8,128)(2,1)S(1)}, bf16[768,256]{1,0:T(8,128)(2,1)S(1)}, u32[]{:S(2)}, u32[]{:S(2)}) collective-permute-start(bf16[768,256]{1,0:T(8,128)(2,1)S(1)} %collective-permute-done.8.refs_10_), channel_id=1, source_target_pairs={{0,8},{8,16},{16,24},{24,32},{32,40},{40,48},{48,56},{56,0},{1,9},... | collective-permute-start | bytes 1179656 | tf_op jit(solution)/shard_map/ppermute | solution.py:210
  75.2 14.4 %collective-permute-start.5 = (bf16[768,256]{1,0:T(8,128)(2,1)}, bf16[768,256]{1,0:T(8,128)(2,1)S(1)}, u32[]{:S(2)}, u32[]{:S(2)}) collective-permute-start(bf16[768,256]{1,0:T(8,128)(2,1)} %collective-permute-done.4.refs_5_), channel_id=1, source_target_pairs={{0,56},{8,0},{16,8},{24,16},{32,24},{40,32},{48,40},{56,48},{1,57}... | collective-permute-start | bytes 1179656 | tf_op jit(solution)/shard_map/ppermute | solution.py:211
  79.8 12.5 %collective-permute-start.13 = (bf16[768,256]{1,0:T(8,128)(2,1)}, bf16[768,256]{1,0:T(8,128)(2,1)S(1)}, u32[]{:S(2)}, u32[]{:S(2)}) collective-permute-start(bf16[768,256]{1,0:T(8,128)(2,1)} %collective-permute-done.12.refs_12_), channel_id=1, source_target_pairs={{0,56},{8,0},{16,8},{24,16},{32,24},{40,32},{48,40},{56,48},{1,57}... | collective-permute-start | bytes 1179656 | tf_op jit(solution)/shard_map/ppermute | solution.py:212
  81.8 16.2 %collective-permute-start.6 = (bf16[768,256]{1,0:T(8,128)(2,1)}, bf16[768,256]{1,0:T(8,128)(2,1)S(1)}, u32[]{:S(2)}, u32[]{:S(2)}) collective-permute-start(bf16[768,256]{1,0:T(8,128)(2,1)} %collective-permute-done.2.refs_3_), channel_id=1, source_target_pairs={{0,8},{8,16},{16,24},{24,32},{32,40},{40,48},{48,56},{56,0},{1,9},... | collective-permute-start | bytes 1179656 | tf_op jit(solution)/shard_map/ppermute | solution.py:212
  89.6 8.4 %copy-start.12 = (bf16[768,256]{1,0:T(8,128)(2,1)}, bf16[768,256]{1,0:T(8,128)(2,1)S(1)}, u32[]{:S(2)}) copy-start(bf16[768,256]{1,0:T(8,128)(2,1)S(1)} %collective-permute-done.9.refs_11_) | copy-start | bytes 1179652
  89.6 8.4 %copy-start.13 = (bf16[768,256]{1,0:T(8,128)(2,1)}, bf16[768,256]{1,0:T(8,128)(2,1)S(1)}, u32[]{:S(2)}) copy-start(bf16[768,256]{1,0:T(8,128)(2,1)S(1)} %collective-permute-done.5.refs_4_) | copy-start | bytes 1179652
  92.3 5.7 %copy-start.14 = (bf16[768,256]{1,0:T(8,128)(2,1)}, bf16[768,256]{1,0:T(8,128)(2,1)S(1)}, u32[]{:S(2)}) copy-start(bf16[768,256]{1,0:T(8,128)(2,1)S(1)} %collective-permute-done.13.refs_15_) | copy-start | bytes 1179652
  97.9 0.8 copy-start.15
  103.5 19.8 %copy-start = (bf16[256,256]{1,0:T(8,128)(2,1)S(1)}, bf16[256,256]{1,0:T(8,128)(2,1)}, u32[]{:S(2)}) copy-start(bf16[256,256]{1,0:T(8,128)(2,1)} %weight_ref.1) | copy-start | bytes 393220
  103.5 19.8 %copy-start.1 = (bf16[128,256]{1,0:T(8,128)(2,1)S(1)}, bf16[128,256]{1,0:T(8,128)(2,1)}, u32[]{:S(2)}) copy-start(bf16[128,256]{1,0:T(8,128)(2,1)} %cotangent_ref.1) | copy-start | bytes 196612
  123.3 0.7 copy-start.2

commit v7 on v6

--- a/solution.py
+++ b/solution.py
@@ -52,12 +52,14 @@
             source.at[pl.ds(pl.multiple_of(start, BLOCK), BLOCK)], picked.at[s], sems.at[s]
         )
 
-    def begin(s, carry):
-        start = start_ref[s]
-        choose(which_ref[s], 0, [fetch(s, source, start).start for source in sources])
+    def begin(i, carry):
+        for k in range(4):
+            s = i * 4 + k
+            start = start_ref[s]
+            choose(which_ref[s], 0, [fetch(s, source, start).start for source in sources])
         return carry
 
-    lax.fori_loop(0, steps * UNROLL, begin, 0)
+    lax.fori_loop(0, steps * (UNROLL // 4), begin, 0)
     total[...] = jnp.zeros_like(total)
     table_copy.wait()
 

time: 177 us -> 177 us (level)
  no operation moved by 1% of the time
where the time goes in v7:
time: 177 us
  blocking collectives  104 us (59%)
  starting transfers between devices  44.3 us (25%)
  waiting for transfers between devices  18.1 us (10%)
  Pallas kernels  5.91 us (3%)
    all_to_all x3, blocking collectives, swap(): return lax.all_to_all(array, axis, split_axis=0, concat_axis=0, tiled=True)  51.2 us
    all_gather x1, blocking collectives, shards(): along_z = lax.all_gather(features, 'z', axis=0, tiled=True)  32.9 us
    ppermute x6, starting transfers between devices, both_ways(): after.append(lax.ppermute(after[-1], axis, down))  27.5 us
    all_to_all x1, blocking collectives, scattered(): return lax.all_to_all(parts, axis, split_axis=0, concat_axis=0, tiled=True)  20.2 us
    ppermute x6, starting transfers between devices, both_ways(): before.append(lax.ppermute(before[-1], axis, up))  11.5 us
    ppermute x6, waiting for transfers between devices, both_ways(): before.append(lax.ppermute(before[-1], axis, up))  9.19 us
    ppermute x1, waiting for transfers between devices, both_ways(): lax.ppermute(before[-1], axis, up)  5.6 us
    pallas_call x1, Pallas kernels, spmm(): pl.pallas_call(spmm_kernel, out_shape=jax.ShapeDtypeStruct((out_rows, wid...  4.23 us
  transfers between devices with their start and end apart: 14, of which 6 were waited for; matrix products, arithmetic and copies ran while one was open for 1% of the time, Pallas kernels for 0%

profile of v7, /device:TPU:1, one launch (start us, length us, event | category | flops | bytes accessed | tf_op | source)
XLA Modules:
  0.0 176.7 jit_solution(5457764815941735244)
XLA Ops:
  0.6 32.9 %all_gather.3 = bf16[1536,256]{1,0:T(8,128)(2,1)S(1)} all-gather(bf16[128,256]{1,0:T(8,128)(2,1)} %param.9), channel_id=1, replica_groups=mesh['z'=12,'y'=8,'x'=4,'core'=2] {'z'}, dimensions={0}, use_global_device_ids=true | all-gather | bytes 851968 | tf_op jit(solution)/shard_map/all_gather | solution.py:225
  33.6 0.1 fusion.6
  33.6 0.0 copy-start.3
  33.6 5.1 %collective-permute-start.10 = (bf16[768,256]{1,0:T(8,128)(2,1)S(1)}, bf16[768,256]{1,0:T(8,128)(2,1)S(1)}, u32[]{:S(2)}, u32[]{:S(2)}) collective-permute-start(bf16[768,256]{1,0:T(8,128)(2,1)S(1)} %get-tuple-element.14.refs_8_), channel_id=1, source_target_pairs={{0,56},{8,0},{16,8},{24,16},{32,24},{40,32},{48,40},{56,48},{1,57}... | collective-permute-start | bytes 1179656 | tf_op jit(solution)/shard_map/ppermute | solution.py:213
  38.7 1.9 %collective-permute-start = (bf16[768,256]{1,0:T(8,128)(2,1)S(1)}, bf16[768,256]{1,0:T(8,128)(2,1)S(1)}, u32[]{:S(2)}, u32[]{:S(2)}) collective-permute-start(bf16[768,256]{1,0:T(8,128)(2,1)S(1)} %get-tuple-element.15.refs_0_), channel_id=1, source_target_pairs={{0,8},{8,16},{16,24},{24,32},{32,40},{40,48},{48,56},{56,0},{1,9},... | collective-permute-start | bytes 1179656 | tf_op jit(solution)/shard_map/ppermute | solution.py:212
  40.7 1.9 %collective-permute-start.7 = (bf16[768,256]{1,0:T(8,128)(2,1)S(1)}, bf16[768,256]{1,0:T(8,128)(2,1)S(1)}, u32[]{:S(2)}, u32[]{:S(2)}) collective-permute-start(bf16[768,256]{1,0:T(8,128)(2,1)S(1)} %get-tuple-element.14.refs_8_), channel_id=1, source_target_pairs={{0,8},{8,16},{16,24},{24,32},{32,40},{40,48},{48,56},{56,0},{1,9},... | collective-permute-start | bytes 1179656 | tf_op jit(solution)/shard_map/ppermute | solution.py:212
  42.6 4.6 %collective-permute-start.3 = (bf16[768,256]{1,0:T(8,128)(2,1)S(1)}, bf16[768,256]{1,0:T(8,128)(2,1)S(1)}, u32[]{:S(2)}, u32[]{:S(2)}) collective-permute-start(bf16[768,256]{1,0:T(8,128)(2,1)S(1)} %get-tuple-element.15.refs_0_), channel_id=1, source_target_pairs={{0,56},{8,0},{16,8},{24,16},{32,24},{40,32},{48,40},{56,48},{1,57}... | collective-permute-start | bytes 1179656 | tf_op jit(solution)/shard_map/ppermute | solution.py:213
  47.2 0.0 collective-permute-done.10.refs_14_
  47.2 3.4 %collective-permute-start.11 = (bf16[768,256]{1,0:T(8,128)(2,1)S(1)}, bf16[768,256]{1,0:T(8,128)(2,1)S(1)}, u32[]{:S(2)}, u32[]{:S(2)}) collective-permute-start(bf16[768,256]{1,0:T(8,128)(2,1)S(1)} %collective-permute-done.10.refs_14_), channel_id=1, source_target_pairs={{0,56},{8,0},{16,8},{24,16},{32,24},{40,32},{48,40},{56,48},{1,57}... | collective-permute-start | bytes 1179656 | tf_op jit(solution)/shard_map/ppermute | solution.py:213
  50.6 0.0 collective-permute-done.refs_1_
  50.6 0.0 copy-start.6
  50.6 1.9 %collective-permute-start.1 = (bf16[768,256]{1,0:T(8,128)(2,1)S(1)}, bf16[768,256]{1,0:T(8,128)(2,1)S(1)}, u32[]{:S(2)}, u32[]{:S(2)}) collective-permute-start(bf16[768,256]{1,0:T(8,128)(2,1)S(1)} %collective-permute-done.refs_1_), channel_id=1, source_target_pairs={{0,8},{8,16},{16,24},{24,32},{32,40},{40,48},{48,56},{56,0},{1,9},... | collective-permute-start | bytes 1179656 | tf_op jit(solution)/shard_map/ppermute | solution.py:212
  52.5 2.2 %collective-permute-done.7.refs_9_ = bf16[768,256]{1,0:T(8,128)(2,1)S(1)} collective-permute-done((bf16[768,256]{1,0:T(8,128)(2,1)S(1)}, bf16[768,256]{1,0:T(8,128)(2,1)S(1)}, u32[]{:S(2)}, u32[]{:S(2)}) %collective-permute-start.7) | collective-permute-done | bytes 393248 | tf_op jit(solution)/shard_map/ppermute | solution.py:212
  54.7 1.9 %collective-permute-start.8 = (bf16[768,256]{1,0:T(8,128)(2,1)S(1)}, bf16[768,256]{1,0:T(8,128)(2,1)S(1)}, u32[]{:S(2)}, u32[]{:S(2)}) collective-permute-start(bf16[768,256]{1,0:T(8,128)(2,1)S(1)} %collective-permute-done.7.refs_9_), channel_id=1, source_target_pairs={{0,8},{8,16},{16,24},{24,32},{32,40},{40,48},{48,56},{56,0},{1,9},... | collective-permute-start | bytes 1179656 | tf_op jit(solution)/shard_map/ppermute | solution.py:212
  56.6 0.0 collective-permute-done.3.refs_6_
  56.6 4.6 %collective-permute-start.4 = (bf16[768,256]{1,0:T(8,128)(2,1)S(1)}, bf16[768,256]{1,0:T(8,128)(2,1)}, u32[]{:S(2)}, u32[]{:S(2)}) collective-permute-start(bf16[768,256]{1,0:T(8,128)(2,1)S(1)} %collective-permute-done.3.refs_6_), channel_id=1, source_target_pairs={{0,56},{8,0},{16,8},{24,16},{32,24},{40,32},{48,40},{56,48},{1,57}... | collective-permute-start | bytes 1179656 | tf_op jit(solution)/shard_map/ppermute | solution.py:213
  61.2 0.6 collective-permute-done.11.refs_13_
  61.8 5.3 %collective-permute-start.12 = (bf16[768,256]{1,0:T(8,128)(2,1)S(1)}, bf16[768,256]{1,0:T(8,128)(2,1)}, u32[]{:S(2)}, u32[]{:S(2)}) collective-permute-start(bf16[768,256]{1,0:T(8,128)(2,1)S(1)} %collective-permute-done.11.refs_13_), channel_id=1, source_target_pairs={{0,56},{8,0},{16,8},{24,16},{32,24},{40,32},{48,40},{56,48},{1,57}... | collective-permute-start | bytes 1179656 | tf_op jit(solution)/shard_map/ppermute | solution.py:213
  67.1 0.0 collective-permute-done.1.refs_2_
  67.1 1.9 %collective-permute-start.2 = (bf16[768,256]{1,0:T(8,128)(2,1)S(1)}, bf16[768,256]{1,0:T(8,128)(2,1)}, u32[]{:S(2)}, u32[]{:S(2)}) collective-permute-start(bf16[768,256]{1,0:T(8,128)(2,1)S(1)} %collective-permute-done.1.refs_2_), channel_id=1, source_target_pairs={{0,8},{8,16},{16,24},{24,32},{32,40},{40,48},{48,56},{56,0},{1,9},... | collective-permute-start | bytes 1179656 | tf_op jit(solution)/shard_map/ppermute | solution.py:212
  69.1 0.0 copy-start.16
  69.7 3.6 %collective-permute-done.8.refs_10_ = bf16[768,256]{1,0:T(8,128)(2,1)S(1)} collective-permute-done((bf16[768,256]{1,0:T(8,128)(2,1)S(1)}, bf16[768,256]{1,0:T(8,128)(2,1)S(1)}, u32[]{:S(2)}, u32[]{:S(2)}) %collective-permute-start.8) | collective-permute-done | bytes 393248 | tf_op jit(solution)/shard_map/ppermute | solution.py:212
  73.3 1.9 %collective-permute-start.9 = (bf16[768,256]{1,0:T(8,128)(2,1)S(1)}, bf16[768,256]{1,0:T(8,128)(2,1)S(1)}, u32[]{:S(2)}, u32[]{:S(2)}) collective-permute-start(bf16[768,256]{1,0:T(8,128)(2,1)S(1)} %collective-permute-done.8.refs_10_), channel_id=1, source_target_pairs={{0,8},{8,16},{16,24},{24,32},{32,40},{40,48},{48,56},{56,0},{1,9},... | collective-permute-start | bytes 1179656 | tf_op jit(solution)/shard_map/ppermute | solution.py:212
  75.2 0.0 collective-permute-done.4.refs_5_
  75.2 4.6 %collective-permute-start.5 = (bf16[768,256]{1,0:T(8,128)(2,1)}, bf16[768,256]{1,0:T(8,128)(2,1)S(1)}, u32[]{:S(2)}, u32[]{:S(2)}) collective-permute-start(bf16[768,256]{1,0:T(8,128)(2,1)} %collective-permute-done.4.refs_5_), channel_id=1, source_target_pairs={{0,56},{8,0},{16,8},{24,16},{32,24},{40,32},{48,40},{56,48},{1,57}... | collective-permute-start | bytes 1179656 | tf_op jit(solution)/shard_map/ppermute | solution.py:213
  79.8 0.0 collective-permute-done.12.refs_12_
  79.8 1.9 %collective-permute-start.13 = (bf16[768,256]{1,0:T(8,128)(2,1)}, bf16[768,256]{1,0:T(8,128)(2,1)S(1)}, u32[]{:S(2)}, u32[]{:S(2)}) collective-permute-start(bf16[768,256]{1,0:T(8,128)(2,1)} %collective-permute-done.12.refs_12_), channel_id=1, source_target_pairs={{0,56},{8,0},{16,8},{24,16},{32,24},{40,32},{48,40},{56,48},{1,57}... | collective-permute-start | bytes 1179656 | tf_op jit(solution)/shard_map/ppermute | solution.py:214
  81.8 0.0 collective-permute-done.2.refs_3_
  81.8 3.4 %collective-permute-start.6 = (bf16[768,256]{1,0:T(8,128)(2,1)}, bf16[768,256]{1,0:T(8,128)(2,1)S(1)}, u32[]{:S(2)}, u32[]{:S(2)}) collective-permute-start(bf16[768,256]{1,0:T(8,128)(2,1)} %collective-permute-done.2.refs_3_), channel_id=1, source_target_pairs={{0,8},{8,16},{16,24},{24,32},{32,40},{40,48},{48,56},{56,0},{1,9},... | collective-permute-start | bytes 1179656 | tf_op jit(solution)/shard_map/ppermute | solution.py:214
  85.2 0.5 and_select_fusion
  85.7 0.5 fusion.1.which_ref
  86.2 3.4 %collective-permute-done.9.refs_11_ = bf16[768,256]{1,0:T(8,128)(2,1)S(1)} collective-permute-done((bf16[768,256]{1,0:T(8,128)(2,1)S(1)}, bf16[768,256]{1,0:T(8,128)(2,1)S(1)}, u32[]{:S(2)}, u32[]{:S(2)}) %collective-permute-start.9) | collective-permute-done | bytes 393248 | tf_op jit(solution)/shard_map/ppermute | solution.py:212
  89.6 0.0 collective-permute-done.5.refs_4_
  89.6 2.7 %collective-permute-done.13.refs_15_ = bf16[768,256]{1,0:T(8,128)(2,1)S(1)} collective-permute-done((bf16[768,256]{1,0:T(8,128)(2,1)}, bf16[768,256]{1,0:T(8,128)(2,1)S(1)}, u32[]{:S(2)}, u32[]{:S(2)}) %collective-permute-start.13) | collective-permute-done | bytes 393248 | tf_op jit(solution)/shard_map/ppermute | solution.py:214
  92.3 5.6 %collective-permute-done.6.refs_7_ = bf16[768,256]{1,0:T(8,128)(2,1)S(1)} collective-permute-done((bf16[768,256]{1,0:T(8,128)(2,1)}, bf16[768,256]{1,0:T(8,128)(2,1)S(1)}, u32[]{:S(2)}, u32[]{:S(2)}) %collective-permute-start.6) | collective-permute-done | bytes 393248 | tf_op jit(solution)/shard_map/ppermute | solution.py:214
  98.0 0.6 copy-done.15
  98.7 4.2 %spmm.1 = bf16[1024,256]{1,0:T(8,128)(2,1)} custom-call(s32[1,1,48]{2,1,0:T(1,128)} %rows_ref.1, s32[1,1,48]{2,1,0:T(1,128)} %tiles_ref.1, s32[1,1]{1,0:T(1,128)S(6)} %copy.12.count_ref, s32[48]{0:T(128)} %fusion.1.which_ref, s32[48]{0:T(128)} %get-tuple-element.11.start_ref, bf16[64,64,64]{2,1,0:T(8,128)(2,1)} %table_ref.1, bf16[768,256]{1,0:T(8,128)(2,1)} %copy-done.4, ...), custom_call_target="tpu_custom_call" | custom-call | tf_op jit(solution)/shard_map/spmm/pallas_call | solution.py:85
  102.9 0.0 copy-start
  102.9 0.0 copy-start.1
  103.0 20.2 %all_to_all.20.parts_ref = bf16[8,128,256]{2,1,0:T(8,128)(2,1)S(1)} all-to-all(bf16[8,128,256]{2,1,0:T(8,128)(2,1)} %bitcast.21), channel_id=1, replica_groups=mesh['z'=12,'y'=8,'x'=4,'core'=2] {'x','core'}, dimensions={0} | all-to-all | bytes 1048576 | tf_op jit(solution)/shard_map/all_to_all | solution.py:191
  123.2 0.0 copy-done.1
  123.2 0.7 copy-done.2
  123.9 0.9 layer.1
  124.7 19.2 %all_to_all.21.parts_ref = bf16[64,16,128]{2,1,0:T(8,128)(2,1)S(1)} all-to-all(bf16[64,16,128]{2,1,0:T(8,128)(2,1)S(1)} %get-tuple-element.8), channel_id=1, replica_groups=mesh['z'=12,'y'=8,'x'=4,'core'=2] {'y','x','core'}, dimensions={0} | all-to-all | bytes 524288 | tf_op jit(solution)/shard_map/all_to_all | solution.py:199
  143.9 0.1 fold.2
  144.0 12.8 %all_to_all.22.parts_ref = bf16[12,16,128]{2,1,0:T(8,128)(2,1)S(1)} all-to-all(bf16[12,16,128]{2,1,0:T(8,128)(2,1)S(1)} %fold.2), channel_id=1, replica_groups=mesh['z'=12,'y'=8,'x'=4,'core'=2] {'z'}, dimensions={0} | all-to-all | bytes 98304 | tf_op jit(solution)/shard_map/all_to_all | solution.py:199
  156.8 19.2 %all_to_all.23.grads_ref = bf16[64,16,128]{2,1,0:T(8,128)(2,1)S(1)} all-to-all(bf16[64,16,128]{2,1,0:T(8,128)(2,1)S(1)} %fold.3), channel_id=1, replica_groups=mesh['z'=12,'y'=8,'x'=4,'core'=2] {'y','x','core'}, dimensions={0} | all-to-all | bytes 524288 | tf_op jit(solution)/shard_map/all_to_all | solution.py:199
  176.0 0.7 finish.1
  (27 shorter events, 0.1 us)
Async XLA Ops:
  33.6 64.3 %copy-start.3 = (bf16[768,256]{1,0:T(8,128)(2,1)}, bf16[768,256]{1,0:T(8,128)(2,1)S(1)}, u32[]{:S(2)}) copy-start(bf16[768,256]{1,0:T(8,128)(2,1)S(1)} %get-tuple-element.14.refs_8_) | copy-start | bytes 1179652
  33.6 64.3 %copy-start.4 = (bf16[768,256]{1,0:T(8,128)(2,1)}, bf16[768,256]{1,0:T(8,128)(2,1)S(1)}, u32[]{:S(2)}) copy-start(bf16[768,256]{1,0:T(8,128)(2,1)S(1)} %get-tuple-element.15.refs_0_) | copy-start | bytes 1179652
  33.6 13.5 %collective-permute-start.10 = (bf16[768,256]{1,0:T(8,128)(2,1)S(1)}, bf16[768,256]{1,0:T(8,128)(2,1)S(1)}, u32[]{:S(2)}, u32[]{:S(2)}) collective-permute-start(bf16[768,256]{1,0:T(8,128)(2,1)S(1)} %get-tuple-element.14.refs_8_), channel_id=1, source_target_pairs={{0,56},{8,0},{16,8},{24,16},{32,24},{40,32},{48,40},{56,48},{1,57}... | collective-permute-start | bytes 1179656 | tf_op jit(solution)/shard_map/ppermute | solution.py:213
  38.7 11.8 %collective-permute-start = (bf16[768,256]{1,0:T(8,128)(2,1)S(1)}, bf16[768,256]{1,0:T(8,128)(2,1)S(1)}, u32[]{:S(2)}, u32[]{:S(2)}) collective-permute-start(bf16[768,256]{1,0:T(8,128)(2,1)S(1)} %get-tuple-element.15.refs_0_), channel_id=1, source_target_pairs={{0,8},{8,16},{16,24},{24,32},{32,40},{40,48},{48,56},{56,0},{1,9},... | collective-permute-start | bytes 1179656 | tf_op jit(solution)/shard_map/ppermute | solution.py:212
  40.7 14.0 %collective-permute-start.7 = (bf16[768,256]{1,0:T(8,128)(2,1)S(1)}, bf16[768,256]{1,0:T(8,128)(2,1)S(1)}, u32[]{:S(2)}, u32[]{:S(2)}) collective-permute-start(bf16[768,256]{1,0:T(8,128)(2,1)S(1)} %get-tuple-element.14.refs_8_), channel_id=1, source_target_pairs={{0,8},{8,16},{16,24},{24,32},{32,40},{40,48},{48,56},{56,0},{1,9},... | collective-permute-start | bytes 1179656 | tf_op jit(solution)/shard_map/ppermute | solution.py:212
  42.6 14.0 %collective-permute-start.3 = (bf16[768,256]{1,0:T(8,128)(2,1)S(1)}, bf16[768,256]{1,0:T(8,128)(2,1)S(1)}, u32[]{:S(2)}, u32[]{:S(2)}) collective-permute-start(bf16[768,256]{1,0:T(8,128)(2,1)S(1)} %get-tuple-element.15.refs_0_), channel_id=1, source_target_pairs={{0,56},{8,0},{16,8},{24,16},{32,24},{40,32},{48,40},{56,48},{1,57}... | collective-permute-start | bytes 1179656 | tf_op jit(solution)/shard_map/ppermute | solution.py:213
  47.2 50.8 %copy-start.5 = (bf16[768,256]{1,0:T(8,128)(2,1)}, bf16[768,256]{1,0:T(8,128)(2,1)S(1)}, u32[]{:S(2)}) copy-start(bf16[768,256]{1,0:T(8,128)(2,1)S(1)} %collective-permute-done.10.refs_14_) | copy-start | bytes 1179652
  47.2 14.6 %collective-permute-start.11 = (bf16[768,256]{1,0:T(8,128)(2,1)S(1)}, bf16[768,256]{1,0:T(8,128)(2,1)S(1)}, u32[]{:S(2)}, u32[]{:S(2)}) collective-permute-start(bf16[768,256]{1,0:T(8,128)(2,1)S(1)} %collective-permute-done.10.refs_14_), channel_id=1, source_target_pairs={{0,56},{8,0},{16,8},{24,16},{32,24},{40,32},{48,40},{56,48},{1,57}... | collective-permute-start | bytes 1179656 | tf_op jit(solution)/shard_map/ppermute | solution.py:213
  50.6 47.4 %copy-start.6 = (bf16[768,256]{1,0:T(8,128)(2,1)}, bf16[768,256]{1,0:T(8,128)(2,1)S(1)}, u32[]{:S(2)}) copy-start(bf16[768,256]{1,0:T(8,128)(2,1)S(1)} %collective-permute-done.refs_1_) | copy-start | bytes 1179652
  50.6 16.5 %collective-permute-start.1 = (bf16[768,256]{1,0:T(8,128)(2,1)S(1)}, bf16[768,256]{1,0:T(8,128)(2,1)S(1)}, u32[]{:S(2)}, u32[]{:S(2)}) collective-permute-start(bf16[768,256]{1,0:T(8,128)(2,1)S(1)} %collective-permute-done.refs_1_), channel_id=1, source_target_pairs={{0,8},{8,16},{16,24},{24,32},{32,40},{40,48},{48,56},{56,0},{1,9},... | collective-permute-start | bytes 1179656 | tf_op jit(solution)/shard_map/ppermute | solution.py:212
  54.7 43.3 %copy-start.7 = (bf16[768,256]{1,0:T(8,128)(2,1)}, bf16[768,256]{1,0:T(8,128)(2,1)S(1)}, u32[]{:S(2)}) copy-start(bf16[768,256]{1,0:T(8,128)(2,1)S(1)} %collective-permute-done.7.refs_9_) | copy-start | bytes 1179652
  54.7 18.6 %collective-permute-start.8 = (bf16[768,256]{1,0:T(8,128)(2,1)S(1)}, bf16[768,256]{1,0:T(8,128)(2,1)S(1)}, u32[]{:S(2)}, u32[]{:S(2)}) collective-permute-start(bf16[768,256]{1,0:T(8,128)(2,1)S(1)} %collective-permute-done.7.refs_9_), channel_id=1, source_target_pairs={{0,8},{8,16},{16,24},{24,32},{32,40},{40,48},{48,56},{56,0},{1,9},... | collective-permute-start | bytes 1179656 | tf_op jit(solution)/shard_map/ppermute | solution.py:212
  56.6 41.3 %copy-start.8 = (bf16[768,256]{1,0:T(8,128)(2,1)}, bf16[768,256]{1,0:T(8,128)(2,1)S(1)}, u32[]{:S(2)}) copy-start(bf16[768,256]{1,0:T(8,128)(2,1)S(1)} %collective-permute-done.3.refs_6_) | copy-start | bytes 1179652
  56.6 18.6 %collective-permute-start.4 = (bf16[768,256]{1,0:T(8,128)(2,1)S(1)}, bf16[768,256]{1,0:T(8,128)(2,1)}, u32[]{:S(2)}, u32[]{:S(2)}) collective-permute-start(bf16[768,256]{1,0:T(8,128)(2,1)S(1)} %collective-permute-done.3.refs_6_), channel_id=1, source_target_pairs={{0,56},{8,0},{16,8},{24,16},{32,24},{40,32},{48,40},{56,48},{1,57}... | collective-permute-start | bytes 1179656 | tf_op jit(solution)/shard_map/ppermute | solution.py:213
  61.8 36.2 %copy-start.9 = (bf16[768,256]{1,0:T(8,128)(2,1)}, bf16[768,256]{1,0:T(8,128)(2,1)S(1)}, u32[]{:S(2)}) copy-start(bf16[768,256]{1,0:T(8,128)(2,1)S(1)} %collective-permute-done.11.refs_13_) | copy-start | bytes 1179652
  61.8 18.0 %collective-permute-start.12 = (bf16[768,256]{1,0:T(8,128)(2,1)S(1)}, bf16[768,256]{1,0:T(8,128)(2,1)}, u32[]{:S(2)}, u32[]{:S(2)}) collective-permute-start(bf16[768,256]{1,0:T(8,128)(2,1)S(1)} %collective-permute-done.11.refs_13_), channel_id=1, source_target_pairs={{0,56},{8,0},{16,8},{24,16},{32,24},{40,32},{48,40},{56,48},{1,57}... | collective-permute-start | bytes 1179656 | tf_op jit(solution)/shard_map/ppermute | solution.py:213
  67.1 30.9 %copy-start.10 = (bf16[768,256]{1,0:T(8,128)(2,1)}, bf16[768,256]{1,0:T(8,128)(2,1)S(1)}, u32[]{:S(2)}) copy-start(bf16[768,256]{1,0:T(8,128)(2,1)S(1)} %collective-permute-done.1.refs_2_) | copy-start | bytes 1179652
  67.1 14.6 %collective-permute-start.2 = (bf16[768,256]{1,0:T(8,128)(2,1)S(1)}, bf16[768,256]{1,0:T(8,128)(2,1)}, u32[]{:S(2)}, u32[]{:S(2)}) collective-permute-start(bf16[768,256]{1,0:T(8,128)(2,1)S(1)} %collective-permute-done.1.refs_2_), channel_id=1, source_target_pairs={{0,8},{8,16},{16,24},{24,32},{32,40},{40,48},{48,56},{56,0},{1,9},... | collective-permute-start | bytes 1179656 | tf_op jit(solution)/shard_map/ppermute | solution.py:212
  69.1 16.1 %copy-start.16 = (s32[1,1,48]{2,1,0:T(1,128)S(1)}, s32[1,1,48]{2,1,0:T(1,128)}, u32[]{:S(2)}) copy-start(s32[1,1,48]{2,1,0:T(1,128)} %param.15) | copy-start | bytes 580
  73.3 24.7 %copy-start.11 = (bf16[768,256]{1,0:T(8,128)(2,1)}, bf16[768,256]{1,0:T(8,128)(2,1)S(1)}, u32[]{:S(2)}) copy-start(bf16[768,256]{1,0:T(8,128)(2,1)S(1)} %collective-permute-done.8.refs_10_) | copy-start | bytes 1179652
  73.3 16.3 %collective-permute-start.9 = (bf16[768,256]{1,0:T(8,128)(2,1)S(1)}, bf16[768,256]{1,0:T(8,128)(2,1)S(1)}, u32[]{:S(2)}, u32[]{:S(2)}) collective-permute-start(bf16[768,256]{1,0:T(8,128)(2,1)S(1)} %collective-permute-done.8.refs_10_), channel_id=1, source_target_pairs={{0,8},{8,16},{16,24},{24,32},{32,40},{40,48},{48,56},{56,0},{1,9},... | collective-permute-start | bytes 1179656 | tf_op jit(solution)/shard_map/ppermute | solution.py:212
  75.2 14.4 %collective-permute-start.5 = (bf16[768,256]{1,0:T(8,128)(2,1)}, bf16[768,256]{1,0:T(8,128)(2,1)S(1)}, u32[]{:S(2)}, u32[]{:S(2)}) collective-permute-start(bf16[768,256]{1,0:T(8,128)(2,1)} %collective-permute-done.4.refs_5_), channel_id=1, source_target_pairs={{0,56},{8,0},{16,8},{24,16},{32,24},{40,32},{48,40},{56,48},{1,57}... | collective-permute-start | bytes 1179656 | tf_op jit(solution)/shard_map/ppermute | solution.py:213
  79.8 12.5 %collective-permute-start.13 = (bf16[768,256]{1,0:T(8,128)(2,1)}, bf16[768,256]{1,0:T(8,128)(2,1)S(1)}, u32[]{:S(2)}, u32[]{:S(2)}) collective-permute-start(bf16[768,256]{1,0:T(8,128)(2,1)} %collective-permute-done.12.refs_12_), channel_id=1, source_target_pairs={{0,56},{8,0},{16,8},{24,16},{32,24},{40,32},{48,40},{56,48},{1,57}... | collective-permute-start | bytes 1179656 | tf_op jit(solution)/shard_map/ppermute | solution.py:214
  81.8 16.2 %collective-permute-start.6 = (bf16[768,256]{1,0:T(8,128)(2,1)}, bf16[768,256]{1,0:T(8,128)(2,1)S(1)}, u32[]{:S(2)}, u32[]{:S(2)}) collective-permute-start(bf16[768,256]{1,0:T(8,128)(2,1)} %collective-permute-done.2.refs_3_), channel_id=1, source_target_pairs={{0,8},{8,16},{16,24},{24,32},{32,40},{40,48},{48,56},{56,0},{1,9},... | collective-permute-start | bytes 1179656 | tf_op jit(solution)/shard_map/ppermute | solution.py:214
  89.6 8.4 %copy-start.12 = (bf16[768,256]{1,0:T(8,128)(2,1)}, bf16[768,256]{1,0:T(8,128)(2,1)S(1)}, u32[]{:S(2)}) copy-start(bf16[768,256]{1,0:T(8,128)(2,1)S(1)} %collective-permute-done.9.refs_11_) | copy-start | bytes 1179652
  89.6 8.4 %copy-start.13 = (bf16[768,256]{1,0:T(8,128)(2,1)}, bf16[768,256]{1,0:T(8,128)(2,1)S(1)}, u32[]{:S(2)}) copy-start(bf16[768,256]{1,0:T(8,128)(2,1)S(1)} %collective-permute-done.5.refs_4_) | copy-start | bytes 1179652
  92.3 5.7 %copy-start.14 = (bf16[768,256]{1,0:T(8,128)(2,1)}, bf16[768,256]{1,0:T(8,128)(2,1)S(1)}, u32[]{:S(2)}) copy-start(bf16[768,256]{1,0:T(8,128)(2,1)S(1)} %collective-permute-done.13.refs_15_) | copy-start | bytes 1179652
  97.9 0.8 copy-start.15
  102.9 20.3 %copy-start = (bf16[256,256]{1,0:T(8,128)(2,1)S(1)}, bf16[256,256]{1,0:T(8,128)(2,1)}, u32[]{:S(2)}) copy-start(bf16[256,256]{1,0:T(8,128)(2,1)} %weight_ref.1) | copy-start | bytes 393220
  102.9 20.2 %copy-start.1 = (bf16[128,256]{1,0:T(8,128)(2,1)S(1)}, bf16[128,256]{1,0:T(8,128)(2,1)}, u32[]{:S(2)}) copy-start(bf16[128,256]{1,0:T(8,128)(2,1)} %cotangent_ref.1) | copy-start | bytes 196612
  123.2 0.7 copy-start.2
